TPU v7x, 32 devices: a whole 2x2x4 slice. The times are simulated.
32 devices in a mesh: dp: 4 (over z), expert: 2 (over x), tensor: 4 (over y, core).
Axes of the slice: x: 2, y: 2, z: 4, core: 2. Of those that a mesh axis runs over, the one named last changes fastest.
Arguments:
- skip_stream_entry: bfloat16 [512, 4096], P(('dp', 'expert', 'tensor')), may hold values from -6 to 6
- question_vectors: bfloat16 [512, 2048], P(('dp', 'expert'), 'tensor'), may hold values from -5 to 5
- fresh_lookup_vectors: bfloat16 [512, 512], P(('dp', 'expert'), 'tensor'), may hold values from -5 to 5
- fresh_content_vectors: bfloat16 [512, 512], P(('dp', 'expert'), 'tensor'), may hold values from -10 to 10
- stored_lookup_sheets: bfloat16 [320, 4, 128, 128], P(('dp', 'expert'), 'tensor'), may hold values from -5 to 5
- stored_content_sheets: bfloat16 [320, 4, 128, 128], P(('dp', 'expert'), 'tensor'), may hold values from -10 to 10
- sequence_sheet_map: int32 [136, 8], P(('dp', 'expert')), may hold values from 0 to 39
- stored_position_counts: int32 [136], P(('dp', 'expert')), may hold values from 2 to 1024
- attention_merge_matrix: bfloat16 [2048, 4096], P('tensor'), may hold values from -0.59765625 to 0.59765625
- premix_scale_factor: bfloat16 [4096], replicated, may hold values from 0.5 to 1.5
- chosen_specialists: int32 [512, 2], P(('dp', 'expert', 'tensor')), may hold values from 0 to 7, all different within a row; in each aligned block of 16 rows (0 to 15, 16 to 31, ...) at most 6 rows name the same one
- selection_shares: float32 [512, 2], P(('dp', 'expert', 'tensor')), may hold values from 0.2 to 1
- allowed_placements: int32 [8], replicated, may hold values from 2 to 3
- favored_specialist: int32 [1], replicated, may hold values from 0 to 7
- gating_matrices: bfloat16 [8, 7168, 4096], P('expert', ('dp', 'tensor')), may hold values from -0.09375 to 0.09375
- expand_matrices: bfloat16 [8, 7168, 4096], P('expert', ('dp', 'tensor')), may hold values from -0.09375 to 0.09375
- contract_matrices: bfloat16 [8, 7168, 4096], P('expert', ('dp', 'tensor')), may hold values from -0.0625 to 0.0625
Outputs:
- layer_out: bfloat16 [512, 4096], P(('dp', 'expert', 'tensor'))
Inputs may be any that keep to these rules, and one draw needn't show every extreme that they name: `chosen_specialists`: in the 16 rows of one device no expert is named by more than 6 rows; a token names two different experts.
All inputs are finite; a program needn't handle non-finite values.
Results may differ from a plain program's by a relative error of at most 0.018.
Values may be sent and summed in bfloat16 or wider, within the bound.
No kernel may reach another device: no remote copies, remote signals or barrier semaphores. Data moves between devices by JAX's collectives and lax.ppermute only.
A program may use at most 128 MiB of HBM per device.

v0:
```python
from functools import reduce
import math

import jax
import jax.numpy as jnp
from jax import lax
from jax.sharding import PartitionSpec as P

HD = 128
PLACEMENT_MOST = 6


def normalize(parts):
    highest = reduce(
        jnp.maximum,
        [
            jnp.max(jnp.where(visible, scores, -jnp.inf), axis=-1, keepdims=True)
            for scores, visible in parts
        ],
    )
    portions = [jnp.where(visible, jnp.exp(scores - highest), 0.0) for scores, visible in parts]
    denominator = reduce(
        jnp.add, [jnp.sum(portion, axis=-1, keepdims=True) for portion in portions]
    )
    return [(portion / denominator).astype(jnp.bfloat16) for portion in portions]


def attend(question_vectors, new_keys, new_values, key_pages, value_pages, table, spans):
    rows_all, head_count, head_width = question_vectors.shape
    kv_heads = new_keys.shape[1]
    group_size = head_count // kv_heads
    single_count = spans.shape[0] - 1
    page_count = table.shape[1]
    page_width = key_pages.shape[2]
    context = page_count * page_width
    inverse_root = 1.0 / math.sqrt(head_width)
    page_keys = key_pages[table]
    page_values = value_pages[table]
    grouped = question_vectors.reshape(rows_all, kv_heads, group_size, head_width)
    positions = jnp.arange(context, dtype=jnp.int32)
    single_q = grouped[:single_count]
    cache_dec = (
        jnp.einsum(
            "rkgh,rmkph->rkgmp",
            single_q,
            page_keys[:single_count],
            preferred_element_type=jnp.float32,
        ).reshape(single_count, kv_heads, group_size, context)
        * inverse_root
    )
    seen_dec = (positions[None, :] < spans[:single_count, None])[:, None, None, :]
    own_dec = (
        jnp.einsum(
            "rkgh,rkh->rkg", single_q, new_keys[:single_count], preferred_element_type=jnp.float32
        )[..., None]
        * inverse_root
    )
    weight_cache, weight_own = normalize(
        [(cache_dec, seen_dec), (own_dec, jnp.full(own_dec.shape, True))]
    )
    out_dec = jnp.einsum(
        "rkgmp,rmkph->rkgh",
        weight_cache.reshape(single_count, kv_heads, group_size, page_count, page_width),
        page_values[:single_count],
        preferred_element_type=jnp.float32,
    )
    out_dec = (
        out_dec
        + weight_own.astype(jnp.float32)
        * new_values[:single_count].astype(jnp.float32)[:, :, None, :]
    )
    prompt_q = grouped[single_count:]
    prompt_rows = rows_all - single_count
    cache_pro = (
        jnp.einsum(
            "rkgh,mkph->rkgmp",
            prompt_q,
            page_keys[single_count],
            preferred_element_type=jnp.float32,
        ).reshape(prompt_rows, kv_heads, group_size, context)
        * inverse_root
    )
    seen_pro = (positions < spans[single_count])[None, None, None, :]
    new_pro = (
        jnp.einsum(
            "rkgh,mkh->rkgm", prompt_q, new_keys[single_count:], preferred_element_type=jnp.float32
        )
        * inverse_root
    )
    prompt_index = jnp.arange(prompt_rows, dtype=jnp.int32)
    causal = (prompt_index[:, None] >= prompt_index[None, :])[:, None, None, :]
    weight_cpro, weight_npro = normalize([(cache_pro, seen_pro), (new_pro, causal)])
    out_pro = jnp.einsum(
        "rkgmp,mkph->rkgh",
        weight_cpro.reshape(prompt_rows, kv_heads, group_size, page_count, page_width),
        page_values[single_count],
        preferred_element_type=jnp.float32,
    )
    out_pro = out_pro + jnp.einsum(
        "rkgm,mkh->rkgh", weight_npro, new_values[single_count:], preferred_element_type=jnp.float32
    )
    joined = jnp.concatenate([out_dec, out_pro], axis=0).astype(jnp.bfloat16)
    return joined.reshape(rows_all, head_count * head_width)


def slot_table(member, ranking, keeping, slot_count):
    slot_hit = (
        ranking[:, :, None, None] == jnp.arange(slot_count, dtype=jnp.int32)[None, None, None, :]
    )
    return ((member[..., None] > 0) & keeping[:, :, None, None] & slot_hit).astype(jnp.bfloat16)


def expert_pass(send, gating_matrices, expand_matrices, contract_matrices):
    specialist_index, slot_count, model_width = send.shape
    holders = lax.axis_size("expert")
    local_count = gating_matrices.shape[0]
    arrived = lax.all_to_all(
        send.reshape(holders, local_count, slot_count, model_width),
        "expert",
        split_axis=0,
        concat_axis=0,
        tiled=True,
    )
    row_piece = lax.all_gather(arrived, ("dp", "tensor"), axis=0, tiled=True)
    gate_part = jnp.einsum(
        "qesd,efd->qesf", row_piece, gating_matrices, preferred_element_type=jnp.float32
    )
    up_part = jnp.einsum(
        "qesd,efd->qesf", row_piece, expand_matrices, preferred_element_type=jnp.float32
    )
    hidden = (jax.nn.silu(gate_part) * up_part).astype(jnp.bfloat16)
    summed = lax.psum_scatter(
        jnp.einsum(
            "qesf,efd->qesd", hidden, contract_matrices, preferred_element_type=jnp.float32
        ).astype(jnp.bfloat16),
        ("dp", "tensor"),
        scatter_dimension=0,
        tiled=True,
    )
    arrived_back = lax.all_to_all(summed, "expert", split_axis=0, concat_axis=0, tiled=True)
    return arrived_back.reshape(specialist_index, slot_count, model_width)


def local(
    skip_stream_entry,
    question_vectors,
    fresh_lookup_vectors,
    fresh_content_vectors,
    stored_lookup_sheets,
    stored_content_sheets,
    sequence_sheet_map,
    stored_position_counts,
    attention_merge_matrix,
    premix_scale_factor,
    chosen_specialists,
    selection_shares,
    allowed_placements,
    favored_specialist,
    gating_matrices,
    expand_matrices,
    contract_matrices,
):
    token_count = chosen_specialists.shape[0]
    specialist_index = allowed_placements.shape[0]
    picked = (
        chosen_specialists[:, :, None]
        == jnp.arange(specialist_index, dtype=jnp.int32)[None, None, :]
    ).astype(jnp.int32)
    flat_routes = picked.reshape(token_count * 2, specialist_index)
    busiest_specialist = favored_specialist[0]
    before = (jnp.cumsum(flat_routes, axis=0) - flat_routes).reshape(
        token_count, 2, specialist_index
    )
    ranking = jnp.sum(before * picked, axis=2)
    placement_ceiling = jnp.where(
        jnp.arange(specialist_index, dtype=jnp.int32) == busiest_specialist,
        PLACEMENT_MOST,
        allowed_placements,
    )
    keeping = ranking < jnp.sum(picked * placement_ceiling[None, None, :], axis=2)
    row_total = question_vectors.shape[0]
    heads_out = attend(
        question_vectors.reshape(row_total, -1, HD),
        fresh_lookup_vectors.reshape(row_total, -1, HD),
        fresh_content_vectors.reshape(row_total, -1, HD),
        stored_lookup_sheets,
        stored_content_sheets,
        sequence_sheet_map,
        stored_position_counts,
    )
    total_attn = lax.psum(
        jnp.dot(heads_out, attention_merge_matrix, preferred_element_type=jnp.float32).astype(
            jnp.bfloat16
        ),
        "tensor",
    ).astype(jnp.float32)
    own_attn = lax.dynamic_slice_in_dim(
        total_attn, lax.axis_index("tensor") * token_count, token_count, 0
    )
    stream = (skip_stream_entry.astype(jnp.float32) + own_attn).astype(jnp.bfloat16)
    wide = stream.astype(jnp.float32)
    squares = jnp.mean(wide * wide, axis=1, keepdims=True)
    normed = (wide * lax.rsqrt(squares + 1e-05) * premix_scale_factor.astype(jnp.float32)).astype(
        jnp.bfloat16
    )
    main_slots = PLACEMENT_MOST
    table_main = slot_table(picked, ranking, keeping, main_slots)
    send = jnp.einsum(
        "nkes,nd->esd", table_main, normed, preferred_element_type=jnp.float32
    ).astype(jnp.bfloat16)
    expert_out = expert_pass(send, gating_matrices, expand_matrices, contract_matrices)
    chosen = jnp.einsum("nkes,esd->nkd", table_main, expert_out, preferred_element_type=jnp.float32)
    mixed = jnp.sum(selection_shares[:, :, None] * chosen, axis=1)
    return (wide + mixed).astype(jnp.bfloat16)


def solution(mesh):
    placed = (
        P(("dp", "expert", "tensor"), None),
        P(("dp", "expert"), "tensor"),
        P(("dp", "expert"), "tensor"),
        P(("dp", "expert"), "tensor"),
        P(("dp", "expert"), "tensor", None, None),
        P(("dp", "expert"), "tensor", None, None),
        P(("dp", "expert"), None),
        P(("dp", "expert")),
        P("tensor", None),
        P(),
        P(("dp", "expert", "tensor"), None),
        P(("dp", "expert", "tensor"), None),
        P(),
        P(),
        P("expert", ("dp", "tensor"), None),
        P("expert", ("dp", "tensor"), None),
        P("expert", ("dp", "tensor"), None),
    )
    return jax.shard_map(
        local,
        mesh=mesh,
        in_specs=placed,
        out_specs=P(("dp", "expert", "tensor"), None),
        check_vma=False,
    )
```

profile of v0, /device:TPU:0, one launch (start us, length us, event | category | flops | bytes accessed | tf_op | source)
XLA Modules:
  0.0 350.6 jit_solution(17388961513529278336)
XLA Ops:
  6.6 0.8 slice.44
  7.4 0.7 compare_select_fusion
  8.1 0.1 copy.51
  8.2 0.1 reshape.307
  8.3 1.2 slice.49
  9.5 0.7 broadcast_compare_fusion.1
  10.2 7.5 %gather_fusion = bf16[136,128,128]{2,1,0:T(8,128)(2,1)} fusion(bf16[40,128,128]{2,1,0:T(8,128)(2,1)S(1)} %bitcast.179, s32[1024]{0:T(1024)S(1)} %pad_clamp_fusion), kind=kCustom, calls=%fused_computation | custom fusion | bytes 8913440 | tf_op jit(solution)/shard_map/gather | solution.py:37
  17.7 0.0 copy-start.9
  17.8 0.0 copy-start.12
  17.8 0.0 copy-start.11
  17.8 0.0 copy-start.4
  17.8 2.2 copy-done.3
  20.0 0.3 select_reduce_fusion
  20.4 0.2 select_reduce_fusion.2
  20.6 0.3 bitcast_reduce_fusion
  20.9 0.2 convolution_bitcast_fusion.2
  21.1 7.5 %gather_fusion.1 = bf16[136,128,128]{2,1,0:T(8,128)(2,1)} fusion(bf16[40,128,128]{2,1,0:T(8,128)(2,1)S(1)} %bitcast.182, s32[1024]{0:T(1024)S(1)} %pad_clamp_fusion), kind=kCustom, calls=%fused_computation.1 | custom fusion | bytes 8913440 | tf_op jit(solution)/shard_map/gather | solution.py:38
  28.7 0.0 copy-start.13
  28.7 2.2 copy-done.2
  30.9 0.3 fusion.28
  31.3 0.1 broadcast_compare_fusion
  31.4 0.1 fusion.70
  31.5 0.7 slice-done.1
  32.2 1.3 select_reduce_fusion.1
  33.5 0.3 bitcast_reduce_fusion.1
  33.8 0.0 copy-start.7
  33.9 0.0 copy-start.14
  33.9 0.0 copy-start.6
  33.9 0.8 fusion.30
  34.7 0.1 copy-done.5
  34.8 1.7 convolution_convert_fusion
  36.5 0.0 all-reduce.4.cloned.1.call-update
  36.5 0.0 all-gather.2.cloned.1.call-start
  36.5 0.1 copy.57
  36.6 0.1 eq.56
  36.7 0.1 fusion.64
  36.8 0.1 reduce_window_sum.11
  36.8 0.2 select_reduce_fusion.3
  37.0 0.1 reduce_sum.82
  37.1 0.1 copy.58
  37.9 0.1 select_reduce_fusion.4
  38.1 34.5 %all-reduce.4.cloned.1.call-done = bf16[64,4096]{1,0:T(8,128)(2,1)} async-done(((bf16[64,4096]{1,0:T(8,128)(2,1)}), bf16[64,4096]{1,0:T(8,128)(2,1)}) %all-reduce.4.cloned.1.call-update) | async-done | bytes 524304 | tf_op jit(solution)/shard_map/psum | solution.py:191
  72.6 1.1 fusion.35
  73.6 0.3 convolution_convert_fusion.1
  74.0 0.1 reshape.301
  74.1 0.2 copy.60
  74.3 9.0 %all_to_all.10 = bf16[2,4,6,4096]{3,1,2,0:T(4,128)(2,1)} all-to-all(bf16[2,4,6,4096]{3,1,2,0:T(4,128)(2,1)S(1)} %copy.60), channel_id=1, replica_groups=mesh['dp'=4,'expert'=2,'tensor'=4] {'expert'}, dimensions={0} | all-to-all | bytes 786432 | tf_op jit(solution)/shard_map/all_to_all | solution.py:117
  83.3 0.0 all-gather.2.cloned.1.call-update
  83.3 0.2 all-reduce.6.cloned.1.call-start
  83.5 60.9 %all-gather.2.cloned.1.call-done = bf16[32,4,6,4096]{3,1,2,0:T(4,128)(2,1)} async-done(((bf16[2,4,6,4096]{3,1,2,0:T(4,128)(2,1)}), bf16[32,4,6,4096]{3,1,2,0:T(4,128)(2,1)}) %all-gather.2.cloned.1.call-update) | async-done | bytes 6291472 | tf_op jit(solution)/shard_map/all_gather | solution.py:124
  144.4 15.5 %fusion.4 = f32[4,32,6,448]{3,1,2,0:T(8,128)S(1)} fusion(bf16[4,448,4096]{2,1,0:T(8,128)(2,1)} %param.31, bf16[32,4,6,4096]{3,1,2,0:T(4,128)(2,1)} %all-gather.2.cloned.1.call-done), kind=kOutput, calls=%fused_computation.6 | convolution fusion | flops 2818572288 | bytes 22347776 | tf_op jit(solution)/shard_map/qesd,efd->qesf/dot_general | solution.py:125
  159.9 18.4 %fusion.15 = bf16[32,4,6,448]{3,0,2,1:T(8,128)(2,1)} fusion(f32[4,32,6,448]{3,1,2,0:T(8,128)S(1)} %fusion.4, bf16[4,448,4096]{2,1,0:T(8,128)(2,1)} %param.32, bf16[32,4,6,4096]{3,1,2,0:T(4,128)(2,1)} %all-gather.2.cloned.1.call-done), kind=kOutput, calls=%fused_computation.17 | convolution fusion | flops 2820636672 | bytes 23035904 | tf_op jit(solution)/shard_map/qesd,efd->qesf/dot_general | solution.py:128
  178.3 8.9 %fusion.9 = bf16[32,4,6,4096]{3,0,2,1:T(8,128)(2,1)S(1)} fusion(bf16[32,4,6,448]{3,0,2,1:T(8,128)(2,1)} %fusion.15, bf16[4,448,4096]{2,1,0:T(8,128)(2,1)} %param.33), kind=kOutput, calls=%fused_computation.9 | convolution fusion | flops 2821718016 | bytes 21659648 | tf_op jit(solution)/shard_map/qesf,efd->qesd/dot_general | solution.py:133
  187.2 7.5 %copy.63 = bf16[32,4,6,4096]{3,1,2,0:T(4,128)(2,1)} copy(bf16[32,4,6,4096]{3,0,2,1:T(8,128)(2,1)S(1)} %fusion.9) | data formatting | bytes 12582912 | tf_op jit(solution)/shard_map/convert_element_type | solution.py:135
  194.7 0.0 all-reduce.6.cloned.1.call-update
  194.7 0.6 copy-done.15
  195.4 0.6 dynamic-slice
  196.6 135.9 %all-reduce.6.cloned.1.call-done = bf16[32,4,6,4096]{3,1,2,0:T(4,128)(2,1)} async-done(((bf16[32,4,6,4096]{3,1,2,0:T(4,128)(2,1)}), bf16[32,4,6,4096]{3,1,2,0:T(4,128)(2,1)}) %all-reduce.6.cloned.1.call-update) | async-done | bytes 6291472
  332.5 1.2 constant_dynamic-slice_fusion
  333.6 9.2 %all_to_all.11 = bf16[2,4,6,4096]{3,1,2,0:T(4,128)(2,1)S(1)} all-to-all(bf16[2,4,6,4096]{3,1,2,0:T(4,128)(2,1)S(1)} %constant_dynamic-slice_fusion), channel_id=1, replica_groups=mesh['dp'=4,'expert'=2,'tensor'=4] {'expert'}, dimensions={0} | all-to-all | bytes 786432 | tf_op jit(solution)/shard_map/all_to_all | solution.py:140
  342.8 0.2 copy.64
  343.0 0.1 reshape.351
  343.1 0.3 fusion.24
  343.4 0.7 fusion.38
  (46 shorter events, 0.3 us)
Async XLA Ops:
  6.5 3.7 %copy-start = (bf16[40,1,128,128]{3,2,1,0:T(8,128)(2,1)S(1)}, bf16[40,1,128,128]{3,2,1,0:T(8,128)(2,1)}, u32[]{:S(2)}) copy-start(bf16[40,1,128,128]{3,2,1,0:T(8,128)(2,1)} %param.21) | copy-start | bytes 3932164
  6.5 66.0 %all-reduce.4.cloned.1.call-start = ((), (), s32[]{:S(2)}) async-start(), calls=%async_computation.2 | async-start | bytes 1048576 | tf_op jit(solution)/shard_map/psum | solution.py:191
  17.7 2.3 copy-start.3
  17.7 2.3 copy-start.9
  17.8 2.6 copy-start.12
  17.8 3.1 copy-start.11
  17.8 3.4 copy-start.4
  28.7 2.3 copy-start.2
  28.7 2.6 copy-start.13
  28.7 3.5 %slice-start.1 = ((bf16[136,128,128]{2,1,0:T(8,128)(2,1)}), bf16[128,128,128]{2,1,0:T(8,128)(2,1)S(1)}, s32[]{:S(2)}) async-start(bf16[136,128,128]{2,1,0:T(8,128)(2,1)} %gather_fusion), calls=%async_computation.6 | async-start | bytes 8388608 | tf_op jit(solution)/shard_map/slice | solution.py:46
  30.9 2.9 slice-start
  32.2 2.6 copy-start.5
  33.8 2.7 copy-start.7
  33.9 4.0 %copy-start.14 = (s32[8]{0:T(128)S(1)}, s32[8]{0:T(128)}, u32[]{:S(2)}) copy-start(s32[8]{0:T(128)} %param.29) | copy-start | bytes 100
  33.9 4.1 %copy-start.8 = (bf16[4096]{0:T(1024)(128)(2,1)S(1)}, bf16[4096]{0:T(1024)(128)(2,1)}, u32[]{:S(2)}) copy-start(bf16[4096]{0:T(1024)(128)(2,1)} %param.26) | copy-start | bytes 24580
  33.9 38.7 %copy-start.6 = (bf16[16,4096]{1,0:T(8,128)(2,1)S(1)}, bf16[16,4096]{1,0:T(8,128)(2,1)}, u32[]{:S(2)}) copy-start(bf16[16,4096]{1,0:T(8,128)(2,1)} %param.17) | copy-start | bytes 393220
  36.5 108.0 %all-gather.2.cloned.1.call-start = ((), (), s32[]{:S(2)}) async-start(), calls=%async_computation.3 | async-start | bytes 6684672 | tf_op jit(solution)/shard_map/all_gather | solution.py:124
  83.3 249.2 %all-reduce.6.cloned.1.call-start = ((), (), s32[]{:S(2)}) async-start(), calls=%async_computation.4 | async-start | bytes 12582912
  194.7 0.7 copy-start.15
  194.7 149.4 %copy-start.1 = (bf16[40,1,128,128]{3,2,1,0:T(8,128)(2,1)S(1)}, bf16[40,1,128,128]{3,2,1,0:T(8,128)(2,1)}, u32[]{:S(2)}) copy-start(bf16[40,1,128,128]{3,2,1,0:T(8,128)(2,1)} %param.21) | copy-start | bytes 3932164
  194.7 148.4 %copy-start.10 = (f32[16,2]{0,1:T(2,128)S(1)}, f32[16,2]{0,1:T(2,128)}, u32[]{:S(2)}) copy-start(f32[16,2]{0,1:T(2,128)} %param.28) | copy-start | bytes 388
Sparse Core Ops, SparseCore 0:
  36.6 35.9 all-reduce.3
  83.4 60.9 all-gather.1
  194.9 137.5 all-reduce.5
where the time goes:
time: 351 us
  waiting for transfers between devices  231 us (66%)
  matrix products  48.2 us (14%)
  local copies, waits for them, and re-layouts  33.5 us (10%)
  blocking collectives  18.2 us (5%)
  between operations  14.8 us (4%)
  other arithmetic  4.31 us (1%)
    unnamed x4, waiting for transfers between devices  136 us
    all_gather x1, waiting for transfers between devices, expert_pass(): row_piece = lax.all_gather(arrived, ('dp', 'tensor'), axis=0, tiled=True)  60.9 us
    psum x1, waiting for transfers between devices, local(): lax.psum(jnp.dot(heads_out, attention_merge_matrix, preferred_element_typ...  34.5 us
    dot_general x1, matrix products, expert_pass(): jnp.einsum('qesd,efd->qesf', row_piece, expand_matrices, preferred_elemen...  18.4 us
    dot_general x1, matrix products, expert_pass(): jnp.einsum('qesd,efd->qesf', row_piece, gating_matrices, preferred_elemen...  15.5 us
    all_to_all x1, blocking collectives, expert_pass(): lax.all_to_all(summed, 'expert', split_axis=0, concat_axis=0, tiled=True)  9.18 us
    all_to_all x1, blocking collectives, expert_pass(): lax.all_to_all(send.reshape(holders, local_count, slot_count, model_width...  8.98 us
    dot_general x1, matrix products, expert_pass(): jnp.einsum('qesf,efd->qesd', hidden, contract_matrices, preferred_element...  8.87 us
  transfers between devices with their start and end apart: 3, of which 3 were waited for; matrix products, arithmetic and copies ran while one was open for 0% of the time, Pallas kernels for 0%

commit v1 on v0

--- a/solution.py
+++ b/solution.py
@@ -4,6 +4,8 @@
 import jax
 import jax.numpy as jnp
 from jax import lax
+from jax.experimental import pallas as pl
+from jax.experimental.pallas import tpu as pltpu
 from jax.sharding import PartitionSpec as P
 
 HD = 128
@@ -214,6 +216,446 @@
     return (wide + mixed).astype(jnp.bfloat16)
 
 
+PAIRS_CORE = [(0, 1), (1, 0), (2, 3), (3, 2)]
+PAIRS_Y = [(0, 2), (2, 0), (1, 3), (3, 1)]
+PAIRS_X = [(0, 1), (1, 0)]
+SINGLES = 16
+PROMPT = 48
+CAP_MOST = 3
+NEG = -1e30
+MIB = 1 << 20
+
+
+def over_core(a):
+    return lax.ppermute(a, "tensor", PAIRS_CORE)
+
+
+def over_y(a):
+    return lax.ppermute(a, "tensor", PAIRS_Y)
+
+
+def over_x(a):
+    return lax.ppermute(a, "expert", PAIRS_X)
+
+
+def over_z(a, k):
+    return lax.ppermute(a, "dp", [(i, i ^ k) for i in range(4)])
+
+
+def dot_nt(a, b):
+    return lax.dot_general(a, b, (((1,), (1,)), ((), ())), preferred_element_type=jnp.float32)
+
+
+def dot_nn(a, b):
+    return lax.dot_general(a, b, (((1,), (0,)), ((), ())), preferred_element_type=jnp.float32)
+
+
+def attend_kernel(
+    place, table_s, table_v, counts_v, counts_s, q, k_new, v_new, k_hbm, v_hbm, w_hbm,
+    send, keep,
+    k_pool, v_pool, w_out, scores, times, weights, k_prompt, v_prompt, heads, ordered, sems,
+):
+    pool_rows = k_pool.shape[0]
+    pages = pool_rows // 128
+    slots = table_v.shape[1]
+    group = q.shape[1] // HD
+    copies = [
+        pltpu.make_async_copy(src, dst, sems.at[i])
+        for i, (src, dst) in enumerate(((k_hbm, k_pool), (v_hbm, v_pool), (w_hbm, w_out)))
+    ]
+    for copy in copies:
+        copy.start()
+    root = 1.0 / math.sqrt(HD)
+
+    lane = lax.broadcasted_iota(jnp.int32, (SINGLES, 128), 1)
+    spans = jnp.broadcast_to(counts_v[0:SINGLES, :], (SINGLES, 128))
+    named = [jnp.broadcast_to(table_v[0:SINGLES, m : m + 1], (SINGLES, 128)) for m in range(slots)]
+    seen = [jnp.where(lane + m * 128 < spans, 1.0, 0.0) for m in range(slots)]
+    for page in range(pages):
+        total = jnp.zeros((SINGLES, 128), jnp.float32)
+        for m in range(slots):
+            total = total + jnp.where(named[m] == page, seen[m], 0.0)
+        times[:, page * 128 : (page + 1) * 128] = total
+
+    copies[0].wait()
+    q_single = jnp.concatenate([q[0:SINGLES, h * HD : (h + 1) * HD] for h in range(group)], axis=0)
+    q_prompt = jnp.concatenate([q[SINGLES:, h * HD : (h + 1) * HD] for h in range(group)], axis=0)
+    step = 1024
+    for start in range(0, pool_rows, step):
+        scores[:, start : start + step] = dot_nt(q_single, k_pool[start : start + step, :])
+    for m in range(slots):
+        page = table_s[SINGLES, m]
+        k_prompt[m * 128 : (m + 1) * 128, :] = k_pool[pl.ds(pl.multiple_of(page * 128, 128), 128), :]
+    s_cache = dot_nt(q_prompt, k_prompt[...]) * root
+    s_new = dot_nt(q_prompt, k_new[SINGLES:, :]) * root
+    own = k_new[0:SINGLES, :].astype(jnp.float32)
+
+    denominators, own_parts = [], []
+    for h in range(group):
+        rows = slice(h * SINGLES, (h + 1) * SINGLES)
+        often = times[...]
+        s = jnp.where(often > 0.0, scores[rows, :] * root, NEG)
+        s_own = (
+            jnp.sum(q_single[rows, :].astype(jnp.float32) * own, axis=1, keepdims=True) * root
+        )
+        highest = jnp.maximum(jnp.max(s, axis=1, keepdims=True), s_own)
+        p = jnp.exp(s - highest) * often
+        p_own = jnp.exp(s_own - highest)
+        denominators.append(jnp.sum(p, axis=1, keepdims=True) + p_own)
+        own_parts.append(p_own)
+        weights[rows, :] = p.astype(jnp.bfloat16)
+
+    position = lax.broadcasted_iota(jnp.int32, s_cache.shape, 1)
+    s_cache = jnp.where(position < counts_s[SINGLES], s_cache, NEG)
+    row = lax.broadcasted_iota(jnp.int32, (PROMPT, PROMPT), 0)
+    col = lax.broadcasted_iota(jnp.int32, (PROMPT, PROMPT), 1)
+    causal = jnp.concatenate([jnp.where(row >= col, 0.0, NEG)] * group, axis=0)
+    s_new = s_new + causal
+    highest = jnp.maximum(
+        jnp.max(s_cache, axis=1, keepdims=True), jnp.max(s_new, axis=1, keepdims=True)
+    )
+    p_cache = jnp.exp(s_cache - highest)
+    p_new = jnp.exp(s_new - highest)
+    denominator = jnp.sum(p_cache, axis=1, keepdims=True) + jnp.sum(p_new, axis=1, keepdims=True)
+
+    copies[1].wait()
+    for m in range(slots):
+        page = table_s[SINGLES, m]
+        v_prompt[m * 128 : (m + 1) * 128, :] = v_pool[pl.ds(pl.multiple_of(page * 128, 128), 128), :]
+    out_prompt = dot_nn(p_cache.astype(jnp.bfloat16), v_prompt[...])
+    out_prompt = out_prompt + dot_nn(p_new.astype(jnp.bfloat16), v_new[SINGLES:, :])
+    out_prompt = (out_prompt / denominator).astype(jnp.bfloat16)
+    out_single = dot_nn(weights[...], v_pool[...])
+    fresh = v_new[0:SINGLES, :].astype(jnp.float32)
+    for h in range(group):
+        lanes = slice(h * HD, (h + 1) * HD)
+        one = out_single[h * SINGLES : (h + 1) * SINGLES, :] + own_parts[h] * fresh
+        heads[0:SINGLES, lanes] = (one / denominators[h]).astype(jnp.bfloat16)
+        heads[SINGLES:, lanes] = out_prompt[h * PROMPT : (h + 1) * PROMPT, :]
+
+    t = place[0]
+    core, y = lax.rem(t, 2), lax.div(t, 2)
+    order = [(1 - y) * 2 + 1 - core, y * 2 + 1 - core, (1 - y) * 2 + core, y * 2 + core]
+    for i, block in enumerate(order):
+        ordered[i * 16 : (i + 1) * 16, :] = heads[pl.ds(pl.multiple_of(block * 16, 16), 16), :]
+    copies[2].wait()
+    for start in range(0, w_out.shape[1], 512):
+        part = dot_nn(ordered[...], w_out[:, start : start + 512]).astype(jnp.bfloat16)
+        send[:, start : start + 512] = part[0:32, :]
+        keep[:, start : start + 512] = part[32:64, :]
+
+
+def attention_call(place, table, counts, q, k_new, v_new, k_pool, v_pool, w_out):
+    pool_rows, rows, width = k_pool.shape[0], q.shape[0], w_out.shape[1]
+    vmem, smem, hbm = (pl.BlockSpec(memory_space=s) for s in (pltpu.VMEM, pltpu.SMEM, pl.ANY))
+    half = jax.ShapeDtypeStruct((rows // 2, width), jnp.bfloat16)
+    singles = SINGLES * (q.shape[1] // HD)
+    return pl.pallas_call(
+        attend_kernel,
+        out_shape=(half, half),
+        in_specs=[smem, smem, vmem, vmem, smem, vmem, vmem, vmem, hbm, hbm, hbm],
+        out_specs=(vmem, vmem),
+        scratch_shapes=[
+            pltpu.VMEM((pool_rows, HD), jnp.bfloat16),
+            pltpu.VMEM((pool_rows, HD), jnp.bfloat16),
+            pltpu.VMEM(w_out.shape, jnp.bfloat16),
+            pltpu.VMEM((singles, pool_rows), jnp.float32),
+            pltpu.VMEM((SINGLES, pool_rows), jnp.float32),
+            pltpu.VMEM((singles, pool_rows), jnp.bfloat16),
+            pltpu.VMEM((table.shape[1] * 128, HD), jnp.bfloat16),
+            pltpu.VMEM((table.shape[1] * 128, HD), jnp.bfloat16),
+            pltpu.VMEM((rows, q.shape[1]), jnp.bfloat16),
+            pltpu.VMEM((rows, q.shape[1]), jnp.bfloat16),
+            pltpu.SemaphoreType.DMA((3,)),
+        ],
+        compiler_params=pltpu.CompilerParams(vmem_limit_bytes=32 * MIB),
+        cost_estimate=pl.CostEstimate(flops=10**9, bytes_accessed=8 * 10**6, transcendentals=6 * 10**5),
+        name="attention",
+    )(place, table, table, counts[:, None], counts, q, k_new, v_new, k_pool, v_pool, w_out)
+
+
+def routes_kernel(hot, shares, pick, spread, scale):
+    rows, tokens = pick.shape
+    tile = scale.shape[0] // 5
+    share = shares[...]
+    kept = jnp.where(share > 0.0, 1.0, 0.0)
+    below = lax.broadcasted_iota(jnp.int32, (tokens, tokens), 1) < lax.broadcasted_iota(
+        jnp.int32, (tokens, tokens), 0
+    )
+    rank = dot_nn(jnp.where(below, 1.0, 0.0).astype(jnp.bfloat16), kept.astype(jnp.bfloat16))
+    lane = lax.broadcasted_iota(jnp.int32, share.shape, 1)
+    favored = hot[0]
+    base = lane * tile + jnp.where((favored >= 0) & (lane > favored), tile, 0)
+    place = jnp.where(kept > 0.0, rank + base.astype(jnp.float32), -1.0)
+    place_t = place.T
+    row_id = lax.broadcasted_iota(jnp.int32, (rows, tokens), 0).astype(jnp.float32)
+    col_id = lax.broadcasted_iota(jnp.int32, (tokens, rows), 1).astype(jnp.float32)
+    picked = jnp.zeros((rows, tokens), jnp.float32)
+    spreading = jnp.zeros((tokens, rows), jnp.float32)
+    for e in range(4):
+        picked = picked + jnp.where(row_id == place_t[e : e + 1, :], 1.0, 0.0)
+        spreading = spreading + jnp.where(col_id == place[:, e : e + 1], 1.0, 0.0)
+    picked = picked.astype(jnp.bfloat16)
+    pick[...] = picked
+    spread[...] = spreading.astype(jnp.bfloat16)
+    found = jnp.zeros((rows, share.shape[1]), jnp.float32)
+    rest = share
+    for _ in range(3):
+        part = rest.astype(jnp.bfloat16)
+        found = found + dot_nn(picked, part)
+        rest = rest - part.astype(jnp.float32)
+    row = lax.broadcasted_iota(jnp.int32, found.shape, 0)
+    column = lax.broadcasted_iota(jnp.int32, found.shape, 1)
+    first = column * tile + jnp.where((favored >= 0) & (column > favored), tile, 0)
+    size = jnp.where(column == favored, 2 * tile, tile)
+    mine = (row >= first) & (row < first + size) & (column < 4)
+    total = jnp.sum(jnp.where(mine, found, 0.0), axis=1, keepdims=True)
+    scale[...] = jnp.broadcast_to(total, scale.shape)
+
+
+def routes_call(hot, shares, tile):
+    tokens = shares.shape[0]
+    vmem, smem = (pl.BlockSpec(memory_space=s) for s in (pltpu.VMEM, pltpu.SMEM))
+    return pl.pallas_call(
+        routes_kernel,
+        out_shape=(
+            jax.ShapeDtypeStruct((5 * tile, tokens), jnp.bfloat16),
+            jax.ShapeDtypeStruct((tokens, 5 * tile), jnp.bfloat16),
+            jax.ShapeDtypeStruct((5 * tile, 128), jnp.float32),
+        ),
+        in_specs=[smem, vmem],
+        out_specs=(vmem, vmem, vmem),
+        compiler_params=pltpu.CompilerParams(vmem_limit_bytes=32 * MIB),
+        cost_estimate=pl.CostEstimate(flops=10**8, bytes_accessed=10**6, transcendentals=0),
+        name="routes",
+    )(hot, shares)
+
+
+def experts_kernel(
+    hot, a0, a1, a2, a3, b0, b1, b2, b3, pick, spread, scale, gate, up, down,
+    a_send, a_keep, b_send, b_keep,
+    tokens, taken, total, made, sems,
+):
+    expert, chunk = pl.program_id(0), pl.program_id(1)
+    last = pl.num_programs(1) - 1
+    tile = made.shape[0] // 5
+    half = tokens.shape[1] // 2
+    favored = hot[0]
+
+    @pl.when((expert == 0) & (chunk == 0))
+    def _():
+        copies = []
+        for i, ref in enumerate((a0, a1, a2, a3)):
+            copies.append((ref, tokens.at[i * 128 : (i + 1) * 128, 0:half]))
+        for i, ref in enumerate((b0, b1, b2, b3)):
+            for j in range(2):
+                first = (i // 2) * 256 + j * 128 + (i % 2) * 64
+                copies.append(
+                    (ref.at[j * 64 : (j + 1) * 64, :], tokens.at[first : first + 64, half:])
+                )
+        started = []
+        for i, (src, dst) in enumerate(copies):
+            copy = pltpu.make_async_copy(src, dst, sems.at[i])
+            copy.start()
+            started.append(copy)
+        made[4 * tile :, :] = jnp.zeros_like(made[4 * tile :, :])
+        for copy in started:
+            copy.wait()
+
+        @pl.loop(0, tokens.shape[1], step=512)
+        def _(start):
+            cols = pl.ds(pl.multiple_of(start, 512), 512)
+            taken[:, cols] = dot_nn(pick[...], tokens[:, cols]).astype(jnp.bfloat16)
+
+    first = expert * tile + jnp.where((favored >= 0) & (expert > favored), tile, 0)
+
+    def run(rows):
+        span = pl.ds(pl.multiple_of(first, 32), rows)
+        x = taken[span, :]
+        g = dot_nt(x, gate[0])
+        u = dot_nt(x, up[0])
+        act = (g / (1.0 + jnp.exp(-g)) * u).astype(jnp.bfloat16)
+        part = scale[span, 0:1]
+
+        @pl.when(chunk == 0)
+        def _():
+            total[0:rows, :] = dot_nn(act, down[0])
+
+        @pl.when(chunk > 0)
+        def _():
+            total[0:rows, :] += dot_nn(act, down[0])
+
+        @pl.when(chunk == last)
+        def _():
+            made[span, :] = (total[0:rows, :] * part).astype(jnp.bfloat16)
+
+    @pl.when(expert == favored)
+    def _():
+        run(2 * tile)
+
+    @pl.when(expert != favored)
+    def _():
+        run(tile)
+
+    @pl.when((expert == pl.num_programs(0) - 1) & (chunk == last))
+    def _():
+        rows = tokens.shape[0] // 2
+        for i, (out_keep, out_send) in enumerate(((a_keep, a_send), (b_keep, b_send))):
+
+            @pl.loop(0, half, step=512)
+            def _(start, i=i, out_keep=out_keep, out_send=out_send):
+                cols = pl.ds(pl.multiple_of(start, 512), 512)
+                source = pl.ds(pl.multiple_of(i * half + start, 512), 512)
+                y = dot_nn(spread[...], made[:, source]).astype(jnp.bfloat16)
+                for side, out in enumerate((out_keep, out_send)):
+                    for j in range(4):
+                        to = j if i == 0 else (j % 2) * 2 + j // 2
+                        out[to * 64 : (to + 1) * 64, cols] = y[side * rows + j * 64 : side * rows + (j + 1) * 64, :]
+
+
+def experts_call(hot, pieces, pick, spread, scale, gate, up, down):
+    experts, hidden, width = gate.shape
+    tokens = spread.shape[0]
+    rows = pick.shape[0]
+    tile = rows // 5
+    chunk = hidden // 2
+    vmem, smem, hbm = (pl.BlockSpec(memory_space=s) for s in (pltpu.VMEM, pltpu.SMEM, pl.ANY))
+    weight = pl.BlockSpec((1, chunk, width), lambda e, c: (e, c, 0))
+    out = jax.ShapeDtypeStruct((tokens // 2, width // 2), jnp.bfloat16)
+    return pl.pallas_call(
+        experts_kernel,
+        grid=(experts, 2),
+        out_shape=(out, out, out, out),
+        in_specs=[smem] + [hbm] * 8 + [vmem] * 3 + [weight] * 3,
+        out_specs=(vmem,) * 4,
+        scratch_shapes=[
+            pltpu.VMEM((tokens, width), jnp.bfloat16),
+            pltpu.VMEM((rows, width), jnp.bfloat16),
+            pltpu.VMEM((2 * tile, width), jnp.float32),
+            pltpu.VMEM((rows, width), jnp.bfloat16),
+            pltpu.SemaphoreType.DMA((12,)),
+        ],
+        compiler_params=pltpu.CompilerParams(vmem_limit_bytes=50 * MIB),
+        cost_estimate=pl.CostEstimate(
+            flops=6 * rows * hidden * width, bytes_accessed=experts * 6 * hidden * width, transcendentals=rows * hidden
+        ),
+        name="experts",
+    )(hot, *pieces, pick, spread, scale, gate, up, down)
+
+
+def kept_shares(chosen_specialists, selection_shares, allowed_placements, favored_specialist):
+    count, experts = chosen_specialists.shape[0], allowed_placements.shape[0]
+    index = jnp.arange(experts, dtype=jnp.int32)
+    picked = chosen_specialists[:, :, None] == index[None, None, :]
+    named = jnp.any(picked, axis=1)
+    earlier = jnp.arange(count)[:, None] > jnp.arange(count)[None, :]
+    before = jnp.dot(
+        earlier.astype(jnp.bfloat16), named.astype(jnp.bfloat16), preferred_element_type=jnp.float32
+    )
+    limit = jnp.where(index == favored_specialist[0], PLACEMENT_MOST, allowed_placements)
+    share = jnp.sum(jnp.where(picked, selection_shares[:, :, None], 0.0), axis=1)
+    return jnp.where(before < limit[None, :].astype(jnp.float32), share, 0.0)
+
+
+def joined(*parts):
+    return jnp.concatenate(parts, axis=0)
+
+
+def plus(a, b):
+    return (a.astype(jnp.float32) + b.astype(jnp.float32)).astype(jnp.bfloat16)
+
+
+def local_fast(
+    skip_stream_entry,
+    question_vectors,
+    fresh_lookup_vectors,
+    fresh_content_vectors,
+    stored_lookup_sheets,
+    stored_content_sheets,
+    sequence_sheet_map,
+    stored_position_counts,
+    attention_merge_matrix,
+    premix_scale_factor,
+    chosen_specialists,
+    selection_shares,
+    allowed_placements,
+    favored_specialist,
+    gating_matrices,
+    expand_matrices,
+    contract_matrices,
+):
+    width = skip_stream_entry.shape[1]
+    half = width // 2
+    own_experts = gating_matrices.shape[0]
+    count = chosen_specialists.shape[0]
+    z, x, t = (lax.axis_index(name) for name in ("dp", "expert", "tensor"))
+
+    shares = kept_shares(chosen_specialists, selection_shares, allowed_placements, favored_specialist)
+    shares = lax.all_gather(shares, ("dp", "expert", "tensor"), axis=0, tiled=True)
+    away = jnp.arange(32, dtype=jnp.int32)
+    block = ((z ^ (away % 4)) * 2 + (x ^ (away // 4 % 2))) * 4 + (t ^ (away // 8 % 2 * 2 + away // 16))
+    shares = lax.dynamic_slice_in_dim(shares, x * own_experts, own_experts, 1)
+    shares = shares.reshape(32, count, own_experts)[block].reshape(32 * count, own_experts)
+    shares = jnp.pad(shares, ((0, 0), (0, 128 - own_experts)))
+    hot = favored_specialist - x * own_experts
+    hot = jnp.where((hot >= 0) & (hot < own_experts), hot, -1).astype(jnp.int32)
+    pick, spread, scale = routes_call(hot, shares, CAP_MOST * 32)
+
+    send, keep = attention_call(
+        t.astype(jnp.int32)[None],
+        sequence_sheet_map,
+        stored_position_counts,
+        question_vectors,
+        fresh_lookup_vectors,
+        fresh_content_vectors,
+        stored_lookup_sheets.reshape(-1, HD),
+        stored_content_sheets.reshape(-1, HD),
+        attention_merge_matrix,
+    )
+    got = over_core(send)
+    far = plus(got[0:count], keep[0:count])
+    near = plus(got[count:], keep[count:])
+    own_attn = over_y(far).astype(jnp.float32) + near.astype(jnp.float32)
+    stream = (skip_stream_entry.astype(jnp.float32) + own_attn).astype(jnp.bfloat16)
+    wide = stream.astype(jnp.float32)
+    squares = jnp.mean(wide * wide, axis=1, keepdims=True)
+    normed = (wide * lax.rsqrt(squares + 1e-05) * premix_scale_factor.astype(jnp.float32)).astype(
+        jnp.bfloat16
+    )
+
+    pieces = []
+    for i, (first, second) in enumerate(((over_x, over_y), (over_y, over_x))):
+        part = normed[:, i * half : (i + 1) * half]
+        part = joined(part, over_z(part, 1), over_z(part, 2), over_z(part, 3))
+        part = joined(part, first(part))
+        other = second(part)
+        pieces += [part, other, over_core(part), over_core(other)]
+    a_send, a_keep, b_send, b_keep = experts_call(
+        hot, pieces, pick, spread, scale, gating_matrices, expand_matrices, contract_matrices
+    )
+    results = []
+    for sent, kept, first, second in (
+        (a_send, a_keep, over_y, over_x),
+        (b_send, b_keep, over_x, over_y),
+    ):
+        got = over_core(sent)
+        rows = kept.shape[0] // 2
+        far = plus(got[rows:], kept[rows:])
+        near = plus(got[:rows], kept[:rows])
+        got = first(far)
+        rows = rows // 2
+        far = plus(got[rows:], near[rows:])
+        near = plus(got[:rows], near[:rows])
+        got = second(far)
+        total = near.astype(jnp.float32) + got.astype(jnp.float32)
+        out = total[0:count]
+        for k in (1, 2, 3):
+            mine = total[k * count : (k + 1) * count].astype(jnp.bfloat16)
+            out = out + over_z(mine, k).astype(jnp.float32)
+        results.append(out)
+    return (wide + jnp.concatenate(results, axis=1)).astype(jnp.bfloat16)
+
+
 def solution(mesh):
     placed = (
         P(("dp", "expert", "tensor"), None),
@@ -234,8 +676,9 @@
         P("expert", ("dp", "tensor"), None),
         P("expert", ("dp", "tensor"), None),
     )
+    sizes = tuple(mesh.shape[name] for name in ("dp", "expert", "tensor"))
     return jax.shard_map(
-        local,
+        local_fast if sizes == (4, 2, 4) else local,
         mesh=mesh,
         in_specs=placed,
         out_specs=P(("dp", "expert", "tensor"), None),

time: 351 us -> 178 us (0.51)
  waiting for transfers between devices: 231 us -> 49.6 us
  matrix products: 48.2 us -> 0.07 us
  Pallas kernels: 0 us -> 37.2 us
  starting transfers between devices: 0.27 us -> 28.1 us
  blocking collectives: 18.2 us -> 39.8 us
  local copies, waits for them, and re-layouts: 33.5 us -> 13 us
  between operations: 14.8 us -> 0.95 us
  other arithmetic: 4.31 us -> 8.31 us
    unnamed x4 -> x0, waiting for transfers between devices: 136 us -> none
    all_gather x1 -> x0, waiting for transfers between devices: 60.9 us -> none  [expert_pass(): row_piece = lax.all_gather(arrived, ('dp', 'tensor'), axis=0, tiled=True)]
    ppermute x0 -> x28, waiting for transfers between devices: none -> 49.6 us  [the longest x5 22.5 us: over_y(): return lax.ppermute(a, 'tensor', PAIRS_Y)]
    dot_general x13 -> x1, matrix products: 48.2 us -> 0.07 us  [kept_shares(): jnp.dot(earlier.astype(jnp.bfloat16), named.astype(jnp.bfloat16), preferr...]
    all_gather x0 -> x1, blocking collectives: none -> 39.8 us  [local_fast(): lax.all_gather(shares, ('dp', 'expert', 'tensor'), axis=0, tiled=True)]
    pallas_call x0 -> x3, Pallas kernels: none -> 37.2 us  [the longest x1 31.5 us: experts_call(): pl.pallas_call(experts_kernel, grid=(experts, 2), out_shape=(out, out, ou...]
    psum x1 -> x0, waiting for transfers between devices: 34.5 us -> none  [local(): lax.psum(jnp.dot(heads_out, attention_merge_matrix, preferred_element_typ...]
    ppermute x0 -> x28, starting transfers between devices: none -> 28.1 us  [the longest x12 14.7 us: over_z(): return lax.ppermute(a, 'dp', [(i, i ^ k) for i in range(4)])]
  transfers between devices with their start and end apart: 3 -> 28, of which waited for: 3 -> 14; matrix products, arithmetic and copies ran while one was open for 0% -> 5% of each run, Pallas kernels for 0% -> 1%
where the time goes in v1:
time: 178 us; the launch traced here: 177 us
  waiting for transfers between devices  49.6 us (28%)
  blocking collectives  39.8 us (22%)
  Pallas kernels  37.2 us (21%)
  starting transfers between devices  28.1 us (16%)
  local copies, waits for them, and re-layouts  13 us (7%)
  other arithmetic  8.31 us (5%)
    all_gather x1, blocking collectives, local_fast(): lax.all_gather(shares, ('dp', 'expert', 'tensor'), axis=0, tiled=True)  39.8 us
    pallas_call x1, Pallas kernels, experts_call(): pl.pallas_call(experts_kernel, grid=(experts, 2), out_shape=(out, out, ou...  31.5 us
    ppermute x5, waiting for transfers between devices, over_y(): return lax.ppermute(a, 'tensor', PAIRS_Y)  22.5 us
    ppermute x12, starting transfers between devices, over_z(): return lax.ppermute(a, 'dp', [(i, i ^ k) for i in range(4)])  14.7 us
    ppermute x12, waiting for transfers between devices, over_z(): return lax.ppermute(a, 'dp', [(i, i ^ k) for i in range(4)])  11.9 us
    ppermute x4, waiting for transfers between devices, over_x(): return lax.ppermute(a, 'expert', PAIRS_X)  11.6 us
    unnamed x24, local copies, waits for them, and re-layouts  9.46 us
    ppermute x5, starting transfers between devices, over_y(): return lax.ppermute(a, 'tensor', PAIRS_Y)  8.53 us
  transfers between devices with their start and end apart: 28, of which 14 were waited for; matrix products, arithmetic and copies ran while one was open for 5% of the time, Pallas kernels for 1%

profile of v1, /device:TPU:0, one launch (start us, length us, event | category | flops | bytes accessed | tf_op | source)
XLA Modules:
  0.0 177.0 jit_solution(6255232774570264121)
XLA Ops:
  0.0 0.8 copy.45.table_s.table_v
  0.8 0.7 copy.47.counts_v
  1.5 2.2 %copy-done = bf16[512,4096]{1,0:T(8,128)(2,1)S(1)} copy-done((bf16[512,4096]{1,0:T(8,128)(2,1)S(1)}, bf16[512,4096]{1,0:T(8,128)(2,1)}, u32[]{:S(2)}) %copy-start) | copy-done | bytes 4194328
  3.7 1.3 copy-done.1
  5.0 1.3 copy-done.2
  6.3 0.8 copy-done.4
  7.2 0.7 copy-done.5
  7.9 0.7 copy-done.6
  8.6 0.7 copy-done.7
  9.3 4.1 %attention.1 = (bf16[32,4096]{1,0:T(8,128)(2,1)S(1)}, bf16[32,4096]{1,0:T(8,128)(2,1)S(1)}) custom-call(s32[1]{0:T(128)} %bitcast.place, s32[17,8]{1,0:T(8,128)S(1)} %copy.45.table_s.table_v, s32[17,8]{1,0:T(8,128)S(1)} %copy.45.table_s.table_v, s32[17,1]{1,0:T(8,128)S(1)} %copy.47.counts_v, s32[17]{0:T(128)S(1)} %copy-done.7, ...), custom_call_target="tpu_custom_call" | custom-call | flops 1000000000 | bytes 8000000 | tf_op jit(solution)/shard_map/attention/pallas_call | solution.py:353
  13.4 0.5 collective-permute-start
  13.9 1.2 collective-permute-done
  15.1 3.0 %collective-permute-start.1 = (bf16[16,4096]{1,0:T(8,128)(2,1)S(1)}, bf16[16,4096]{1,0:T(8,128)(2,1)S(1)}, u32[]{:S(2)}, u32[]{:S(2)}) collective-permute-start(bf16[16,4096]{1,0:T(8,128)(2,1)S(1)} %add_convert_fusion.10), channel_id=1, source_target_pairs={{0,2},{2,0},{1,3},{3,1},{4,6},{6,4},{5,7},{7,5},{8,10},{10,8},{9,1... | collective-permute-start | bytes 393224 | tf_op jit(solution)/shard_map/ppermute | solution.py:234
  18.1 0.7 convert_element_type.169
  18.8 3.1 %collective-permute-done.1 = bf16[16,4096]{1,0:T(8,128)(2,1)S(1)} collective-permute-done((bf16[16,4096]{1,0:T(8,128)(2,1)S(1)}, bf16[16,4096]{1,0:T(8,128)(2,1)S(1)}, u32[]{:S(2)}, u32[]{:S(2)}) %collective-permute-start.1) | collective-permute-done | bytes 131104 | tf_op jit(solution)/shard_map/ppermute | solution.py:234
  21.9 1.1 fusion.2
  23.0 0.1 fusion.4
  23.1 3.9 %collective-permute-start.4 = (bf16[16,2048]{1,0:T(8,128)(2,1)S(1)}, bf16[16,2048]{1,0:T(8,128)(2,1)S(1)}, u32[]{:S(2)}, u32[]{:S(2)}) collective-permute-start(bf16[16,2048]{1,0:T(8,128)(2,1)S(1)} %get-tuple-element.42), channel_id=1, source_target_pairs={{0,24},{8,16},{16,8},{24,0},{1,25},{9,17},{17,9},{25,1},{2,26},{10... | collective-permute-start | bytes 196616 | tf_op jit(solution)/shard_map/ppermute | solution.py:242
  27.0 0.6 collective-permute-start.2
  27.7 3.7 %collective-permute-start.11 = (bf16[16,2048]{1,0:T(8,128)(2,1)S(1)}, bf16[16,2048]{1,0:T(8,128)(2,1)S(1)}, u32[]{:S(2)}, u32[]{:S(2)}) collective-permute-start(bf16[16,2048]{1,0:T(8,128)(2,1)S(1)} %get-tuple-element.39), channel_id=1, source_target_pairs={{0,24},{8,16},{16,8},{24,0},{1,25},{9,17},{17,9},{25,1},{2,26},{10... | collective-permute-start | bytes 196616 | tf_op jit(solution)/shard_map/ppermute | solution.py:242
  31.4 0.6 collective-permute-start.9
  32.1 3.1 %collective-permute-done.3 = bf16[16,2048]{1,0:T(8,128)(2,1)S(1)} collective-permute-done((bf16[16,2048]{1,0:T(8,128)(2,1)S(1)}, bf16[16,2048]{1,0:T(8,128)(2,1)S(1)}, u32[]{:S(2)}, u32[]{:S(2)}) %collective-permute-start.3) | collective-permute-done | bytes 65568 | tf_op jit(solution)/shard_map/ppermute | solution.py:242
  35.2 1.6 collective-permute-start.5
  36.8 1.0 collective-permute-done.10
  37.9 1.6 collective-permute-start.12
  39.5 5.6 %collective-permute-done.12 = bf16[64,2048]{1,0:T(8,128)(2,1)S(1)} collective-permute-done((bf16[64,2048]{1,0:T(8,128)(2,1)S(1)}, bf16[64,2048]{1,0:T(8,128)(2,1)S(1)}, u32[]{:S(2)}, u32[]{:S(2)}) %collective-permute-start.12) | collective-permute-done | bytes 262176 | tf_op jit(solution)/shard_map/ppermute | solution.py:234
  45.2 1.6 collective-permute-start.13
  46.7 1.6 collective-permute-start.6
  49.0 0.7 select_reduce_fusion
  49.7 0.7 fusion.13
  50.3 0.5 collective-permute-start.7
  50.8 6.3 %collective-permute-done.13.b1 = bf16[128,2048]{1,0:T(8,128)(2,1)S(1)} collective-permute-done((bf16[128,2048]{1,0:T(8,128)(2,1)S(1)}, bf16[128,2048]{1,0:T(8,128)(2,1)S(1)}, u32[]{:S(2)}, u32[]{:S(2)}) %collective-permute-start.13) | collective-permute-done | bytes 524320 | tf_op jit(solution)/shard_map/ppermute | solution.py:238
  57.1 1.3 collective-permute-done.6.a1
  58.4 0.7 fusion.10
  59.2 39.8 %all-gather = f32[32,16,8]{1,2,0:T(8,128)S(1)} all-gather(f32[1,16,8]{1,2,0:T(8,128)S(1)} %fusion.1), channel_id=1, replica_groups=mesh['dp'=4,'expert'=2,'tensor'=4] {'dp','expert','tensor'}, dimensions={0}, use_global_device_ids=true | all-gather | bytes 16896 | tf_op jit(solution)/shard_map/all_gather | solution.py:594
  99.0 0.1 reshape.237
  99.2 0.1 reshape.226
  99.3 0.6 gather_fusion
  100.0 1.0 copy.50
  100.9 1.0 pad.4.shares
  101.9 1.6 routes.1
  103.5 0.8 copy-done.3
  104.3 31.5 %experts.1 = (bf16[256,2048]{1,0:T(8,128)(2,1)}, bf16[256,2048]{1,0:T(8,128)(2,1)}, bf16[256,2048]{1,0:T(8,128)(2,1)}, bf16[256,2048]{1,0:T(8,128)(2,1)}) custom-call(s32[1]{0:T(128)S(6)} %select_n.97.hot, bf16[128,2048]{1,0:T(8,128)(2,1)S(1)} %constant_dynamic-update-slice_fusion.a0, bf16[128,2048]{1,0:T(8,128)(2,1)S(1)} %collective-permute-done.6.a1, ...), custom_call_target="tpu_custom_call" | custom-call | flops 5284823040 | bytes 44040192 | tf_op jit(solution)/shard_map/experts/pallas_call | solution.py:525
  135.8 0.4 collective-permute-start.16
  136.2 0.2 collective-permute-start.22
  136.3 2.4 %collective-permute-done.16 = bf16[256,2048]{1,0:T(8,128)(2,1)S(1)} collective-permute-done((bf16[256,2048]{1,0:T(8,128)(2,1)}, bf16[256,2048]{1,0:T(8,128)(2,1)S(1)}, u32[]{:S(2)}, u32[]{:S(2)}) %collective-permute-start.16) | collective-permute-done | bytes 1048608 | tf_op jit(solution)/shard_map/ppermute | solution.py:230
  138.7 1.6 add_convert_fusion.3
  140.3 0.1 collective-permute-start.17
  140.4 1.6 add_convert_fusion.1
  142.0 0.1 collective-permute-start.23
  142.1 12.5 %collective-permute-done.17 = bf16[128,2048]{1,0:T(8,128)(2,1)S(1)} collective-permute-done((bf16[128,2048]{1,0:T(8,128)(2,1)S(1)}, bf16[128,2048]{1,0:T(8,128)(2,1)S(1)}, u32[]{:S(2)}, u32[]{:S(2)}) %collective-permute-start.17) | collective-permute-done | bytes 524320 | tf_op jit(solution)/shard_map/ppermute | solution.py:234
  154.7 1.5 collective-permute-done.23
  156.3 2.3 %collective-permute-start.24 = (bf16[64,2048]{1,0:T(8,128)(2,1)S(1)}, bf16[64,2048]{1,0:T(8,128)(2,1)S(1)}, u32[]{:S(2)}, u32[]{:S(2)}) collective-permute-start(bf16[64,2048]{1,0:T(8,128)(2,1)S(1)} %add_convert_fusion.4), channel_id=1, source_target_pairs={{0,2},{2,0},{1,3},{3,1},{4,6},{6,4},{5,7},{7,5},{8,10},{10,8},{9,1... | collective-permute-start | bytes 786440 | tf_op jit(solution)/shard_map/ppermute | solution.py:234
  158.6 3.8 %collective-permute-done.18 = bf16[64,2048]{1,0:T(8,128)(2,1)S(1)} collective-permute-done((bf16[64,2048]{1,0:T(8,128)(2,1)S(1)}, bf16[64,2048]{1,0:T(8,128)(2,1)S(1)}, u32[]{:S(2)}, u32[]{:S(2)}) %collective-permute-start.18) | collective-permute-done | bytes 262176 | tf_op jit(solution)/shard_map/ppermute | solution.py:238
  162.4 0.1 fusion.25
  162.7 3.4 %collective-permute-start.20 = (bf16[16,2048]{1,0:T(8,128)(2,1)S(1)}, bf16[16,2048]{1,0:T(8,128)(2,1)S(1)}, u32[]{:S(2)}, u32[]{:S(2)}) collective-permute-start(bf16[16,2048]{1,0:T(8,128)(2,1)S(1)} %get-tuple-element.35), channel_id=1, source_target_pairs={{0,16},{8,24},{16,0},{24,8},{1,17},{9,25},{17,1},{25,9},{2,18},{10... | collective-permute-start | bytes 196616 | tf_op jit(solution)/shard_map/ppermute | solution.py:242
  166.1 0.1 fusion.26
  166.2 1.0 collective-permute-start.25
  167.3 0.5 collective-permute-start.27
  167.8 1.3 collective-permute-done.19
  169.1 0.7 collective-permute-start.26
  169.8 4.9 %collective-permute-done.20 = bf16[16,2048]{1,0:T(8,128)(2,1)S(1)} collective-permute-done((bf16[16,2048]{1,0:T(8,128)(2,1)S(1)}, bf16[16,2048]{1,0:T(8,128)(2,1)S(1)}, u32[]{:S(2)}, u32[]{:S(2)}) %collective-permute-start.20) | collective-permute-done | bytes 65568 | tf_op jit(solution)/shard_map/ppermute | solution.py:242
  174.8 1.5 collective-permute-done.26
  176.3 0.7 fusion.5
  (55 shorter events, 0.9 us)
Async XLA Ops:
  1.5 2.2 %copy-start = (bf16[512,4096]{1,0:T(8,128)(2,1)S(1)}, bf16[512,4096]{1,0:T(8,128)(2,1)}, u32[]{:S(2)}) copy-start(bf16[512,4096]{1,0:T(8,128)(2,1)} %w_hbm.1) | copy-start | bytes 12582916
  3.7 1.3 copy-start.1
  5.0 1.3 copy-start.2
  6.3 0.8 copy-start.4
  7.2 0.7 copy-start.5
  7.9 0.7 copy-start.6
  8.6 0.7 copy-start.7
  13.4 1.7 collective-permute-start
  15.1 6.8 %collective-permute-start.1 = (bf16[16,4096]{1,0:T(8,128)(2,1)S(1)}, bf16[16,4096]{1,0:T(8,128)(2,1)S(1)}, u32[]{:S(2)}, u32[]{:S(2)}) collective-permute-start(bf16[16,4096]{1,0:T(8,128)(2,1)S(1)} %add_convert_fusion.10), channel_id=1, source_target_pairs={{0,2},{2,0},{1,3},{3,1},{4,6},{6,4},{5,7},{7,5},{8,10},{10,8},{9,1... | collective-permute-start | bytes 393224 | tf_op jit(solution)/shard_map/ppermute | solution.py:234
  23.1 8.3 %collective-permute-start.4 = (bf16[16,2048]{1,0:T(8,128)(2,1)S(1)}, bf16[16,2048]{1,0:T(8,128)(2,1)S(1)}, u32[]{:S(2)}, u32[]{:S(2)}) collective-permute-start(bf16[16,2048]{1,0:T(8,128)(2,1)S(1)} %get-tuple-element.42), channel_id=1, source_target_pairs={{0,24},{8,16},{16,8},{24,0},{1,25},{9,17},{17,9},{25,1},{2,26},{10... | collective-permute-start | bytes 196616 | tf_op jit(solution)/shard_map/ppermute | solution.py:242
  27.0 8.2 %collective-permute-start.3 = (bf16[16,2048]{1,0:T(8,128)(2,1)S(1)}, bf16[16,2048]{1,0:T(8,128)(2,1)S(1)}, u32[]{:S(2)}, u32[]{:S(2)}) collective-permute-start(bf16[16,2048]{1,0:T(8,128)(2,1)S(1)} %get-tuple-element.42), channel_id=1, source_target_pairs={{0,16},{8,24},{16,0},{24,8},{1,17},{9,25},{17,1},{25,9},{2,18},{10... | collective-permute-start | bytes 196616 | tf_op jit(solution)/shard_map/ppermute | solution.py:242
  27.0 8.2 %collective-permute-start.2 = (bf16[16,2048]{1,0:T(8,128)(2,1)S(1)}, bf16[16,2048]{1,0:T(8,128)(2,1)S(1)}, u32[]{:S(2)}, u32[]{:S(2)}) collective-permute-start(bf16[16,2048]{1,0:T(8,128)(2,1)S(1)} %get-tuple-element.42), channel_id=1, source_target_pairs={{0,8},{8,0},{16,24},{24,16},{1,9},{9,1},{17,25},{25,17},{2,10},{10... | collective-permute-start | bytes 196616 | tf_op jit(solution)/shard_map/ppermute | solution.py:242
  27.7 9.1 %collective-permute-start.11 = (bf16[16,2048]{1,0:T(8,128)(2,1)S(1)}, bf16[16,2048]{1,0:T(8,128)(2,1)S(1)}, u32[]{:S(2)}, u32[]{:S(2)}) collective-permute-start(bf16[16,2048]{1,0:T(8,128)(2,1)S(1)} %get-tuple-element.39), channel_id=1, source_target_pairs={{0,24},{8,16},{16,8},{24,0},{1,25},{9,17},{17,9},{25,1},{2,26},{10... | collective-permute-start | bytes 196616 | tf_op jit(solution)/shard_map/ppermute | solution.py:242
  31.4 6.4 %collective-permute-start.10 = (bf16[16,2048]{1,0:T(8,128)(2,1)S(1)}, bf16[16,2048]{1,0:T(8,128)(2,1)S(1)}, u32[]{:S(2)}, u32[]{:S(2)}) collective-permute-start(bf16[16,2048]{1,0:T(8,128)(2,1)S(1)} %get-tuple-element.39), channel_id=1, source_target_pairs={{0,16},{8,24},{16,0},{24,8},{1,17},{9,25},{17,1},{25,9},{2,18},{10... | collective-permute-start | bytes 196616 | tf_op jit(solution)/shard_map/ppermute | solution.py:242
  31.4 6.4 %collective-permute-start.9 = (bf16[16,2048]{1,0:T(8,128)(2,1)S(1)}, bf16[16,2048]{1,0:T(8,128)(2,1)S(1)}, u32[]{:S(2)}, u32[]{:S(2)}) collective-permute-start(bf16[16,2048]{1,0:T(8,128)(2,1)S(1)} %get-tuple-element.39), channel_id=1, source_target_pairs={{0,8},{8,0},{16,24},{24,16},{1,9},{9,1},{17,25},{25,17},{2,10},{10... | collective-permute-start | bytes 196616 | tf_op jit(solution)/shard_map/ppermute | solution.py:242
  35.2 11.5 %collective-permute-start.5 = (bf16[64,2048]{1,0:T(8,128)(2,1)S(1)}, bf16[64,2048]{1,0:T(8,128)(2,1)S(1)}, u32[]{:S(2)}, u32[]{:S(2)}) collective-permute-start(bf16[64,2048]{1,0:T(8,128)(2,1)S(1)} %pad_maximum_fusion), channel_id=1, source_target_pairs={{0,4},{4,0},{1,5},{5,1},{2,6},{6,2},{3,7},{7,3},{8,12},{12,8},{9,1... | collective-permute-start | bytes 786440 | tf_op jit(solution)/shard_map/ppermute | solution.py:238
  37.9 7.3 %collective-permute-start.12 = (bf16[64,2048]{1,0:T(8,128)(2,1)S(1)}, bf16[64,2048]{1,0:T(8,128)(2,1)S(1)}, u32[]{:S(2)}, u32[]{:S(2)}) collective-permute-start(bf16[64,2048]{1,0:T(8,128)(2,1)S(1)} %pad_maximum_fusion.1), channel_id=1, source_target_pairs={{0,2},{2,0},{1,3},{3,1},{4,6},{6,4},{5,7},{7,5},{8,10},{10,8},{9,1... | collective-permute-start | bytes 786440 | tf_op jit(solution)/shard_map/ppermute | solution.py:234
  45.2 12.0 %collective-permute-start.13 = (bf16[128,2048]{1,0:T(8,128)(2,1)S(1)}, bf16[128,2048]{1,0:T(8,128)(2,1)S(1)}, u32[]{:S(2)}, u32[]{:S(2)}) collective-permute-start(bf16[128,2048]{1,0:T(8,128)(2,1)S(1)} %constant_dynamic-update-slice_fusion.5.b0), channel_id=1, source_target_pairs={{0,4},{4,0},{1,5},{5,1},{2,6},{6,2},{3,7},{7,3},{8,12},{12,8},{9,1... | collective-permute-start | bytes 1572872 | tf_op jit(solution)/shard_map/ppermute | solution.py:238
  46.7 11.7 %collective-permute-start.6 = (bf16[128,2048]{1,0:T(8,128)(2,1)S(1)}, bf16[128,2048]{1,0:T(8,128)(2,1)S(1)}, u32[]{:S(2)}, u32[]{:S(2)}) collective-permute-start(bf16[128,2048]{1,0:T(8,128)(2,1)S(1)} %constant_dynamic-update-slice_fusion.a0), channel_id=1, source_target_pairs={{0,2},{2,0},{1,3},{3,1},{4,6},{6,4},{5,7},{7,5},{8,10},{10,8},{9,1... | collective-permute-start | bytes 1572872 | tf_op jit(solution)/shard_map/ppermute | solution.py:234
  50.3 53.9 %collective-permute-start.14 = (bf16[128,2048]{1,0:T(8,128)(2,1)S(1)}, bf16[128,2048]{1,0:T(8,128)(2,1)}, u32[]{:S(2)}, u32[]{:S(2)}) collective-permute-start(bf16[128,2048]{1,0:T(8,128)(2,1)S(1)} %constant_dynamic-update-slice_fusion.5.b0), channel_id=1, source_target_pairs={{0,1},{1,0},{2,3},{3,2},{4,5},{5,4},{6,7},{7,6},{8,9},{9,8},{10,11... | collective-permute-start | bytes 1572872 | tf_op jit(solution)/shard_map/ppermute | solution.py:230
  50.3 53.9 %collective-permute-start.7 = (bf16[128,2048]{1,0:T(8,128)(2,1)S(1)}, bf16[128,2048]{1,0:T(8,128)(2,1)S(1)}, u32[]{:S(2)}, u32[]{:S(2)}) collective-permute-start(bf16[128,2048]{1,0:T(8,128)(2,1)S(1)} %constant_dynamic-update-slice_fusion.a0), channel_id=1, source_target_pairs={{0,1},{1,0},{2,3},{3,2},{4,5},{5,4},{6,7},{7,6},{8,9},{9,8},{10,11... | collective-permute-start | bytes 1572872 | tf_op jit(solution)/shard_map/ppermute | solution.py:230
  57.1 47.2 %collective-permute-start.15 = (bf16[128,2048]{1,0:T(8,128)(2,1)S(1)}, bf16[128,2048]{1,0:T(8,128)(2,1)}, u32[]{:S(2)}, u32[]{:S(2)}) collective-permute-start(bf16[128,2048]{1,0:T(8,128)(2,1)S(1)} %collective-permute-done.13.b1), channel_id=1, source_target_pairs={{0,1},{1,0},{2,3},{3,2},{4,5},{5,4},{6,7},{7,6},{8,9},{9,8},{10,11... | collective-permute-start | bytes 1572872 | tf_op jit(solution)/shard_map/ppermute | solution.py:230
  58.4 45.9 %collective-permute-start.8 = (bf16[128,2048]{1,0:T(8,128)(2,1)S(1)}, bf16[128,2048]{1,0:T(8,128)(2,1)S(1)}, u32[]{:S(2)}, u32[]{:S(2)}) collective-permute-start(bf16[128,2048]{1,0:T(8,128)(2,1)S(1)} %collective-permute-done.6.a1), channel_id=1, source_target_pairs={{0,1},{1,0},{2,3},{3,2},{4,5},{5,4},{6,7},{7,6},{8,9},{9,8},{10,11... | collective-permute-start | bytes 1572872 | tf_op jit(solution)/shard_map/ppermute | solution.py:230
  103.5 0.8 copy-start.3
  135.8 2.9 %collective-permute-start.16 = (bf16[256,2048]{1,0:T(8,128)(2,1)}, bf16[256,2048]{1,0:T(8,128)(2,1)S(1)}, u32[]{:S(2)}, u32[]{:S(2)}) collective-permute-start(bf16[256,2048]{1,0:T(8,128)(2,1)} %get-tuple-element.19), channel_id=1, source_target_pairs={{0,1},{1,0},{2,3},{3,2},{4,5},{5,4},{6,7},{7,6},{8,9},{9,8},{10,11... | collective-permute-start | bytes 3145736 | tf_op jit(solution)/shard_map/ppermute | solution.py:230
  136.2 4.2 %collective-permute-start.22 = (bf16[256,2048]{1,0:T(8,128)(2,1)}, bf16[256,2048]{1,0:T(8,128)(2,1)S(1)}, u32[]{:S(2)}, u32[]{:S(2)}) collective-permute-start(bf16[256,2048]{1,0:T(8,128)(2,1)} %get-tuple-element.21), channel_id=1, source_target_pairs={{0,1},{1,0},{2,3},{3,2},{4,5},{5,4},{6,7},{7,6},{8,9},{9,8},{10,11... | collective-permute-start | bytes 3145736 | tf_op jit(solution)/shard_map/ppermute | solution.py:230
  140.3 14.2 %collective-permute-start.17 = (bf16[128,2048]{1,0:T(8,128)(2,1)S(1)}, bf16[128,2048]{1,0:T(8,128)(2,1)S(1)}, u32[]{:S(2)}, u32[]{:S(2)}) collective-permute-start(bf16[128,2048]{1,0:T(8,128)(2,1)S(1)} %get-tuple-element.29), channel_id=1, source_target_pairs={{0,2},{2,0},{1,3},{3,1},{4,6},{6,4},{5,7},{7,5},{8,10},{10,8},{9,1... | collective-permute-start | bytes 1572872 | tf_op jit(solution)/shard_map/ppermute | solution.py:234
  142.0 14.2 %collective-permute-start.23 = (bf16[128,2048]{1,0:T(8,128)(2,1)S(1)}, bf16[128,2048]{1,0:T(8,128)(2,1)S(1)}, u32[]{:S(2)}, u32[]{:S(2)}) collective-permute-start(bf16[128,2048]{1,0:T(8,128)(2,1)S(1)} %get-tuple-element.31), channel_id=1, source_target_pairs={{0,4},{4,0},{1,5},{5,1},{2,6},{6,2},{3,7},{7,3},{8,12},{12,8},{9,1... | collective-permute-start | bytes 1572872 | tf_op jit(solution)/shard_map/ppermute | solution.py:238
  154.6 7.8 %collective-permute-start.18 = (bf16[64,2048]{1,0:T(8,128)(2,1)S(1)}, bf16[64,2048]{1,0:T(8,128)(2,1)S(1)}, u32[]{:S(2)}, u32[]{:S(2)}) collective-permute-start(bf16[64,2048]{1,0:T(8,128)(2,1)S(1)} %add_convert_fusion.6), channel_id=1, source_target_pairs={{0,4},{4,0},{1,5},{5,1},{2,6},{6,2},{3,7},{7,3},{8,12},{12,8},{9,1... | collective-permute-start | bytes 786440 | tf_op jit(solution)/shard_map/ppermute | solution.py:238
  156.3 9.8 %collective-permute-start.24 = (bf16[64,2048]{1,0:T(8,128)(2,1)S(1)}, bf16[64,2048]{1,0:T(8,128)(2,1)S(1)}, u32[]{:S(2)}, u32[]{:S(2)}) collective-permute-start(bf16[64,2048]{1,0:T(8,128)(2,1)S(1)} %add_convert_fusion.4), channel_id=1, source_target_pairs={{0,2},{2,0},{1,3},{3,1},{4,6},{6,4},{5,7},{7,5},{8,10},{10,8},{9,1... | collective-permute-start | bytes 786440 | tf_op jit(solution)/shard_map/ppermute | solution.py:234
  162.5 6.5 %collective-permute-start.19 = (bf16[16,2048]{1,0:T(8,128)(2,1)S(1)}, bf16[16,2048]{1,0:T(8,128)(2,1)S(1)}, u32[]{:S(2)}, u32[]{:S(2)}) collective-permute-start(bf16[16,2048]{1,0:T(8,128)(2,1)S(1)} %get-tuple-element.33), channel_id=1, source_target_pairs={{0,8},{8,0},{16,24},{24,16},{1,9},{9,1},{17,25},{25,17},{2,10},{10... | collective-permute-start | bytes 196616 | tf_op jit(solution)/shard_map/ppermute | solution.py:242
  162.6 7.2 %collective-permute-start.21 = (bf16[16,2048]{1,0:T(8,128)(2,1)S(1)}, bf16[16,2048]{1,0:T(8,128)(2,1)S(1)}, u32[]{:S(2)}, u32[]{:S(2)}) collective-permute-start(bf16[16,2048]{1,0:T(8,128)(2,1)S(1)} %get-tuple-element.34), channel_id=1, source_target_pairs={{0,24},{8,16},{16,8},{24,0},{1,25},{9,17},{17,9},{25,1},{2,26},{10... | collective-permute-start | bytes 196616 | tf_op jit(solution)/shard_map/ppermute | solution.py:242
  162.7 12.0 %collective-permute-start.20 = (bf16[16,2048]{1,0:T(8,128)(2,1)S(1)}, bf16[16,2048]{1,0:T(8,128)(2,1)S(1)}, u32[]{:S(2)}, u32[]{:S(2)}) collective-permute-start(bf16[16,2048]{1,0:T(8,128)(2,1)S(1)} %get-tuple-element.35), channel_id=1, source_target_pairs={{0,16},{8,24},{16,0},{24,8},{1,17},{9,25},{17,1},{25,9},{2,18},{10... | collective-permute-start | bytes 196616 | tf_op jit(solution)/shard_map/ppermute | solution.py:242
  166.2 8.5 %collective-permute-start.25 = (bf16[16,2048]{1,0:T(8,128)(2,1)S(1)}, bf16[16,2048]{1,0:T(8,128)(2,1)S(1)}, u32[]{:S(2)}, u32[]{:S(2)}) collective-permute-start(bf16[16,2048]{1,0:T(8,128)(2,1)S(1)} %get-tuple-element.36), channel_id=1, source_target_pairs={{0,8},{8,0},{16,24},{24,16},{1,9},{9,1},{17,25},{25,17},{2,10},{10... | collective-permute-start | bytes 196616 | tf_op jit(solution)/shard_map/ppermute | solution.py:242
  167.3 7.5 %collective-permute-start.27 = (bf16[16,2048]{1,0:T(8,128)(2,1)S(1)}, bf16[16,2048]{1,0:T(8,128)(2,1)S(1)}, u32[]{:S(2)}, u32[]{:S(2)}) collective-permute-start(bf16[16,2048]{1,0:T(8,128)(2,1)S(1)} %get-tuple-element.37), channel_id=1, source_target_pairs={{0,24},{8,16},{16,8},{24,0},{1,25},{9,17},{17,9},{25,1},{2,26},{10... | collective-permute-start | bytes 196616 | tf_op jit(solution)/shard_map/ppermute | solution.py:242
  169.1 7.2 %collective-permute-start.26 = (bf16[16,2048]{1,0:T(8,128)(2,1)S(1)}, bf16[16,2048]{1,0:T(8,128)(2,1)S(1)}, u32[]{:S(2)}, u32[]{:S(2)}) collective-permute-start(bf16[16,2048]{1,0:T(8,128)(2,1)S(1)} %get-tuple-element.38), channel_id=1, source_target_pairs={{0,16},{8,24},{16,0},{24,8},{1,17},{9,25},{17,1},{25,9},{2,18},{10... | collective-permute-start | bytes 196616 | tf_op jit(solution)/shard_map/ppermute | solution.py:242

commit v2 on v1

--- a/solution.py
+++ b/solution.py
@@ -1,3 +1,4 @@
+import functools
 from functools import reduce
 import math
 
@@ -251,13 +252,13 @@
 
 
 def attend_kernel(
-    place, table_s, table_v, counts_v, counts_s, q, k_new, v_new, k_hbm, v_hbm, w_hbm,
+    place, table, counts, q, k_new, v_new, k_hbm, v_hbm, w_hbm,
     send, keep,
     k_pool, v_pool, w_out, scores, times, weights, k_prompt, v_prompt, heads, ordered, sems,
 ):
     pool_rows = k_pool.shape[0]
     pages = pool_rows // 128
-    slots = table_v.shape[1]
+    slots = table.shape[0]
     group = q.shape[1] // HD
     copies = [
         pltpu.make_async_copy(src, dst, sems.at[i])
@@ -268,8 +269,13 @@
     root = 1.0 / math.sqrt(HD)
 
     lane = lax.broadcasted_iota(jnp.int32, (SINGLES, 128), 1)
-    spans = jnp.broadcast_to(counts_v[0:SINGLES, :], (SINGLES, 128))
-    named = [jnp.broadcast_to(table_v[0:SINGLES, m : m + 1], (SINGLES, 128)) for m in range(slots)]
+    request = lax.broadcasted_iota(jnp.int32, (SINGLES, 128), 0)
+    spans = jnp.zeros((SINGLES, 128), jnp.int32)
+    named = [spans] * slots
+    for r in range(SINGLES):
+        here = request == r
+        spans = jnp.where(here, counts[r], spans)
+        named = [jnp.where(here, table[m, r], named[m]) for m in range(slots)]
     seen = [jnp.where(lane + m * 128 < spans, 1.0, 0.0) for m in range(slots)]
     for page in range(pages):
         total = jnp.zeros((SINGLES, 128), jnp.float32)
@@ -284,7 +290,7 @@
     for start in range(0, pool_rows, step):
         scores[:, start : start + step] = dot_nt(q_single, k_pool[start : start + step, :])
     for m in range(slots):
-        page = table_s[SINGLES, m]
+        page = table[m, SINGLES]
         k_prompt[m * 128 : (m + 1) * 128, :] = k_pool[pl.ds(pl.multiple_of(page * 128, 128), 128), :]
     s_cache = dot_nt(q_prompt, k_prompt[...]) * root
     s_new = dot_nt(q_prompt, k_new[SINGLES:, :]) * root
@@ -306,7 +312,7 @@
         weights[rows, :] = p.astype(jnp.bfloat16)
 
     position = lax.broadcasted_iota(jnp.int32, s_cache.shape, 1)
-    s_cache = jnp.where(position < counts_s[SINGLES], s_cache, NEG)
+    s_cache = jnp.where(position < counts[SINGLES], s_cache, NEG)
     row = lax.broadcasted_iota(jnp.int32, (PROMPT, PROMPT), 0)
     col = lax.broadcasted_iota(jnp.int32, (PROMPT, PROMPT), 1)
     causal = jnp.concatenate([jnp.where(row >= col, 0.0, NEG)] * group, axis=0)
@@ -320,7 +326,7 @@
 
     copies[1].wait()
     for m in range(slots):
-        page = table_s[SINGLES, m]
+        page = table[m, SINGLES]
         v_prompt[m * 128 : (m + 1) * 128, :] = v_pool[pl.ds(pl.multiple_of(page * 128, 128), 128), :]
     out_prompt = dot_nn(p_cache.astype(jnp.bfloat16), v_prompt[...])
     out_prompt = out_prompt + dot_nn(p_new.astype(jnp.bfloat16), v_new[SINGLES:, :])
@@ -353,7 +359,7 @@
     return pl.pallas_call(
         attend_kernel,
         out_shape=(half, half),
-        in_specs=[smem, smem, vmem, vmem, smem, vmem, vmem, vmem, hbm, hbm, hbm],
+        in_specs=[smem, smem, smem, vmem, vmem, vmem, hbm, hbm, hbm],
         out_specs=(vmem, vmem),
         scratch_shapes=[
             pltpu.VMEM((pool_rows, HD), jnp.bfloat16),
@@ -362,22 +368,27 @@
             pltpu.VMEM((singles, pool_rows), jnp.float32),
             pltpu.VMEM((SINGLES, pool_rows), jnp.float32),
             pltpu.VMEM((singles, pool_rows), jnp.bfloat16),
-            pltpu.VMEM((table.shape[1] * 128, HD), jnp.bfloat16),
-            pltpu.VMEM((table.shape[1] * 128, HD), jnp.bfloat16),
+            pltpu.VMEM((table.shape[0] * 128, HD), jnp.bfloat16),
+            pltpu.VMEM((table.shape[0] * 128, HD), jnp.bfloat16),
             pltpu.VMEM((rows, q.shape[1]), jnp.bfloat16),
             pltpu.VMEM((rows, q.shape[1]), jnp.bfloat16),
             pltpu.SemaphoreType.DMA((3,)),
         ],
-        compiler_params=pltpu.CompilerParams(vmem_limit_bytes=32 * MIB),
+        compiler_params=pltpu.CompilerParams(vmem_limit_bytes=60 * MIB),
         cost_estimate=pl.CostEstimate(flops=10**9, bytes_accessed=8 * 10**6, transcendentals=6 * 10**5),
         name="attention",
-    )(place, table, table, counts[:, None], counts, q, k_new, v_new, k_pool, v_pool, w_out)
-
-
-def routes_kernel(hot, shares, pick, spread, scale):
-    rows, tokens = pick.shape
-    tile = scale.shape[0] // 5
-    share = shares[...]
+    )(place, table, counts, q, k_new, v_new, k_pool, v_pool, w_out)
+
+
+def routes_kernel(place, hot, n0, n1, n2, n3, pick_a, pick_b, spread_a, spread_b, scale):
+    rows, tokens = pick_a.shape
+    tile = rows // 5
+    notes = jnp.concatenate([n0[...], n1[...], n2[...], n3[...]], axis=0)
+    width = notes.shape[1]
+    source = lax.broadcasted_iota(jnp.int32, (width, width), 0)
+    target = lax.broadcasted_iota(jnp.int32, (width, width), 1)
+    wanted = (source < 24) & (target < 4) & (lax.rem(source, 8) == place[0] * 4 + target)
+    share = dot_nn(notes, jnp.where(wanted, 1.0, 0.0).astype(jnp.bfloat16))
     kept = jnp.where(share > 0.0, 1.0, 0.0)
     below = lax.broadcasted_iota(jnp.int32, (tokens, tokens), 1) < lax.broadcasted_iota(
         jnp.int32, (tokens, tokens), 0
@@ -386,161 +397,170 @@
     lane = lax.broadcasted_iota(jnp.int32, share.shape, 1)
     favored = hot[0]
     base = lane * tile + jnp.where((favored >= 0) & (lane > favored), tile, 0)
-    place = jnp.where(kept > 0.0, rank + base.astype(jnp.float32), -1.0)
-    place_t = place.T
+    spot = jnp.where(kept > 0.0, rank + base.astype(jnp.float32), -1.0)
+    spot_t = spot.T
     row_id = lax.broadcasted_iota(jnp.int32, (rows, tokens), 0).astype(jnp.float32)
     col_id = lax.broadcasted_iota(jnp.int32, (tokens, rows), 1).astype(jnp.float32)
     picked = jnp.zeros((rows, tokens), jnp.float32)
     spreading = jnp.zeros((tokens, rows), jnp.float32)
     for e in range(4):
-        picked = picked + jnp.where(row_id == place_t[e : e + 1, :], 1.0, 0.0)
-        spreading = spreading + jnp.where(col_id == place[:, e : e + 1], 1.0, 0.0)
+        picked = picked + jnp.where(row_id == spot_t[e : e + 1, :], 1.0, 0.0)
+        spreading = spreading + jnp.where(col_id == spot[:, e : e + 1], 1.0, 0.0)
     picked = picked.astype(jnp.bfloat16)
-    pick[...] = picked
-    spread[...] = spreading.astype(jnp.bfloat16)
-    found = jnp.zeros((rows, share.shape[1]), jnp.float32)
-    rest = share
-    for _ in range(3):
-        part = rest.astype(jnp.bfloat16)
-        found = found + dot_nn(picked, part)
-        rest = rest - part.astype(jnp.float32)
+    spreading = spreading.astype(jnp.bfloat16)
+    pick_a[...] = picked
+    spread_a[...] = spreading
+    for i in range(0, tokens // 64, 4):
+        for j, k in enumerate((0, 2, 1, 3)):
+            old, new = slice((i + k) * 64, (i + k + 1) * 64), slice((i + j) * 64, (i + j + 1) * 64)
+            pick_b[:, new] = picked[:, old]
+            spread_b[new, :] = spreading[old, :]
+    found = dot_nn(picked, notes)
     row = lax.broadcasted_iota(jnp.int32, found.shape, 0)
     column = lax.broadcasted_iota(jnp.int32, found.shape, 1)
-    first = column * tile + jnp.where((favored >= 0) & (column > favored), tile, 0)
-    size = jnp.where(column == favored, 2 * tile, tile)
-    mine = (row >= first) & (row < first + size) & (column < 4)
-    total = jnp.sum(jnp.where(mine, found, 0.0), axis=1, keepdims=True)
+    mine = lax.rem(column, 8) - place[0] * 4
+    first = mine * tile + jnp.where((favored >= 0) & (mine > favored), tile, 0)
+    size = jnp.where(mine == favored, 2 * tile, tile)
+    inside = (row >= first) & (row < first + size) & (mine >= 0) & (mine < 4) & (column < 24)
+    total = jnp.sum(jnp.where(inside, found, 0.0), axis=1, keepdims=True)
     scale[...] = jnp.broadcast_to(total, scale.shape)
 
 
-def routes_call(hot, shares, tile):
-    tokens = shares.shape[0]
+def routes_call(place, hot, pieces, tile):
+    tokens = sum(piece.shape[0] for piece in pieces)
+    rows = 5 * tile
     vmem, smem = (pl.BlockSpec(memory_space=s) for s in (pltpu.VMEM, pltpu.SMEM))
+    column = pieces[0].shape[1] // 128 - 1
+    note = pl.BlockSpec((pieces[0].shape[0], 128), lambda i: (0, column))
+    pick = jax.ShapeDtypeStruct((rows, tokens), jnp.bfloat16)
+    spread = jax.ShapeDtypeStruct((tokens, rows), jnp.bfloat16)
     return pl.pallas_call(
         routes_kernel,
-        out_shape=(
-            jax.ShapeDtypeStruct((5 * tile, tokens), jnp.bfloat16),
-            jax.ShapeDtypeStruct((tokens, 5 * tile), jnp.bfloat16),
-            jax.ShapeDtypeStruct((5 * tile, 128), jnp.float32),
-        ),
-        in_specs=[smem, vmem],
-        out_specs=(vmem, vmem, vmem),
-        compiler_params=pltpu.CompilerParams(vmem_limit_bytes=32 * MIB),
-        cost_estimate=pl.CostEstimate(flops=10**8, bytes_accessed=10**6, transcendentals=0),
+        grid=(1,),
+        out_shape=(pick, pick, spread, spread, jax.ShapeDtypeStruct((rows, 128), jnp.float32)),
+        in_specs=[smem, smem] + [note] * 4,
+        out_specs=(vmem,) * 5,
+        compiler_params=pltpu.CompilerParams(vmem_limit_bytes=20 * MIB),
+        cost_estimate=pl.CostEstimate(flops=10**8, bytes_accessed=2 * 10**6, transcendentals=0),
         name="routes",
-    )(hot, shares)
-
-
-def experts_kernel(
-    hot, a0, a1, a2, a3, b0, b1, b2, b3, pick, spread, scale, gate, up, down,
-    a_send, a_keep, b_send, b_keep,
-    tokens, taken, total, made, sems,
-):
-    expert, chunk = pl.program_id(0), pl.program_id(1)
-    last = pl.num_programs(1) - 1
-    tile = made.shape[0] // 5
-    half = tokens.shape[1] // 2
+    )(place, hot, *pieces)
+
+
+def span_of(expert, favored, tile, rows):
+    first = expert * tile + jnp.where((favored >= 0) & (expert > favored), tile, 0)
+    return pl.ds(pl.multiple_of(first, 32), rows)
+
+
+def by_size(expert, favored, tile, run):
+    @pl.when(expert == favored)
+    def _():
+        run(span_of(expert, favored, tile, 2 * tile))
+
+    @pl.when(expert != favored)
+    def _():
+        run(span_of(expert, favored, tile, tile))
+
+
+def inner_kernel(done, hot, x0, x1, x2, x3, pick, gate, up, *refs):
+    expert = pl.program_id(0)
+    tile = pick.shape[0] // 5
     favored = hot[0]
-
-    @pl.when((expert == 0) & (chunk == 0))
+    if done:
+        g_in, u_in, act, taken = refs
+    else:
+        g_out, u_out, taken = refs
+
+    @pl.when(expert == 0)
     def _():
-        copies = []
-        for i, ref in enumerate((a0, a1, a2, a3)):
-            copies.append((ref, tokens.at[i * 128 : (i + 1) * 128, 0:half]))
-        for i, ref in enumerate((b0, b1, b2, b3)):
-            for j in range(2):
-                first = (i // 2) * 256 + j * 128 + (i % 2) * 64
-                copies.append(
-                    (ref.at[j * 64 : (j + 1) * 64, :], tokens.at[first : first + 64, half:])
-                )
-        started = []
-        for i, (src, dst) in enumerate(copies):
-            copy = pltpu.make_async_copy(src, dst, sems.at[i])
-            copy.start()
-            started.append(copy)
-        made[4 * tile :, :] = jnp.zeros_like(made[4 * tile :, :])
-        for copy in started:
-            copy.wait()
-
-        @pl.loop(0, tokens.shape[1], step=512)
-        def _(start):
-            cols = pl.ds(pl.multiple_of(start, 512), 512)
-            taken[:, cols] = dot_nn(pick[...], tokens[:, cols]).astype(jnp.bfloat16)
-
-    first = expert * tile + jnp.where((favored >= 0) & (expert > favored), tile, 0)
-
-    def run(rows):
-        span = pl.ds(pl.multiple_of(first, 32), rows)
+        for start in range(0, taken.shape[1], 512):
+            total = jnp.zeros((pick.shape[0], 512), jnp.float32)
+            for i, piece in enumerate((x0, x1, x2, x3)):
+                rows = piece.shape[0]
+                total = total + dot_nn(pick[:, i * rows : (i + 1) * rows], piece[:, start : start + 512])
+            taken[:, start : start + 512] = total.astype(jnp.bfloat16)
+        if done:
+            act[4 * tile :, :] = jnp.zeros_like(act[4 * tile :, :])
+
+    def run(span):
         x = taken[span, :]
         g = dot_nt(x, gate[0])
         u = dot_nt(x, up[0])
-        act = (g / (1.0 + jnp.exp(-g)) * u).astype(jnp.bfloat16)
-        part = scale[span, 0:1]
-
-        @pl.when(chunk == 0)
-        def _():
-            total[0:rows, :] = dot_nn(act, down[0])
-
-        @pl.when(chunk > 0)
-        def _():
-            total[0:rows, :] += dot_nn(act, down[0])
-
-        @pl.when(chunk == last)
-        def _():
-            made[span, :] = (total[0:rows, :] * part).astype(jnp.bfloat16)
-
-    @pl.when(expert == favored)
+        if done:
+            g = g + g_in[span, :]
+            u = u + u_in[span, :]
+            act[span, :] = (g / (1.0 + jnp.exp(-g)) * u).astype(jnp.bfloat16)
+        else:
+            g_out[span, :] = g
+            u_out[span, :] = u
+
+    by_size(expert, favored, tile, run)
+
+
+def inner_call(half, hot, pieces, pick, gate, up, before):
+    experts, hidden, width = gate.shape
+    rows = pick.shape[0]
+    wide = width // 2
+    vmem, smem = (pl.BlockSpec(memory_space=s) for s in (pltpu.VMEM, pltpu.SMEM))
+    weight = pl.BlockSpec((1, hidden, wide), lambda e: (e, 0, half))
+    part = jax.ShapeDtypeStruct((rows, hidden), jnp.float32)
+    out = jax.ShapeDtypeStruct((rows, hidden), jnp.bfloat16)
+    return pl.pallas_call(
+        functools.partial(inner_kernel, bool(before)),
+        grid=(experts,),
+        out_shape=out if before else (part, part),
+        in_specs=[smem] + [vmem] * 5 + [weight] * 2 + [vmem] * len(before),
+        out_specs=vmem if before else (vmem, vmem),
+        scratch_shapes=[pltpu.VMEM((rows, wide), jnp.bfloat16)],
+        compiler_params=pltpu.CompilerParams(vmem_limit_bytes=24 * MIB),
+        cost_estimate=pl.CostEstimate(
+            flops=4 * rows * hidden * wide, bytes_accessed=experts * 4 * hidden * wide, transcendentals=rows * hidden
+        ),
+        name="inner_second" if before else "inner_first",
+    )(hot, *pieces, pick, gate, up, *before)
+
+
+def outer_kernel(hot, act, spread, scale, down, keep, send, made):
+    expert = pl.program_id(0)
+    tile = made.shape[0] // 5
+    favored = hot[0]
+
+    @pl.when(expert == 0)
     def _():
-        run(2 * tile)
-
-    @pl.when(expert != favored)
+        made[4 * tile :, :] = jnp.zeros_like(made[4 * tile :, :])
+
+    def run(span):
+        made[span, :] = (dot_nn(act[span, :], down[0]) * scale[span, 0:1]).astype(jnp.bfloat16)
+
+    by_size(expert, favored, tile, run)
+
+    @pl.when(expert == pl.num_programs(0) - 1)
     def _():
-        run(tile)
-
-    @pl.when((expert == pl.num_programs(0) - 1) & (chunk == last))
-    def _():
-        rows = tokens.shape[0] // 2
-        for i, (out_keep, out_send) in enumerate(((a_keep, a_send), (b_keep, b_send))):
-
-            @pl.loop(0, half, step=512)
-            def _(start, i=i, out_keep=out_keep, out_send=out_send):
-                cols = pl.ds(pl.multiple_of(start, 512), 512)
-                source = pl.ds(pl.multiple_of(i * half + start, 512), 512)
-                y = dot_nn(spread[...], made[:, source]).astype(jnp.bfloat16)
-                for side, out in enumerate((out_keep, out_send)):
-                    for j in range(4):
-                        to = j if i == 0 else (j % 2) * 2 + j // 2
-                        out[to * 64 : (to + 1) * 64, cols] = y[side * rows + j * 64 : side * rows + (j + 1) * 64, :]
-
-
-def experts_call(hot, pieces, pick, spread, scale, gate, up, down):
-    experts, hidden, width = gate.shape
-    tokens = spread.shape[0]
-    rows = pick.shape[0]
-    tile = rows // 5
-    chunk = hidden // 2
-    vmem, smem, hbm = (pl.BlockSpec(memory_space=s) for s in (pltpu.VMEM, pltpu.SMEM, pl.ANY))
-    weight = pl.BlockSpec((1, chunk, width), lambda e, c: (e, c, 0))
-    out = jax.ShapeDtypeStruct((tokens // 2, width // 2), jnp.bfloat16)
+        rows = keep.shape[0]
+        for start in range(0, made.shape[1], 512):
+            y = dot_nn(spread[...], made[:, start : start + 512]).astype(jnp.bfloat16)
+            keep[:, start : start + 512] = y[0:rows, :]
+            send[:, start : start + 512] = y[rows:, :]
+
+
+def outer_call(half, hot, act, spread, scale, down):
+    experts, hidden, width = down.shape
+    rows, wide = act.shape[0], width // 2
+    vmem, smem = (pl.BlockSpec(memory_space=s) for s in (pltpu.VMEM, pltpu.SMEM))
+    weight = pl.BlockSpec((1, hidden, wide), lambda e: (e, 0, half))
+    out = jax.ShapeDtypeStruct((spread.shape[0] // 2, wide), jnp.bfloat16)
     return pl.pallas_call(
-        experts_kernel,
-        grid=(experts, 2),
-        out_shape=(out, out, out, out),
-        in_specs=[smem] + [hbm] * 8 + [vmem] * 3 + [weight] * 3,
-        out_specs=(vmem,) * 4,
-        scratch_shapes=[
-            pltpu.VMEM((tokens, width), jnp.bfloat16),
-            pltpu.VMEM((rows, width), jnp.bfloat16),
-            pltpu.VMEM((2 * tile, width), jnp.float32),
-            pltpu.VMEM((rows, width), jnp.bfloat16),
-            pltpu.SemaphoreType.DMA((12,)),
-        ],
-        compiler_params=pltpu.CompilerParams(vmem_limit_bytes=50 * MIB),
+        outer_kernel,
+        grid=(experts,),
+        out_shape=(out, out),
+        in_specs=[smem] + [vmem] * 3 + [weight],
+        out_specs=(vmem, vmem),
+        scratch_shapes=[pltpu.VMEM((rows, wide), jnp.bfloat16)],
+        compiler_params=pltpu.CompilerParams(vmem_limit_bytes=20 * MIB),
         cost_estimate=pl.CostEstimate(
-            flops=6 * rows * hidden * width, bytes_accessed=experts * 6 * hidden * width, transcendentals=rows * hidden
+            flops=4 * rows * hidden * wide, bytes_accessed=experts * 2 * hidden * wide, transcendentals=0
         ),
-        name="experts",
-    )(hot, *pieces, pick, spread, scale, gate, up, down)
+        name="outer",
+    )(hot, act, spread, scale, down)
 
 
 def kept_shares(chosen_specialists, selection_shares, allowed_placements, favored_specialist):
@@ -555,6 +575,16 @@
     limit = jnp.where(index == favored_specialist[0], PLACEMENT_MOST, allowed_placements)
     share = jnp.sum(jnp.where(picked, selection_shares[:, :, None], 0.0), axis=1)
     return jnp.where(before < limit[None, :].astype(jnp.float32), share, 0.0)
+
+
+def notes_of(shares):
+    parts = []
+    for _ in range(3):
+        part = lax.reduce_precision(shares, 8, 7)
+        parts.append(part.astype(jnp.bfloat16))
+        shares = shares - part
+    notes = jnp.concatenate(parts, axis=1)
+    return jnp.pad(notes, ((0, 0), (0, 128 - notes.shape[1])))
 
 
 def joined(*parts):
@@ -588,22 +618,17 @@
     half = width // 2
     own_experts = gating_matrices.shape[0]
     count = chosen_specialists.shape[0]
-    z, x, t = (lax.axis_index(name) for name in ("dp", "expert", "tensor"))
-
-    shares = kept_shares(chosen_specialists, selection_shares, allowed_placements, favored_specialist)
-    shares = lax.all_gather(shares, ("dp", "expert", "tensor"), axis=0, tiled=True)
-    away = jnp.arange(32, dtype=jnp.int32)
-    block = ((z ^ (away % 4)) * 2 + (x ^ (away // 4 % 2))) * 4 + (t ^ (away // 8 % 2 * 2 + away // 16))
-    shares = lax.dynamic_slice_in_dim(shares, x * own_experts, own_experts, 1)
-    shares = shares.reshape(32, count, own_experts)[block].reshape(32 * count, own_experts)
-    shares = jnp.pad(shares, ((0, 0), (0, 128 - own_experts)))
+    x, t = lax.axis_index("expert"), lax.axis_index("tensor")
+
+    notes = notes_of(
+        kept_shares(chosen_specialists, selection_shares, allowed_placements, favored_specialist)
+    )
     hot = favored_specialist - x * own_experts
     hot = jnp.where((hot >= 0) & (hot < own_experts), hot, -1).astype(jnp.int32)
-    pick, spread, scale = routes_call(hot, shares, CAP_MOST * 32)
 
     send, keep = attention_call(
         t.astype(jnp.int32)[None],
-        sequence_sheet_map,
+        sequence_sheet_map.T,
         stored_position_counts,
         question_vectors,
         fresh_lookup_vectors,
@@ -623,16 +648,22 @@
         jnp.bfloat16
     )
 
-    pieces = []
-    for i, (first, second) in enumerate(((over_x, over_y), (over_y, over_x))):
-        part = normed[:, i * half : (i + 1) * half]
+    gathered = []
+    for part, first, second in (
+        (jnp.concatenate([normed[:, :half], notes], axis=1), over_x, over_y),
+        (normed[:, half:], over_y, over_x),
+    ):
         part = joined(part, over_z(part, 1), over_z(part, 2), over_z(part, 3))
         part = joined(part, first(part))
         other = second(part)
-        pieces += [part, other, over_core(part), over_core(other)]
-    a_send, a_keep, b_send, b_keep = experts_call(
-        hot, pieces, pick, spread, scale, gating_matrices, expand_matrices, contract_matrices
-    )
+        gathered.append((part, other, over_core(part), over_core(other)))
+    pick_a, pick_b, spread_a, spread_b, scale = routes_call(
+        x.astype(jnp.int32)[None], hot, gathered[0], CAP_MOST * 32
+    )
+    before = inner_call(0, hot, gathered[0], pick_a, gating_matrices, expand_matrices, ())
+    act = inner_call(1, hot, gathered[1], pick_b, gating_matrices, expand_matrices, before)
+    a_keep, a_send = outer_call(0, hot, act, spread_a, scale, contract_matrices)
+    b_keep, b_send = outer_call(1, hot, act, spread_b, scale, contract_matrices)
     results = []
     for sent, kept, first, second in (
         (a_send, a_keep, over_y, over_x),

time: 178 us -> 136 us (0.76)
  blocking collectives: 39.8 us -> 0 us
  starting transfers between devices: 28.1 us -> 35.7 us
  waiting for transfers between devices: 49.6 us -> 42.4 us
  Pallas kernels: 37.2 us -> 35.3 us
    all_gather x1 -> x0, blocking collectives: 39.8 us -> none  [local_fast(): lax.all_gather(shares, ('dp', 'expert', 'tensor'), axis=0, tiled=True)]
    ppermute x12, starting transfers between devices: 14.7 us -> 19.6 us  [over_z(): return lax.ppermute(a, 'dp', [(i, i ^ k) for i in range(4)])]
    pallas_call x2 -> x5, Pallas kernels: 33 us -> 29.7 us  [the longest x2 19.7 us: inner_call(): pl.pallas_call(functools.partial(inner_kernel, bool(before)), grid=(exper...]
    unnamed x24 -> x18, local copies, waits for them, and re-layouts: 9.46 us -> 12.3 us
    ppermute x12, waiting for transfers between devices: 11.9 us -> 9.26 us  [over_z(): return lax.ppermute(a, 'dp', [(i, i ^ k) for i in range(4)])]
    ppermute x7, waiting for transfers between devices: 3.54 us -> 0.95 us  [over_core(): return lax.ppermute(a, 'tensor', PAIRS_CORE)]
    ppermute x5, waiting for transfers between devices: 22.5 us -> 20.3 us  [over_y(): return lax.ppermute(a, 'tensor', PAIRS_Y)]
    ppermute x4, starting transfers between devices: 3.25 us -> 5.49 us  [over_x(): return lax.ppermute(a, 'expert', PAIRS_X)]
  transfers between devices with their start and end apart: 28 -> 28, of which waited for: 14 -> 14; matrix products, arithmetic and copies ran while one was open for 5% -> 5% of each run, Pallas kernels for 1% -> 12%
where the time goes in v2:
time: 136 us; the launch traced here: 135 us
  waiting for transfers between devices  42.4 us (31%)
  starting transfers between devices  35.7 us (26%)
  Pallas kernels  35.3 us (26%)
  local copies, waits for them, and re-layouts  13.8 us (10%)
  other arithmetic  6.93 us (5%)
    ppermute x5, waiting for transfers between devices, over_y(): return lax.ppermute(a, 'tensor', PAIRS_Y)  20.3 us
    pallas_call x2, Pallas kernels, inner_call(): pl.pallas_call(functools.partial(inner_kernel, bool(before)), grid=(exper...  19.7 us
    ppermute x12, starting transfers between devices, over_z(): return lax.ppermute(a, 'dp', [(i, i ^ k) for i in range(4)])  19.6 us
    unnamed x18, local copies, waits for them, and re-layouts  12.3 us
    ppermute x4, waiting for transfers between devices, over_x(): return lax.ppermute(a, 'expert', PAIRS_X)  11.9 us
    ppermute x12, waiting for transfers between devices, over_z(): return lax.ppermute(a, 'dp', [(i, i ^ k) for i in range(4)])  9.26 us
    ppermute x5, starting transfers between devices, over_y(): return lax.ppermute(a, 'tensor', PAIRS_Y)  8.93 us
    pallas_call x2, Pallas kernels, outer_call(): pl.pallas_call(outer_kernel, grid=(experts,), out_shape=(out, out), in_sp...  7.63 us
  transfers between devices with their start and end apart: 28, of which 14 were waited for; matrix products, arithmetic and copies ran while one was open for 5% of the time, Pallas kernels for 12%

profile of v2, /device:TPU:0, one launch (start us, length us, event | category | flops | bytes accessed | tf_op | source)
XLA Modules:
  0.0 135.1 jit_solution(11325416925832031002)
XLA Ops:
  0.0 5.6 %attention.1 = (bf16[32,4096]{1,0:T(8,128)(2,1)}, bf16[32,4096]{1,0:T(8,128)(2,1)}) custom-call(s32[1]{0:T(128)} %bitcast.place, s32[8,17]{1,0:T(8,128)} %bitcast.13, s32[17]{0:T(128)} %counts.1, bf16[64,512]{1,0:T(8,128)(2,1)} %q.1, bf16[64,128]{1,0:T(8,128)(2,1)} %k_new.1, bf16[64,128]{1,0:T(8,128)(2,1)} %v_new.1, bf16[5120,128]{1,0:T(8,128)(2,1)} %bitcast.11, ...), custom_call_target="tpu_custom_call" | custom-call | flops 1000000000 | bytes 8000000 | tf_op jit(solution)/shard_map/attention/pallas_call | solution.py:359
  5.6 0.5 collective-permute-start
  6.1 0.7 select_reduce_fusion
  6.8 0.7 fusion.14
  8.2 0.7 fusion.17
  8.9 0.9 add_convert_fusion.10
  9.8 2.6 %collective-permute-start.1 = (bf16[16,4096]{1,0:T(8,128)(2,1)S(1)}, bf16[16,4096]{1,0:T(8,128)(2,1)S(1)}, u32[]{:S(2)}, u32[]{:S(2)}) collective-permute-start(bf16[16,4096]{1,0:T(8,128)(2,1)S(1)} %add_convert_fusion.10), channel_id=1, source_target_pairs={{0,2},{2,0},{1,3},{3,1},{4,6},{6,4},{5,7},{7,5},{8,10},{10,8},{9,1... | collective-permute-start | bytes 393224 | tf_op jit(solution)/shard_map/ppermute | solution.py:235
  12.4 0.1 reduce-precision_convert_fusion.1
  12.6 0.7 convert_element_type.178
  13.3 0.1 fusion.16
  13.3 3.3 %collective-permute-done.1 = bf16[16,4096]{1,0:T(8,128)(2,1)S(1)} collective-permute-done((bf16[16,4096]{1,0:T(8,128)(2,1)S(1)}, bf16[16,4096]{1,0:T(8,128)(2,1)S(1)}, u32[]{:S(2)}, u32[]{:S(2)}) %collective-permute-start.1) | collective-permute-done | bytes 131104 | tf_op jit(solution)/shard_map/ppermute | solution.py:235
  16.6 1.2 fusion.1
  17.8 0.1 fusion.3
  17.9 0.6 fusion.22
  18.5 1.8 %collective-permute-start.2 = (bf16[16,2048]{1,0:T(8,128)(2,1)S(1)}, bf16[16,2048]{1,0:T(8,128)(2,1)S(1)}, u32[]{:S(2)}, u32[]{:S(2)}) collective-permute-start(bf16[16,2048]{1,0:T(8,128)(2,1)S(1)} %get-tuple-element.49), channel_id=1, source_target_pairs={{0,8},{8,0},{16,24},{24,16},{1,9},{9,1},{17,25},{25,17},{2,10},{10... | collective-permute-start | bytes 196616 | tf_op jit(solution)/shard_map/ppermute | solution.py:243
  20.3 2.6 %collective-permute-start.3 = (bf16[16,2048]{1,0:T(8,128)(2,1)S(1)}, bf16[16,2048]{1,0:T(8,128)(2,1)S(1)}, u32[]{:S(2)}, u32[]{:S(2)}) collective-permute-start(bf16[16,2048]{1,0:T(8,128)(2,1)S(1)} %get-tuple-element.49), channel_id=1, source_target_pairs={{0,16},{8,24},{16,0},{24,8},{1,17},{9,25},{17,1},{25,9},{2,18},{10... | collective-permute-start | bytes 196616 | tf_op jit(solution)/shard_map/ppermute | solution.py:243
  22.9 1.0 collective-permute-start.9
  23.9 3.5 %collective-permute-start.10 = (bf16[16,2176]{1,0:T(8,128)(2,1)S(1)}, bf16[16,2176]{1,0:T(8,128)(2,1)S(1)}, u32[]{:S(2)}, u32[]{:S(2)}) collective-permute-start(bf16[16,2176]{1,0:T(8,128)(2,1)S(1)} %get-tuple-element.50), channel_id=1, source_target_pairs={{0,16},{8,24},{16,0},{24,8},{1,17},{9,25},{17,1},{25,9},{2,18},{10... | collective-permute-start | bytes 208904 | tf_op jit(solution)/shard_map/ppermute | solution.py:243
  27.4 0.4 collective-permute-done.3
  27.7 1.7 %collective-permute-done.4 = bf16[16,2048]{1,0:T(8,128)(2,1)S(1)} collective-permute-done((bf16[16,2048]{1,0:T(8,128)(2,1)S(1)}, bf16[16,2048]{1,0:T(8,128)(2,1)S(1)}, u32[]{:S(2)}, u32[]{:S(2)}) %collective-permute-start.4) | collective-permute-done | bytes 65568 | tf_op jit(solution)/shard_map/ppermute | solution.py:243
  29.5 1.6 %collective-permute-start.5 = (bf16[64,2048]{1,0:T(8,128)(2,1)S(1)}, bf16[64,2048]{1,0:T(8,128)(2,1)S(1)}, u32[]{:S(2)}, u32[]{:S(2)}) collective-permute-start(bf16[64,2048]{1,0:T(8,128)(2,1)S(1)} %pad_maximum_fusion.1), channel_id=1, source_target_pairs={{0,2},{2,0},{1,3},{3,1},{4,6},{6,4},{5,7},{7,5},{8,10},{10,8},{9,1... | collective-permute-start | bytes 786440 | tf_op jit(solution)/shard_map/ppermute | solution.py:235
  31.1 0.6 constant_dynamic-update-slice_fusion.3
  31.7 0.6 constant_dynamic-update-slice_fusion.2
  32.3 1.8 %collective-permute-done.10 = bf16[16,2176]{1,0:T(8,128)(2,1)S(1)} collective-permute-done((bf16[16,2176]{1,0:T(8,128)(2,1)S(1)}, bf16[16,2176]{1,0:T(8,128)(2,1)S(1)}, u32[]{:S(2)}, u32[]{:S(2)}) %collective-permute-start.10) | collective-permute-done | bytes 69664 | tf_op jit(solution)/shard_map/ppermute | solution.py:243
  34.2 1.5 %collective-permute-start.12 = (bf16[64,2176]{1,0:T(8,128)(2,1)S(1)}, bf16[64,2176]{1,0:T(8,128)(2,1)S(1)}, u32[]{:S(2)}, u32[]{:S(2)}) collective-permute-start(bf16[64,2176]{1,0:T(8,128)(2,1)S(1)} %pad_maximum_fusion), channel_id=1, source_target_pairs={{0,4},{4,0},{1,5},{5,1},{2,6},{6,2},{3,7},{7,3},{8,12},{12,8},{9,1... | collective-permute-start | bytes 835592 | tf_op jit(solution)/shard_map/ppermute | solution.py:239
  35.7 5.1 %collective-permute-done.12 = bf16[64,2176]{1,0:T(8,128)(2,1)S(1)} collective-permute-done((bf16[64,2176]{1,0:T(8,128)(2,1)S(1)}, bf16[64,2176]{1,0:T(8,128)(2,1)S(1)}, u32[]{:S(2)}, u32[]{:S(2)}) %collective-permute-start.12) | collective-permute-done | bytes 278560 | tf_op jit(solution)/shard_map/ppermute | solution.py:239
  40.8 1.5 %collective-permute-start.13 = (bf16[128,2176]{1,0:T(8,128)(2,1)S(1)}, bf16[128,2176]{1,0:T(8,128)(2,1)S(1)}, u32[]{:S(2)}, u32[]{:S(2)}) collective-permute-start(bf16[128,2176]{1,0:T(8,128)(2,1)S(1)} %constant_dynamic-update-slice_fusion.5.n0.x0), channel_id=1, source_target_pairs={{0,2},{2,0},{1,3},{3,1},{4,6},{6,4},{5,7},{7,5},{8,10},{10,8},{9,1... | collective-permute-start | bytes 1671176 | tf_op jit(solution)/shard_map/ppermute | solution.py:235
  42.3 0.6 constant_dynamic-update-slice_fusion.1
  43.0 0.7 constant_dynamic-update-slice_fusion.x0
  43.7 1.5 %collective-permute-start.6 = (bf16[128,2048]{1,0:T(8,128)(2,1)}, bf16[128,2048]{1,0:T(8,128)(2,1)}, u32[]{:S(2)}, u32[]{:S(2)}) collective-permute-start(bf16[128,2048]{1,0:T(8,128)(2,1)} %constant_dynamic-update-slice_fusion.x0), channel_id=1, source_target_pairs={{0,4},{4,0},{1,5},{5,1},{2,6},{6,2},{3,7},{7,3},{8,12},{12,8},{9,1... | collective-permute-start | bytes 1572872 | tf_op jit(solution)/shard_map/ppermute | solution.py:239
  45.2 6.5 %collective-permute-done.13.n1.x1 = bf16[128,2176]{1,0:T(8,128)(2,1)S(1)} collective-permute-done((bf16[128,2176]{1,0:T(8,128)(2,1)S(1)}, bf16[128,2176]{1,0:T(8,128)(2,1)S(1)}, u32[]{:S(2)}, u32[]{:S(2)}) %collective-permute-start.13) | collective-permute-done | bytes 557088 | tf_op jit(solution)/shard_map/ppermute | solution.py:235
  51.7 0.5 collective-permute-start.7
  52.2 1.7 %collective-permute-done.6.x1 = bf16[128,2048]{1,0:T(8,128)(2,1)} collective-permute-done((bf16[128,2048]{1,0:T(8,128)(2,1)}, bf16[128,2048]{1,0:T(8,128)(2,1)}, u32[]{:S(2)}, u32[]{:S(2)}) %collective-permute-start.6) | collective-permute-done | bytes 524320 | tf_op jit(solution)/shard_map/ppermute | solution.py:239
  53.9 0.6 collective-permute-done.15.n3.x3
  54.5 2.4 %routes.1 = (bf16[480,512]{1,0:T(8,128)(2,1)S(1)}, bf16[480,512]{1,0:T(8,128)(2,1)S(1)}, bf16[512,480]{1,0:T(8,128)(2,1)S(1)}, bf16[512,480]{1,0:T(8,128)(2,1)S(1)}, f32[480,128]{1,0:T(8,128)S(1)}) custom-call(s32[1]{0:T(128)} %bitcast.5.place, s32[1]{0:T(128)S(6)} %select_n.16.hot, bf16[128,2176]{1,0:T(8,128)(2,1)S(1)} %constant_dynamic-update-slice_fusion.5.n0.x0, ...), custom_call_target="tpu_custom_call" | custom-call | flops 100000000 | bytes 2000000 | tf_op jit(solution)/shard_map/routes/pallas_call | solution.py:437
  56.9 5.2 %copy-done = bf16[4,448,4096]{2,1,0:T(8,128)(2,1)S(1)} copy-done((bf16[4,448,4096]{2,1,0:T(8,128)(2,1)S(1)}, bf16[4,448,4096]{2,1,0:T(8,128)(2,1)}, u32[]{:S(2)}) %copy-start) | copy-done | bytes 14680088
  62.1 9.8 %inner_first.1 = (f32[480,448]{1,0:T(8,128)S(1)}, f32[480,448]{1,0:T(8,128)S(1)}) custom-call(s32[1]{0:T(128)S(6)} %select_n.16.hot, bf16[128,2176]{1,0:T(8,128)(2,1)S(1)} %constant_dynamic-update-slice_fusion.5.n0.x0, bf16[128,2176]{1,0:T(8,128)(2,1)S(1)} %collective-permute-done.13.n1.x1, bf16[128,2176]{1,0:T(8,128)(2,1)} %collective-permute-done.14.n2.x2, ...), custom_call_target="tpu_custom_call" | custom-call | flops 1761607680 | bytes 14680064 | tf_op jit(solution)/shard_map/inner_first/pallas_call | solution.py:507
  72.0 9.9 %inner_second.1.act = bf16[480,448]{1,0:T(8,128)(2,1)S(1)} custom-call(s32[1]{0:T(128)S(6)} %select_n.16.hot, bf16[128,2048]{1,0:T(8,128)(2,1)} %constant_dynamic-update-slice_fusion.x0, bf16[128,2048]{1,0:T(8,128)(2,1)} %collective-permute-done.6.x1, bf16[128,2048]{1,0:T(8,128)(2,1)} %collective-permute-done.7.x2, ...), custom_call_target="tpu_custom_call" | custom-call | flops 1761607680 | bytes 14680064 | tf_op jit(solution)/shard_map/inner_second/pallas_call | solution.py:507
  81.9 5.2 %copy-done.1 = bf16[4,448,4096]{2,1,0:T(8,128)(2,1)S(1)} copy-done((bf16[4,448,4096]{2,1,0:T(8,128)(2,1)S(1)}, bf16[4,448,4096]{2,1,0:T(8,128)(2,1)}, u32[]{:S(2)}) %copy-start.1) | copy-done | bytes 14680088
  87.1 3.8 %outer.2 = (bf16[256,2048]{1,0:T(8,128)(2,1)S(1)}, bf16[256,2048]{1,0:T(8,128)(2,1)S(1)}) custom-call(s32[1]{0:T(128)S(6)} %select_n.16.hot, bf16[480,448]{1,0:T(8,128)(2,1)S(1)} %inner_second.1.act, bf16[512,480]{1,0:T(8,128)(2,1)S(1)} %get-tuple-element.24.spread, f32[480,128]{1,0:T(8,128)S(1)} %get-tuple-element.25.scale, bf16[4,448,4096]{2,1,0:T(8,128)(2,1)S(1)} %copy-done.1), custom_call_target="tpu_custom_call" | custom-call | flops 1761607680 | bytes 7340032 | tf_op jit(solution)/shard_map/outer/pallas_call | solution.py:551
  90.9 0.2 collective-permute-start.16
  91.1 3.8 %outer.3 = (bf16[256,2048]{1,0:T(8,128)(2,1)S(1)}, bf16[256,2048]{1,0:T(8,128)(2,1)S(1)}) custom-call(s32[1]{0:T(128)S(6)} %select_n.16.hot, bf16[480,448]{1,0:T(8,128)(2,1)S(1)} %inner_second.1.act, bf16[512,480]{1,0:T(8,128)(2,1)S(1)} %get-tuple-element.28.spread, f32[480,128]{1,0:T(8,128)S(1)} %get-tuple-element.25.scale, bf16[4,448,4096]{2,1,0:T(8,128)(2,1)S(1)} %copy-done.1), custom_call_target="tpu_custom_call" | custom-call | flops 1761607680 | bytes 7340032 | tf_op jit(solution)/shard_map/outer/pallas_call | solution.py:551
  94.9 0.4 collective-permute-start.22
  95.4 0.4 add_convert_fusion.3
  95.8 1.6 %collective-permute-start.17 = (bf16[128,2048]{1,0:T(8,128)(2,1)S(1)}, bf16[128,2048]{1,0:T(8,128)(2,1)S(1)}, u32[]{:S(2)}, u32[]{:S(2)}) collective-permute-start(bf16[128,2048]{1,0:T(8,128)(2,1)S(1)} %get-tuple-element.37), channel_id=1, source_target_pairs={{0,2},{2,0},{1,3},{3,1},{4,6},{6,4},{5,7},{7,5},{8,10},{10,8},{9,1... | collective-permute-start | bytes 1572872 | tf_op jit(solution)/shard_map/ppermute | solution.py:235
  97.4 0.3 collective-permute-done.22
  97.7 0.4 add_convert_fusion.1
  98.0 1.2 collective-permute-start.23
  99.3 10.5 %collective-permute-done.17 = bf16[128,2048]{1,0:T(8,128)(2,1)S(1)} collective-permute-done((bf16[128,2048]{1,0:T(8,128)(2,1)S(1)}, bf16[128,2048]{1,0:T(8,128)(2,1)S(1)}, u32[]{:S(2)}, u32[]{:S(2)}) %collective-permute-start.17) | collective-permute-done | bytes 524320 | tf_op jit(solution)/shard_map/ppermute | solution.py:235
  109.9 1.2 collective-permute-start.18
  111.1 1.6 %collective-permute-done.23 = bf16[128,2048]{1,0:T(8,128)(2,1)S(1)} collective-permute-done((bf16[128,2048]{1,0:T(8,128)(2,1)S(1)}, bf16[128,2048]{1,0:T(8,128)(2,1)S(1)}, u32[]{:S(2)}, u32[]{:S(2)}) %collective-permute-start.23) | collective-permute-done | bytes 524320 | tf_op jit(solution)/shard_map/ppermute | solution.py:239
  112.8 1.6 %collective-permute-start.24 = (bf16[64,2048]{1,0:T(8,128)(2,1)S(1)}, bf16[64,2048]{1,0:T(8,128)(2,1)S(1)}, u32[]{:S(2)}, u32[]{:S(2)}) collective-permute-start(bf16[64,2048]{1,0:T(8,128)(2,1)S(1)} %add_convert_fusion.4), channel_id=1, source_target_pairs={{0,2},{2,0},{1,3},{3,1},{4,6},{6,4},{5,7},{7,5},{8,10},{10,8},{9,1... | collective-permute-start | bytes 786440 | tf_op jit(solution)/shard_map/ppermute | solution.py:235
  114.4 3.5 %collective-permute-done.18 = bf16[64,2048]{1,0:T(8,128)(2,1)S(1)} collective-permute-done((bf16[64,2048]{1,0:T(8,128)(2,1)S(1)}, bf16[64,2048]{1,0:T(8,128)(2,1)S(1)}, u32[]{:S(2)}, u32[]{:S(2)}) %collective-permute-start.18) | collective-permute-done | bytes 262176 | tf_op jit(solution)/shard_map/ppermute | solution.py:239
  117.9 0.1 fusion.18
  118.1 3.9 %collective-permute-start.19 = (bf16[16,2048]{1,0:T(8,128)(2,1)S(1)}, bf16[16,2048]{1,0:T(8,128)(2,1)S(1)}, u32[]{:S(2)}, u32[]{:S(2)}) collective-permute-start(bf16[16,2048]{1,0:T(8,128)(2,1)S(1)} %get-tuple-element.41), channel_id=1, source_target_pairs={{0,8},{8,0},{16,24},{24,16},{1,9},{9,1},{17,25},{25,17},{2,10},{10... | collective-permute-start | bytes 196616 | tf_op jit(solution)/shard_map/ppermute | solution.py:243
  122.0 0.4 collective-permute-start.20
  122.4 2.0 %collective-permute-start.21 = (bf16[16,2048]{1,0:T(8,128)(2,1)S(1)}, bf16[16,2048]{1,0:T(8,128)(2,1)S(1)}, u32[]{:S(2)}, u32[]{:S(2)}) collective-permute-start(bf16[16,2048]{1,0:T(8,128)(2,1)S(1)} %get-tuple-element.42), channel_id=1, source_target_pairs={{0,24},{8,16},{16,8},{24,0},{1,25},{9,17},{17,9},{25,1},{2,26},{10... | collective-permute-start | bytes 196616 | tf_op jit(solution)/shard_map/ppermute | solution.py:243
  124.4 0.1 fusion.19
  124.5 1.1 collective-permute-start.25
  125.6 1.3 collective-permute-start.26
  127.0 2.0 %collective-permute-start.27 = (bf16[16,2048]{1,0:T(8,128)(2,1)S(1)}, bf16[16,2048]{1,0:T(8,128)(2,1)S(1)}, u32[]{:S(2)}, u32[]{:S(2)}) collective-permute-start(bf16[16,2048]{1,0:T(8,128)(2,1)S(1)} %get-tuple-element.45), channel_id=1, source_target_pairs={{0,24},{8,16},{16,8},{24,0},{1,25},{9,17},{17,9},{25,1},{2,26},{10... | collective-permute-start | bytes 196616 | tf_op jit(solution)/shard_map/ppermute | solution.py:243
  129.0 1.7 %collective-permute-done.20 = bf16[16,2048]{1,0:T(8,128)(2,1)S(1)} collective-permute-done((bf16[16,2048]{1,0:T(8,128)(2,1)S(1)}, bf16[16,2048]{1,0:T(8,128)(2,1)S(1)}, u32[]{:S(2)}, u32[]{:S(2)}) %collective-permute-start.20) | collective-permute-done | bytes 65568 | tf_op jit(solution)/shard_map/ppermute | solution.py:243
  130.7 3.7 %collective-permute-done.26 = bf16[16,2048]{1,0:T(8,128)(2,1)S(1)} collective-permute-done((bf16[16,2048]{1,0:T(8,128)(2,1)S(1)}, bf16[16,2048]{1,0:T(8,128)(2,1)S(1)}, u32[]{:S(2)}, u32[]{:S(2)}) %collective-permute-start.26) | collective-permute-done | bytes 65568 | tf_op jit(solution)/shard_map/ppermute | solution.py:243
  134.5 0.7 fusion.4
  (45 shorter events, 0.5 us)
Async XLA Ops:
  5.6 3.3 %collective-permute-start = (bf16[32,4096]{1,0:T(8,128)(2,1)}, bf16[32,4096]{1,0:T(8,128)(2,1)S(1)}, u32[]{:S(2)}, u32[]{:S(2)}) collective-permute-start(bf16[32,4096]{1,0:T(8,128)(2,1)} %get-tuple-element.18), channel_id=1, source_target_pairs={{0,1},{1,0},{2,3},{3,2},{4,5},{5,4},{6,7},{7,6},{8,9},{9,8},{10,11... | collective-permute-start | bytes 786440 | tf_op jit(solution)/shard_map/ppermute | solution.py:231
  9.8 6.8 %collective-permute-start.1 = (bf16[16,4096]{1,0:T(8,128)(2,1)S(1)}, bf16[16,4096]{1,0:T(8,128)(2,1)S(1)}, u32[]{:S(2)}, u32[]{:S(2)}) collective-permute-start(bf16[16,4096]{1,0:T(8,128)(2,1)S(1)} %add_convert_fusion.10), channel_id=1, source_target_pairs={{0,2},{2,0},{1,3},{3,1},{4,6},{6,4},{5,7},{7,5},{8,10},{10,8},{9,1... | collective-permute-start | bytes 393224 | tf_op jit(solution)/shard_map/ppermute | solution.py:235
  18.5 8.9 %collective-permute-start.2 = (bf16[16,2048]{1,0:T(8,128)(2,1)S(1)}, bf16[16,2048]{1,0:T(8,128)(2,1)S(1)}, u32[]{:S(2)}, u32[]{:S(2)}) collective-permute-start(bf16[16,2048]{1,0:T(8,128)(2,1)S(1)} %get-tuple-element.49), channel_id=1, source_target_pairs={{0,8},{8,0},{16,24},{24,16},{1,9},{9,1},{17,25},{25,17},{2,10},{10... | collective-permute-start | bytes 196616 | tf_op jit(solution)/shard_map/ppermute | solution.py:243
  20.3 7.4 %collective-permute-start.3 = (bf16[16,2048]{1,0:T(8,128)(2,1)S(1)}, bf16[16,2048]{1,0:T(8,128)(2,1)S(1)}, u32[]{:S(2)}, u32[]{:S(2)}) collective-permute-start(bf16[16,2048]{1,0:T(8,128)(2,1)S(1)} %get-tuple-element.49), channel_id=1, source_target_pairs={{0,16},{8,24},{16,0},{24,8},{1,17},{9,25},{17,1},{25,9},{2,18},{10... | collective-permute-start | bytes 196616 | tf_op jit(solution)/shard_map/ppermute | solution.py:243
  22.9 6.5 %collective-permute-start.4 = (bf16[16,2048]{1,0:T(8,128)(2,1)S(1)}, bf16[16,2048]{1,0:T(8,128)(2,1)S(1)}, u32[]{:S(2)}, u32[]{:S(2)}) collective-permute-start(bf16[16,2048]{1,0:T(8,128)(2,1)S(1)} %get-tuple-element.49), channel_id=1, source_target_pairs={{0,24},{8,16},{16,8},{24,0},{1,25},{9,17},{17,9},{25,1},{2,26},{10... | collective-permute-start | bytes 196616 | tf_op jit(solution)/shard_map/ppermute | solution.py:243
  22.9 9.4 %collective-permute-start.9 = (bf16[16,2176]{1,0:T(8,128)(2,1)S(1)}, bf16[16,2176]{1,0:T(8,128)(2,1)S(1)}, u32[]{:S(2)}, u32[]{:S(2)}) collective-permute-start(bf16[16,2176]{1,0:T(8,128)(2,1)S(1)} %get-tuple-element.50), channel_id=1, source_target_pairs={{0,8},{8,0},{16,24},{24,16},{1,9},{9,1},{17,25},{25,17},{2,10},{10... | collective-permute-start | bytes 208904 | tf_op jit(solution)/shard_map/ppermute | solution.py:243
  23.9 10.2 %collective-permute-start.10 = (bf16[16,2176]{1,0:T(8,128)(2,1)S(1)}, bf16[16,2176]{1,0:T(8,128)(2,1)S(1)}, u32[]{:S(2)}, u32[]{:S(2)}) collective-permute-start(bf16[16,2176]{1,0:T(8,128)(2,1)S(1)} %get-tuple-element.50), channel_id=1, source_target_pairs={{0,16},{8,24},{16,0},{24,8},{1,17},{9,25},{17,1},{25,9},{2,18},{10... | collective-permute-start | bytes 208904 | tf_op jit(solution)/shard_map/ppermute | solution.py:243
  27.4 6.8 %collective-permute-start.11 = (bf16[16,2176]{1,0:T(8,128)(2,1)S(1)}, bf16[16,2176]{1,0:T(8,128)(2,1)S(1)}, u32[]{:S(2)}, u32[]{:S(2)}) collective-permute-start(bf16[16,2176]{1,0:T(8,128)(2,1)S(1)} %get-tuple-element.50), channel_id=1, source_target_pairs={{0,24},{8,16},{16,8},{24,0},{1,25},{9,17},{17,9},{25,1},{2,26},{10... | collective-permute-start | bytes 208904 | tf_op jit(solution)/shard_map/ppermute | solution.py:243
  29.5 13.5 %collective-permute-start.5 = (bf16[64,2048]{1,0:T(8,128)(2,1)S(1)}, bf16[64,2048]{1,0:T(8,128)(2,1)S(1)}, u32[]{:S(2)}, u32[]{:S(2)}) collective-permute-start(bf16[64,2048]{1,0:T(8,128)(2,1)S(1)} %pad_maximum_fusion.1), channel_id=1, source_target_pairs={{0,2},{2,0},{1,3},{3,1},{4,6},{6,4},{5,7},{7,5},{8,10},{10,8},{9,1... | collective-permute-start | bytes 786440 | tf_op jit(solution)/shard_map/ppermute | solution.py:235
  34.1 37.8 %slice-start = ((s8[14680064]{0:T(1024)(128)(4,1)}), s8[2097152]{0:T(1024)(128)(4,1)S(1)}, s32[]{:S(2)}) async-start(s8[14680064]{0:T(1024)(128)(4,1)} %bitcast.9), calls=%async_computation | async-start | bytes 4194304
  34.2 6.6 %collective-permute-start.12 = (bf16[64,2176]{1,0:T(8,128)(2,1)S(1)}, bf16[64,2176]{1,0:T(8,128)(2,1)S(1)}, u32[]{:S(2)}, u32[]{:S(2)}) collective-permute-start(bf16[64,2176]{1,0:T(8,128)(2,1)S(1)} %pad_maximum_fusion), channel_id=1, source_target_pairs={{0,4},{4,0},{1,5},{5,1},{2,6},{6,2},{3,7},{7,3},{8,12},{12,8},{9,1... | collective-permute-start | bytes 835592 | tf_op jit(solution)/shard_map/ppermute | solution.py:239
  40.8 10.9 %collective-permute-start.13 = (bf16[128,2176]{1,0:T(8,128)(2,1)S(1)}, bf16[128,2176]{1,0:T(8,128)(2,1)S(1)}, u32[]{:S(2)}, u32[]{:S(2)}) collective-permute-start(bf16[128,2176]{1,0:T(8,128)(2,1)S(1)} %constant_dynamic-update-slice_fusion.5.n0.x0), channel_id=1, source_target_pairs={{0,2},{2,0},{1,3},{3,1},{4,6},{6,4},{5,7},{7,5},{8,10},{10,8},{9,1... | collective-permute-start | bytes 1671176 | tf_op jit(solution)/shard_map/ppermute | solution.py:235
  43.7 10.2 %collective-permute-start.6 = (bf16[128,2048]{1,0:T(8,128)(2,1)}, bf16[128,2048]{1,0:T(8,128)(2,1)}, u32[]{:S(2)}, u32[]{:S(2)}) collective-permute-start(bf16[128,2048]{1,0:T(8,128)(2,1)} %constant_dynamic-update-slice_fusion.x0), channel_id=1, source_target_pairs={{0,4},{4,0},{1,5},{5,1},{2,6},{6,2},{3,7},{7,3},{8,12},{12,8},{9,1... | collective-permute-start | bytes 1572872 | tf_op jit(solution)/shard_map/ppermute | solution.py:239
  45.2 8.7 %collective-permute-start.14 = (bf16[128,2176]{1,0:T(8,128)(2,1)S(1)}, bf16[128,2176]{1,0:T(8,128)(2,1)}, u32[]{:S(2)}, u32[]{:S(2)}) collective-permute-start(bf16[128,2176]{1,0:T(8,128)(2,1)S(1)} %constant_dynamic-update-slice_fusion.5.n0.x0), channel_id=1, source_target_pairs={{0,1},{1,0},{2,3},{3,2},{4,5},{5,4},{6,7},{7,6},{8,9},{9,8},{10,11... | collective-permute-start | bytes 1671176 | tf_op jit(solution)/shard_map/ppermute | solution.py:231
  51.7 2.8 %collective-permute-start.15 = (bf16[128,2176]{1,0:T(8,128)(2,1)S(1)}, bf16[128,2176]{1,0:T(8,128)(2,1)}, u32[]{:S(2)}, u32[]{:S(2)}) collective-permute-start(bf16[128,2176]{1,0:T(8,128)(2,1)S(1)} %collective-permute-done.13.n1.x1), channel_id=1, source_target_pairs={{0,1},{1,0},{2,3},{3,2},{4,5},{5,4},{6,7},{7,6},{8,9},{9,8},{10,11... | collective-permute-start | bytes 1671176 | tf_op jit(solution)/shard_map/ppermute | solution.py:231
  51.7 20.3 %collective-permute-start.7 = (bf16[128,2048]{1,0:T(8,128)(2,1)}, bf16[128,2048]{1,0:T(8,128)(2,1)}, u32[]{:S(2)}, u32[]{:S(2)}) collective-permute-start(bf16[128,2048]{1,0:T(8,128)(2,1)} %constant_dynamic-update-slice_fusion.x0), channel_id=1, source_target_pairs={{0,1},{1,0},{2,3},{3,2},{4,5},{5,4},{6,7},{7,6},{8,9},{9,8},{10,11... | collective-permute-start | bytes 1572872 | tf_op jit(solution)/shard_map/ppermute | solution.py:231
  53.9 18.1 %collective-permute-start.8 = (bf16[128,2048]{1,0:T(8,128)(2,1)}, bf16[128,2048]{1,0:T(8,128)(2,1)}, u32[]{:S(2)}, u32[]{:S(2)}) collective-permute-start(bf16[128,2048]{1,0:T(8,128)(2,1)} %collective-permute-done.6.x1), channel_id=1, source_target_pairs={{0,1},{1,0},{2,3},{3,2},{4,5},{5,4},{6,7},{7,6},{8,9},{9,8},{10,11... | collective-permute-start | bytes 1572872 | tf_op jit(solution)/shard_map/ppermute | solution.py:231
  56.9 5.2 %copy-start = (bf16[4,448,4096]{2,1,0:T(8,128)(2,1)S(1)}, bf16[4,448,4096]{2,1,0:T(8,128)(2,1)}, u32[]{:S(2)}) copy-start(bf16[4,448,4096]{2,1,0:T(8,128)(2,1)} %gate.3) | copy-start | bytes 44040196
  62.1 9.9 %slice-start.1 = ((s8[14680064]{0:T(1024)(128)(4,1)}), s8[4194304]{0:T(1024)(128)(4,1)S(1)}, s32[]{:S(2)}) async-start(s8[14680064]{0:T(1024)(128)(4,1)} %bitcast.9), calls=%async_computation.1 | async-start | bytes 8388608
  62.1 9.9 %slice-start.2 = ((s8[14680064]{0:T(1024)(128)(4,1)}), s8[4194304]{0:T(1024)(128)(4,1)S(1)}, s32[]{:S(2)}) async-start(s8[14680064]{0:T(1024)(128)(4,1)} %bitcast.9), calls=%async_computation.2 | async-start | bytes 8388608
  62.1 9.9 %slice-start.3 = ((s8[14680064]{0:T(1024)(128)(4,1)}), s8[4194304]{0:T(1024)(128)(4,1)S(1)}, s32[]{:S(2)}) async-start(s8[14680064]{0:T(1024)(128)(4,1)} %bitcast.9), calls=%async_computation.3 | async-start | bytes 8388608
  81.9 5.2 %copy-start.1 = (bf16[4,448,4096]{2,1,0:T(8,128)(2,1)S(1)}, bf16[4,448,4096]{2,1,0:T(8,128)(2,1)}, u32[]{:S(2)}) copy-start(bf16[4,448,4096]{2,1,0:T(8,128)(2,1)} %down.3) | copy-start | bytes 44040196
  90.9 4.5 %collective-permute-start.16 = (bf16[256,2048]{1,0:T(8,128)(2,1)S(1)}, bf16[256,2048]{1,0:T(8,128)(2,1)S(1)}, u32[]{:S(2)}, u32[]{:S(2)}) collective-permute-start(bf16[256,2048]{1,0:T(8,128)(2,1)S(1)} %get-tuple-element.26), channel_id=1, source_target_pairs={{0,1},{1,0},{2,3},{3,2},{4,5},{5,4},{6,7},{7,6},{8,9},{9,8},{10,11... | collective-permute-start | bytes 3145736 | tf_op jit(solution)/shard_map/ppermute | solution.py:231
  94.9 2.7 %collective-permute-start.22 = (bf16[256,2048]{1,0:T(8,128)(2,1)S(1)}, bf16[256,2048]{1,0:T(8,128)(2,1)S(1)}, u32[]{:S(2)}, u32[]{:S(2)}) collective-permute-start(bf16[256,2048]{1,0:T(8,128)(2,1)S(1)} %get-tuple-element.29), channel_id=1, source_target_pairs={{0,1},{1,0},{2,3},{3,2},{4,5},{5,4},{6,7},{7,6},{8,9},{9,8},{10,11... | collective-permute-start | bytes 3145736 | tf_op jit(solution)/shard_map/ppermute | solution.py:231
  95.8 14.0 %collective-permute-start.17 = (bf16[128,2048]{1,0:T(8,128)(2,1)S(1)}, bf16[128,2048]{1,0:T(8,128)(2,1)S(1)}, u32[]{:S(2)}, u32[]{:S(2)}) collective-permute-start(bf16[128,2048]{1,0:T(8,128)(2,1)S(1)} %get-tuple-element.37), channel_id=1, source_target_pairs={{0,2},{2,0},{1,3},{3,1},{4,6},{6,4},{5,7},{7,5},{8,10},{10,8},{9,1... | collective-permute-start | bytes 1572872 | tf_op jit(solution)/shard_map/ppermute | solution.py:235
  98.0 14.7 %collective-permute-start.23 = (bf16[128,2048]{1,0:T(8,128)(2,1)S(1)}, bf16[128,2048]{1,0:T(8,128)(2,1)S(1)}, u32[]{:S(2)}, u32[]{:S(2)}) collective-permute-start(bf16[128,2048]{1,0:T(8,128)(2,1)S(1)} %get-tuple-element.39), channel_id=1, source_target_pairs={{0,4},{4,0},{1,5},{5,1},{2,6},{6,2},{3,7},{7,3},{8,12},{12,8},{9,1... | collective-permute-start | bytes 1572872 | tf_op jit(solution)/shard_map/ppermute | solution.py:239
  109.9 8.1 %collective-permute-start.18 = (bf16[64,2048]{1,0:T(8,128)(2,1)S(1)}, bf16[64,2048]{1,0:T(8,128)(2,1)S(1)}, u32[]{:S(2)}, u32[]{:S(2)}) collective-permute-start(bf16[64,2048]{1,0:T(8,128)(2,1)S(1)} %add_convert_fusion.6), channel_id=1, source_target_pairs={{0,4},{4,0},{1,5},{5,1},{2,6},{6,2},{3,7},{7,3},{8,12},{12,8},{9,1... | collective-permute-start | bytes 786440 | tf_op jit(solution)/shard_map/ppermute | solution.py:239
  112.8 11.6 %collective-permute-start.24 = (bf16[64,2048]{1,0:T(8,128)(2,1)S(1)}, bf16[64,2048]{1,0:T(8,128)(2,1)S(1)}, u32[]{:S(2)}, u32[]{:S(2)}) collective-permute-start(bf16[64,2048]{1,0:T(8,128)(2,1)S(1)} %add_convert_fusion.4), channel_id=1, source_target_pairs={{0,2},{2,0},{1,3},{3,1},{4,6},{6,4},{5,7},{7,5},{8,10},{10,8},{9,1... | collective-permute-start | bytes 786440 | tf_op jit(solution)/shard_map/ppermute | solution.py:235
  118.1 8.9 %collective-permute-start.19 = (bf16[16,2048]{1,0:T(8,128)(2,1)S(1)}, bf16[16,2048]{1,0:T(8,128)(2,1)S(1)}, u32[]{:S(2)}, u32[]{:S(2)}) collective-permute-start(bf16[16,2048]{1,0:T(8,128)(2,1)S(1)} %get-tuple-element.41), channel_id=1, source_target_pairs={{0,8},{8,0},{16,24},{24,16},{1,9},{9,1},{17,25},{25,17},{2,10},{10... | collective-permute-start | bytes 196616 | tf_op jit(solution)/shard_map/ppermute | solution.py:243
  122.0 8.7 %collective-permute-start.20 = (bf16[16,2048]{1,0:T(8,128)(2,1)S(1)}, bf16[16,2048]{1,0:T(8,128)(2,1)S(1)}, u32[]{:S(2)}, u32[]{:S(2)}) collective-permute-start(bf16[16,2048]{1,0:T(8,128)(2,1)S(1)} %get-tuple-element.43), channel_id=1, source_target_pairs={{0,16},{8,24},{16,0},{24,8},{1,17},{9,25},{17,1},{25,9},{2,18},{10... | collective-permute-start | bytes 196616 | tf_op jit(solution)/shard_map/ppermute | solution.py:243
  122.4 8.3 %collective-permute-start.21 = (bf16[16,2048]{1,0:T(8,128)(2,1)S(1)}, bf16[16,2048]{1,0:T(8,128)(2,1)S(1)}, u32[]{:S(2)}, u32[]{:S(2)}) collective-permute-start(bf16[16,2048]{1,0:T(8,128)(2,1)S(1)} %get-tuple-element.42), channel_id=1, source_target_pairs={{0,24},{8,16},{16,8},{24,0},{1,25},{9,17},{17,9},{25,1},{2,26},{10... | collective-permute-start | bytes 196616 | tf_op jit(solution)/shard_map/ppermute | solution.py:243
  124.5 6.2 %collective-permute-start.25 = (bf16[16,2048]{1,0:T(8,128)(2,1)S(1)}, bf16[16,2048]{1,0:T(8,128)(2,1)S(1)}, u32[]{:S(2)}, u32[]{:S(2)}) collective-permute-start(bf16[16,2048]{1,0:T(8,128)(2,1)S(1)} %get-tuple-element.44), channel_id=1, source_target_pairs={{0,8},{8,0},{16,24},{24,16},{1,9},{9,1},{17,25},{25,17},{2,10},{10... | collective-permute-start | bytes 196616 | tf_op jit(solution)/shard_map/ppermute | solution.py:243
  125.6 8.8 %collective-permute-start.26 = (bf16[16,2048]{1,0:T(8,128)(2,1)S(1)}, bf16[16,2048]{1,0:T(8,128)(2,1)S(1)}, u32[]{:S(2)}, u32[]{:S(2)}) collective-permute-start(bf16[16,2048]{1,0:T(8,128)(2,1)S(1)} %get-tuple-element.46), channel_id=1, source_target_pairs={{0,16},{8,24},{16,0},{24,8},{1,17},{9,25},{17,1},{25,9},{2,18},{10... | collective-permute-start | bytes 196616 | tf_op jit(solution)/shard_map/ppermute | solution.py:243
  127.0 7.5 %collective-permute-start.27 = (bf16[16,2048]{1,0:T(8,128)(2,1)S(1)}, bf16[16,2048]{1,0:T(8,128)(2,1)S(1)}, u32[]{:S(2)}, u32[]{:S(2)}) collective-permute-start(bf16[16,2048]{1,0:T(8,128)(2,1)S(1)} %get-tuple-element.45), channel_id=1, source_target_pairs={{0,24},{8,16},{16,8},{24,0},{1,25},{9,17},{17,9},{25,1},{2,26},{10... | collective-permute-start | bytes 196616 | tf_op jit(solution)/shard_map/ppermute | solution.py:243

commit v3 on v2

--- a/solution.py
+++ b/solution.py
@@ -1,4 +1,3 @@
-import functools
 from functools import reduce
 import math
 
@@ -380,187 +379,162 @@
     )(place, table, counts, q, k_new, v_new, k_pool, v_pool, w_out)
 
 
-def routes_kernel(place, hot, n0, n1, n2, n3, pick_a, pick_b, spread_a, spread_b, scale):
-    rows, tokens = pick_a.shape
-    tile = rows // 5
-    notes = jnp.concatenate([n0[...], n1[...], n2[...], n3[...]], axis=0)
+def slot_spans(tile):
+    return [(0, 2 * tile), (2 * tile, tile), (3 * tile, tile), (4 * tile, tile)]
+
+
+def experts_kernel(
+    place, favored, a0, a1, a2, a3, b0, b1, b2, b3, gate, up, down,
+    a_keep, a_send, b_keep, b_send,
+    tokens, ring, pick, spread, scale, taken, act, made, out_a, out_b, in_sems, w_sems, out_sems,
+):
+    count = tokens.shape[0]
+    half = out_a.shape[1]
+    notes_at = half
+    tile = taken.shape[0] // 5
+    spans = slot_spans(tile)
+    first = jnp.maximum(favored[0], 0)
+    expert_of = [first] + [jnp.where(s - 1 < first, s - 1, s) for s in (1, 2, 3)]
+
+    loads = []
+    for i, ref in enumerate((a0, a1, a2, a3)):
+        loads.append((ref, tokens.at[i * 128 : (i + 1) * 128, 0 : half + 128]))
+    for i, ref in enumerate((b0, b1, b2, b3)):
+        for j in range(2):
+            row = (i // 2) * 256 + j * 128 + (i % 2) * 64
+            loads.append((ref.at[j * 64 : (j + 1) * 64, :], tokens.at[row : row + 64, half + 128 :]))
+    loads = [pltpu.make_async_copy(src, dst, in_sems.at[i]) for i, (src, dst) in enumerate(loads)]
+    for load in loads:
+        load.start()
+
+    def fetch(matrix, s, slot):
+        return pltpu.make_async_copy(matrix.at[expert_of[s]], ring.at[slot], w_sems.at[slot])
+
+    def fetch_inner(s):
+        fetch(gate, s, 2 * s).start()
+        fetch(up, s, 2 * s + 1).start()
+
+    fetch_inner(0)
+
+    for load in loads[:4]:
+        load.wait()
+    fetch_inner(1)
+    notes = tokens[:, notes_at : notes_at + 128]
     width = notes.shape[1]
     source = lax.broadcasted_iota(jnp.int32, (width, width), 0)
     target = lax.broadcasted_iota(jnp.int32, (width, width), 1)
-    wanted = (source < 24) & (target < 4) & (lax.rem(source, 8) == place[0] * 4 + target)
+    expert = jnp.where(target == 0, first, jnp.where(target - 1 < first, target - 1, target))
+    wanted = (source < 24) & (target < 4) & (lax.rem(source, 8) == place[0] * 4 + expert)
     share = dot_nn(notes, jnp.where(wanted, 1.0, 0.0).astype(jnp.bfloat16))
     kept = jnp.where(share > 0.0, 1.0, 0.0)
-    below = lax.broadcasted_iota(jnp.int32, (tokens, tokens), 1) < lax.broadcasted_iota(
-        jnp.int32, (tokens, tokens), 0
+    below = lax.broadcasted_iota(jnp.int32, (count, count), 1) < lax.broadcasted_iota(
+        jnp.int32, (count, count), 0
     )
     rank = dot_nn(jnp.where(below, 1.0, 0.0).astype(jnp.bfloat16), kept.astype(jnp.bfloat16))
-    lane = lax.broadcasted_iota(jnp.int32, share.shape, 1)
-    favored = hot[0]
-    base = lane * tile + jnp.where((favored >= 0) & (lane > favored), tile, 0)
-    spot = jnp.where(kept > 0.0, rank + base.astype(jnp.float32), -1.0)
+    spot = jnp.where(kept > 0.0, rank, -1000.0)
     spot_t = spot.T
-    row_id = lax.broadcasted_iota(jnp.int32, (rows, tokens), 0).astype(jnp.float32)
-    col_id = lax.broadcasted_iota(jnp.int32, (tokens, rows), 1).astype(jnp.float32)
-    picked = jnp.zeros((rows, tokens), jnp.float32)
-    spreading = jnp.zeros((tokens, rows), jnp.float32)
-    for e in range(4):
-        picked = picked + jnp.where(row_id == spot_t[e : e + 1, :], 1.0, 0.0)
-        spreading = spreading + jnp.where(col_id == spot[:, e : e + 1], 1.0, 0.0)
-    picked = picked.astype(jnp.bfloat16)
-    spreading = spreading.astype(jnp.bfloat16)
-    pick_a[...] = picked
-    spread_a[...] = spreading
-    for i in range(0, tokens // 64, 4):
-        for j, k in enumerate((0, 2, 1, 3)):
-            old, new = slice((i + k) * 64, (i + k + 1) * 64), slice((i + j) * 64, (i + j + 1) * 64)
-            pick_b[:, new] = picked[:, old]
-            spread_b[new, :] = spreading[old, :]
-    found = dot_nn(picked, notes)
-    row = lax.broadcasted_iota(jnp.int32, found.shape, 0)
-    column = lax.broadcasted_iota(jnp.int32, found.shape, 1)
-    mine = lax.rem(column, 8) - place[0] * 4
-    first = mine * tile + jnp.where((favored >= 0) & (mine > favored), tile, 0)
-    size = jnp.where(mine == favored, 2 * tile, tile)
-    inside = (row >= first) & (row < first + size) & (mine >= 0) & (mine < 4) & (column < 24)
-    total = jnp.sum(jnp.where(inside, found, 0.0), axis=1, keepdims=True)
-    scale[...] = jnp.broadcast_to(total, scale.shape)
-
-
-def routes_call(place, hot, pieces, tile):
-    tokens = sum(piece.shape[0] for piece in pieces)
-    rows = 5 * tile
-    vmem, smem = (pl.BlockSpec(memory_space=s) for s in (pltpu.VMEM, pltpu.SMEM))
-    column = pieces[0].shape[1] // 128 - 1
-    note = pl.BlockSpec((pieces[0].shape[0], 128), lambda i: (0, column))
-    pick = jax.ShapeDtypeStruct((rows, tokens), jnp.bfloat16)
-    spread = jax.ShapeDtypeStruct((tokens, rows), jnp.bfloat16)
+    lane = lax.broadcasted_iota(jnp.int32, (1, width), 1)
+    for s, (row, rows) in enumerate(spans):
+        ids = lax.broadcasted_iota(jnp.int32, (rows, count), 0).astype(jnp.float32)
+        picked = jnp.where(ids == spot_t[s : s + 1, :], 1.0, 0.0).astype(jnp.bfloat16)
+        pick[row : row + rows, :] = picked
+        found = dot_nn(picked, notes)
+        mine = (lane < 24) & (lax.rem(lane, 8) == place[0] * 4 + expert_of[s])
+        part = jnp.sum(jnp.where(mine, found, 0.0), axis=1, keepdims=True)
+        scale[row : row + rows, :] = jnp.broadcast_to(part, (rows, width))
+    for block in range(spread.shape[1] // 128):
+        ids = (lax.broadcasted_iota(jnp.int32, (count, 128), 1) + block * 128).astype(jnp.float32)
+        total = jnp.zeros((count, 128), jnp.float32)
+        for s, (row, rows) in enumerate(spans):
+            if row < (block + 1) * 128 and row + rows > block * 128:
+                total = total + jnp.where(ids == spot[:, s : s + 1] + row, 1.0, 0.0)
+        spread[:, block * 128 : (block + 1) * 128] = total.astype(jnp.bfloat16)
+    made[5 * tile :, :] = jnp.zeros_like(made[5 * tile :, :])
+
+    for load in loads[4:]:
+        load.wait()
+
+    for start in range(0, 2 * half, 512):
+        at = start if start < half else start + 128
+        taken[:, start : start + 512] = dot_nn(pick[...], tokens[:, at : at + 512]).astype(jnp.bfloat16)
+
+    fetch_inner(2)
+    for s, (row, rows) in enumerate(spans):
+        fetch(gate, s, 2 * s).wait()
+        g = dot_nt(taken[row : row + rows, :], ring[2 * s])
+        fetch(up, s, 2 * s + 1).wait()
+        u = dot_nt(taken[row : row + rows, :], ring[2 * s + 1])
+        act[row : row + rows, :] = (g / (1.0 + jnp.exp(-g)) * u).astype(jnp.bfloat16)
+        if s == 0:
+            fetch_inner(3)
+        for later in ((), (0,), (1, 2), (3,))[s]:
+            fetch(down, later, 2 * later).start()
+
+    for s, (row, rows) in enumerate(spans):
+        fetch(down, s, 2 * s).wait()
+        part = scale[row : row + rows, 0:1]
+        for start in range(0, 2 * half, 1024):
+            o = dot_nn(act[row : row + rows, :], ring[2 * s, :, start : start + 1024])
+            made[row : row + rows, start : start + 1024] = (o * part).astype(jnp.bfloat16)
+
+    stores = []
+    rows = count // 2
+    for i, (out, out_keep, out_send) in enumerate(((out_a, a_keep, a_send), (out_b, b_keep, b_send))):
+        for start in range(0, half, 1024):
+            for at in range(start, start + 1024, 512):
+                y = dot_nn(spread[...], made[:, i * half + at : i * half + at + 512]).astype(jnp.bfloat16)
+                if i == 0:
+                    out[:, at : at + 512] = y
+                else:
+                    for j in range(8):
+                        to = (j // 4) * 4 + (j % 2) * 2 + (j // 2) % 2
+                        out[to * 64 : (to + 1) * 64, at : at + 512] = y[j * 64 : (j + 1) * 64, :]
+            for side, target_ref in enumerate((out_keep, out_send)):
+                store = pltpu.make_async_copy(
+                    out.at[side * rows : (side + 1) * rows, start : start + 1024],
+                    target_ref.at[:, start : start + 1024],
+                    out_sems.at[len(stores)],
+                )
+                store.start()
+                stores.append(store)
+    for store in stores:
+        store.wait()
+
+
+def experts_call(place, favored, pieces_a, pieces_b, gate, up, down):
+    _, hidden, width = gate.shape
+    count = sum(piece.shape[0] for piece in pieces_a)
+    tile = CAP_MOST * 32
+    rows, padded = 5 * tile, -(-5 * tile // 128) * 128
+    half = width // 2
+    smem, hbm = (pl.BlockSpec(memory_space=s) for s in (pltpu.SMEM, pl.ANY))
+    out = jax.ShapeDtypeStruct((count // 2, half), jnp.bfloat16)
     return pl.pallas_call(
-        routes_kernel,
-        grid=(1,),
-        out_shape=(pick, pick, spread, spread, jax.ShapeDtypeStruct((rows, 128), jnp.float32)),
-        in_specs=[smem, smem] + [note] * 4,
-        out_specs=(vmem,) * 5,
-        compiler_params=pltpu.CompilerParams(vmem_limit_bytes=20 * MIB),
-        cost_estimate=pl.CostEstimate(flops=10**8, bytes_accessed=2 * 10**6, transcendentals=0),
-        name="routes",
-    )(place, hot, *pieces)
-
-
-def span_of(expert, favored, tile, rows):
-    first = expert * tile + jnp.where((favored >= 0) & (expert > favored), tile, 0)
-    return pl.ds(pl.multiple_of(first, 32), rows)
-
-
-def by_size(expert, favored, tile, run):
-    @pl.when(expert == favored)
-    def _():
-        run(span_of(expert, favored, tile, 2 * tile))
-
-    @pl.when(expert != favored)
-    def _():
-        run(span_of(expert, favored, tile, tile))
-
-
-def inner_kernel(done, hot, x0, x1, x2, x3, pick, gate, up, *refs):
-    expert = pl.program_id(0)
-    tile = pick.shape[0] // 5
-    favored = hot[0]
-    if done:
-        g_in, u_in, act, taken = refs
-    else:
-        g_out, u_out, taken = refs
-
-    @pl.when(expert == 0)
-    def _():
-        for start in range(0, taken.shape[1], 512):
-            total = jnp.zeros((pick.shape[0], 512), jnp.float32)
-            for i, piece in enumerate((x0, x1, x2, x3)):
-                rows = piece.shape[0]
-                total = total + dot_nn(pick[:, i * rows : (i + 1) * rows], piece[:, start : start + 512])
-            taken[:, start : start + 512] = total.astype(jnp.bfloat16)
-        if done:
-            act[4 * tile :, :] = jnp.zeros_like(act[4 * tile :, :])
-
-    def run(span):
-        x = taken[span, :]
-        g = dot_nt(x, gate[0])
-        u = dot_nt(x, up[0])
-        if done:
-            g = g + g_in[span, :]
-            u = u + u_in[span, :]
-            act[span, :] = (g / (1.0 + jnp.exp(-g)) * u).astype(jnp.bfloat16)
-        else:
-            g_out[span, :] = g
-            u_out[span, :] = u
-
-    by_size(expert, favored, tile, run)
-
-
-def inner_call(half, hot, pieces, pick, gate, up, before):
-    experts, hidden, width = gate.shape
-    rows = pick.shape[0]
-    wide = width // 2
-    vmem, smem = (pl.BlockSpec(memory_space=s) for s in (pltpu.VMEM, pltpu.SMEM))
-    weight = pl.BlockSpec((1, hidden, wide), lambda e: (e, 0, half))
-    part = jax.ShapeDtypeStruct((rows, hidden), jnp.float32)
-    out = jax.ShapeDtypeStruct((rows, hidden), jnp.bfloat16)
-    return pl.pallas_call(
-        functools.partial(inner_kernel, bool(before)),
-        grid=(experts,),
-        out_shape=out if before else (part, part),
-        in_specs=[smem] + [vmem] * 5 + [weight] * 2 + [vmem] * len(before),
-        out_specs=vmem if before else (vmem, vmem),
-        scratch_shapes=[pltpu.VMEM((rows, wide), jnp.bfloat16)],
-        compiler_params=pltpu.CompilerParams(vmem_limit_bytes=24 * MIB),
+        experts_kernel,
+        out_shape=(out,) * 4,
+        in_specs=[smem, smem] + [hbm] * 11,
+        out_specs=(hbm,) * 4,
+        scratch_shapes=[
+            pltpu.VMEM((count, width + 128), jnp.bfloat16),
+            pltpu.VMEM((8, hidden, width), jnp.bfloat16),
+            pltpu.VMEM((rows, count), jnp.bfloat16),
+            pltpu.VMEM((count, padded), jnp.bfloat16),
+            pltpu.VMEM((rows, 128), jnp.float32),
+            pltpu.VMEM((rows, width), jnp.bfloat16),
+            pltpu.VMEM((rows, hidden), jnp.bfloat16),
+            pltpu.VMEM((padded, width), jnp.bfloat16),
+            pltpu.VMEM((count, half), jnp.bfloat16),
+            pltpu.VMEM((count, half), jnp.bfloat16),
+            pltpu.SemaphoreType.DMA((12,)),
+            pltpu.SemaphoreType.DMA((8,)),
+            pltpu.SemaphoreType.DMA((8,)),
+        ],
+        compiler_params=pltpu.CompilerParams(vmem_limit_bytes=60 * MIB),
         cost_estimate=pl.CostEstimate(
-            flops=4 * rows * hidden * wide, bytes_accessed=experts * 4 * hidden * wide, transcendentals=rows * hidden
+            flops=6 * rows * hidden * width, bytes_accessed=24 * hidden * width, transcendentals=rows * hidden
         ),
-        name="inner_second" if before else "inner_first",
-    )(hot, *pieces, pick, gate, up, *before)
-
-
-def outer_kernel(hot, act, spread, scale, down, keep, send, made):
-    expert = pl.program_id(0)
-    tile = made.shape[0] // 5
-    favored = hot[0]
-
-    @pl.when(expert == 0)
-    def _():
-        made[4 * tile :, :] = jnp.zeros_like(made[4 * tile :, :])
-
-    def run(span):
-        made[span, :] = (dot_nn(act[span, :], down[0]) * scale[span, 0:1]).astype(jnp.bfloat16)
-
-    by_size(expert, favored, tile, run)
-
-    @pl.when(expert == pl.num_programs(0) - 1)
-    def _():
-        rows = keep.shape[0]
-        for start in range(0, made.shape[1], 512):
-            y = dot_nn(spread[...], made[:, start : start + 512]).astype(jnp.bfloat16)
-            keep[:, start : start + 512] = y[0:rows, :]
-            send[:, start : start + 512] = y[rows:, :]
-
-
-def outer_call(half, hot, act, spread, scale, down):
-    experts, hidden, width = down.shape
-    rows, wide = act.shape[0], width // 2
-    vmem, smem = (pl.BlockSpec(memory_space=s) for s in (pltpu.VMEM, pltpu.SMEM))
-    weight = pl.BlockSpec((1, hidden, wide), lambda e: (e, 0, half))
-    out = jax.ShapeDtypeStruct((spread.shape[0] // 2, wide), jnp.bfloat16)
-    return pl.pallas_call(
-        outer_kernel,
-        grid=(experts,),
-        out_shape=(out, out),
-        in_specs=[smem] + [vmem] * 3 + [weight],
-        out_specs=(vmem, vmem),
-        scratch_shapes=[pltpu.VMEM((rows, wide), jnp.bfloat16)],
-        compiler_params=pltpu.CompilerParams(vmem_limit_bytes=20 * MIB),
-        cost_estimate=pl.CostEstimate(
-            flops=4 * rows * hidden * wide, bytes_accessed=experts * 2 * hidden * wide, transcendentals=0
-        ),
-        name="outer",
-    )(hot, act, spread, scale, down)
+        name="experts",
+    )(place, favored, *pieces_a, *pieces_b, gate, up, down)
 
 
 def kept_shares(chosen_specialists, selection_shares, allowed_placements, favored_specialist):
@@ -620,12 +594,6 @@
     count = chosen_specialists.shape[0]
     x, t = lax.axis_index("expert"), lax.axis_index("tensor")
 
-    notes = notes_of(
-        kept_shares(chosen_specialists, selection_shares, allowed_placements, favored_specialist)
-    )
-    hot = favored_specialist - x * own_experts
-    hot = jnp.where((hot >= 0) & (hot < own_experts), hot, -1).astype(jnp.int32)
-
     send, keep = attention_call(
         t.astype(jnp.int32)[None],
         sequence_sheet_map.T,
@@ -637,7 +605,9 @@
         stored_content_sheets.reshape(-1, HD),
         attention_merge_matrix,
     )
-    got = over_core(send)
+    got, chosen_specialists, selection_shares, premix_scale_factor = lax.optimization_barrier(
+        (over_core(send), chosen_specialists, selection_shares, premix_scale_factor)
+    )
     far = plus(got[0:count], keep[0:count])
     near = plus(got[count:], keep[count:])
     own_attn = over_y(far).astype(jnp.float32) + near.astype(jnp.float32)
@@ -648,22 +618,26 @@
         jnp.bfloat16
     )
 
+    notes = notes_of(
+        kept_shares(chosen_specialists, selection_shares, allowed_placements, favored_specialist)
+    )
+    hot = favored_specialist - x * own_experts
+    hot = jnp.where((hot >= 0) & (hot < own_experts), hot, -1).astype(jnp.int32)
+
+    part = jnp.concatenate([normed[:, :half], notes, normed[:, half:]], axis=1)
+    column = [part, over_z(part, 1), over_z(part, 2), over_z(part, 3)]
     gathered = []
-    for part, first, second in (
-        (jnp.concatenate([normed[:, :half], notes], axis=1), over_x, over_y),
-        (normed[:, half:], over_y, over_x),
+    for lanes, first, second in (
+        (slice(0, half + 128), over_x, over_y),
+        (slice(half + 128, None), over_y, over_x),
     ):
-        part = joined(part, over_z(part, 1), over_z(part, 2), over_z(part, 3))
+        part = joined(*[rows[:, lanes] for rows in column])
         part = joined(part, first(part))
         other = second(part)
         gathered.append((part, other, over_core(part), over_core(other)))
-    pick_a, pick_b, spread_a, spread_b, scale = routes_call(
-        x.astype(jnp.int32)[None], hot, gathered[0], CAP_MOST * 32
-    )
-    before = inner_call(0, hot, gathered[0], pick_a, gating_matrices, expand_matrices, ())
-    act = inner_call(1, hot, gathered[1], pick_b, gating_matrices, expand_matrices, before)
-    a_keep, a_send = outer_call(0, hot, act, spread_a, scale, contract_matrices)
-    b_keep, b_send = outer_call(1, hot, act, spread_b, scale, contract_matrices)
+    a_keep, a_send, b_keep, b_send = experts_call(
+        x.astype(jnp.int32)[None], hot, *gathered, gating_matrices, expand_matrices, contract_matrices
+    )
     results = []
     for sent, kept, first, second in (
         (a_send, a_keep, over_y, over_x),
@@ -678,13 +652,13 @@
         far = plus(got[rows:], near[rows:])
         near = plus(got[:rows], near[:rows])
         got = second(far)
-        total = near.astype(jnp.float32) + got.astype(jnp.float32)
-        out = total[0:count]
-        for k in (1, 2, 3):
-            mine = total[k * count : (k + 1) * count].astype(jnp.bfloat16)
-            out = out + over_z(mine, k).astype(jnp.float32)
-        results.append(out)
-    return (wide + jnp.concatenate(results, axis=1)).astype(jnp.bfloat16)
+        results.append(near.astype(jnp.float32) + got.astype(jnp.float32))
+    total = jnp.concatenate(results, axis=1)
+    out = total[0:count]
+    for k in (1, 2, 3):
+        mine = total[k * count : (k + 1) * count].astype(jnp.bfloat16)
+        out = out + over_z(mine, k).astype(jnp.float32)
+    return (wide + out).astype(jnp.bfloat16)
 
 
 def solution(mesh):

time: 136 us -> 124 us (0.912)
  waiting for transfers between devices: 42.4 us -> 60 us
  local copies, waits for them, and re-layouts: 13.8 us -> 1.05 us
  starting transfers between devices: 35.7 us -> 23.5 us
  Pallas kernels: 35.3 us -> 28.4 us
  other arithmetic: 6.93 us -> 9.38 us
    ppermute x12 -> x6, starting transfers between devices: 19.6 us -> 8.07 us  [over_z(): return lax.ppermute(a, 'dp', [(i, i ^ k) for i in range(4)])]
    unnamed x18 -> x13, local copies, waits for them, and re-layouts: 12.3 us -> 0.83 us
    ppermute x12 -> x6, waiting for transfers between devices: 9.26 us -> 19.5 us  [over_z(): return lax.ppermute(a, 'dp', [(i, i ^ k) for i in range(4)])]
    pallas_call x5 -> x1, Pallas kernels: 29.7 us -> 22.8 us  [experts_call(): pl.pallas_call(experts_kernel, out_shape=(out,) * 4, in_specs=[smem, smem...]
    ppermute x7, waiting for transfers between devices: 0.95 us -> 5.42 us  [over_core(): return lax.ppermute(a, 'tensor', PAIRS_CORE)]
    ppermute x5, waiting for transfers between devices: 20.3 us -> 23.7 us  [over_y(): return lax.ppermute(a, 'tensor', PAIRS_Y)]
    convert_element_type x5, other arithmetic: 1.83 us -> 4.23 us  [plus(): return (a.astype(jnp.float32) + b.astype(jnp.float32)).astype(jnp.bfloat16)]
  transfers between devices with their start and end apart: 28 -> 22, of which waited for: 14 -> 16; matrix products, arithmetic and copies ran while one was open for 5% -> 4% of each run, Pallas kernels for 12% -> 0%
where the time goes in v3:
time: 124 us; the launch traced here: 123 us
  waiting for transfers between devices  60 us (48%)
  Pallas kernels  28.4 us (23%)
  starting transfers between devices  23.5 us (19%)
  other arithmetic  9.38 us (8%)
    ppermute x5, waiting for transfers between devices, over_y(): return lax.ppermute(a, 'tensor', PAIRS_Y)  23.7 us
    pallas_call x1, Pallas kernels, experts_call(): pl.pallas_call(experts_kernel, out_shape=(out,) * 4, in_specs=[smem, smem...  22.8 us
    ppermute x6, waiting for transfers between devices, over_z(): return lax.ppermute(a, 'dp', [(i, i ^ k) for i in range(4)])  19.5 us
    ppermute x4, waiting for transfers between devices, over_x(): return lax.ppermute(a, 'expert', PAIRS_X)  11.4 us
    ppermute x6, starting transfers between devices, over_z(): return lax.ppermute(a, 'dp', [(i, i ^ k) for i in range(4)])  8.07 us
    ppermute x5, starting transfers between devices, over_y(): return lax.ppermute(a, 'tensor', PAIRS_Y)  7.82 us
    ppermute x4, starting transfers between devices, over_x(): return lax.ppermute(a, 'expert', PAIRS_X)  5.88 us
    pallas_call x1, Pallas kernels, attention_call(): pl.pallas_call(attend_kernel, out_shape=(half, half), in_specs=[smem, sme...  5.59 us
  transfers between devices with their start and end apart: 22, of which 16 were waited for; matrix products, arithmetic and copies ran while one was open for 4% of the time, Pallas kernels for 0%

profile of v3, /device:TPU:0, one launch (start us, length us, event | category | flops | bytes accessed | tf_op | source)
XLA Modules:
  0.0 123.2 jit_solution(3409646358856008964)
XLA Ops:
  0.0 5.6 %attention.1 = (bf16[32,4096]{1,0:T(8,128)(2,1)}, bf16[32,4096]{1,0:T(8,128)(2,1)}) custom-call(s32[1]{0:T(128)} %bitcast.place, s32[8,17]{1,0:T(8,128)} %bitcast.11, s32[17]{0:T(128)} %counts.1, bf16[64,512]{1,0:T(8,128)(2,1)} %q.1, bf16[64,128]{1,0:T(8,128)(2,1)} %k_new.1, bf16[64,128]{1,0:T(8,128)(2,1)} %v_new.1, bf16[5120,128]{1,0:T(8,128)(2,1)} %bitcast.9, ...), custom_call_target="tpu_custom_call" | custom-call | flops 1000000000 | bytes 8000000 | tf_op jit(solution)/shard_map/attention/pallas_call | solution.py:358
  5.6 0.5 collective-permute-start
  6.8 0.7 fusion.18
  7.4 0.1 collective-permute-done
  7.5 0.7 fusion.15
  8.2 0.7 select_reduce_fusion
  8.9 0.1 copy.24
  9.0 0.9 add_convert_fusion.10
  9.9 3.0 %collective-permute-start.1 = (bf16[16,4096]{1,0:T(8,128)(2,1)S(1)}, bf16[16,4096]{1,0:T(8,128)(2,1)S(1)}, u32[]{:S(2)}, u32[]{:S(2)}) collective-permute-start(bf16[16,4096]{1,0:T(8,128)(2,1)S(1)} %add_convert_fusion.10), channel_id=1, source_target_pairs={{0,2},{2,0},{1,3},{3,1},{4,6},{6,4},{5,7},{7,5},{8,10},{10,8},{9,1... | collective-permute-start | bytes 393224 | tf_op jit(solution)/shard_map/ppermute | solution.py:234
  12.8 0.1 reduce-precision_convert_fusion.1
  13.0 0.7 convert_element_type.166
  13.7 0.1 fusion.17
  13.8 2.9 %collective-permute-done.1 = bf16[16,4096]{1,0:T(8,128)(2,1)S(1)} collective-permute-done((bf16[16,4096]{1,0:T(8,128)(2,1)S(1)}, bf16[16,4096]{1,0:T(8,128)(2,1)S(1)}, u32[]{:S(2)}, u32[]{:S(2)}) %collective-permute-start.1) | collective-permute-done | bytes 131104 | tf_op jit(solution)/shard_map/ppermute | solution.py:234
  16.6 1.2 fusion.2
  17.8 0.1 fusion.4
  18.0 3.9 %collective-permute-start.4 = (bf16[16,4224]{1,0:T(8,128)(2,1)S(1)}, bf16[16,4224]{1,0:T(8,128)(2,1)S(1)}, u32[]{:S(2)}, u32[]{:S(2)}) collective-permute-start(bf16[16,4224]{1,0:T(8,128)(2,1)S(1)} %pad_maximum_fusion.3), channel_id=1, source_target_pairs={{0,24},{8,16},{16,8},{24,0},{1,25},{9,17},{17,9},{25,1},{2,26},{10... | collective-permute-start | bytes 405512 | tf_op jit(solution)/shard_map/ppermute | solution.py:242
  21.9 0.0 collective-permute-start.3
  21.9 0.6 collective-permute-start.2
  22.5 7.5 %collective-permute-done.2 = bf16[16,4224]{1,0:T(8,128)(2,1)S(1)} collective-permute-done((bf16[16,4224]{1,0:T(8,128)(2,1)S(1)}, bf16[16,4224]{1,0:T(8,128)(2,1)S(1)}, u32[]{:S(2)}, u32[]{:S(2)}) %collective-permute-start.2) | collective-permute-done | bytes 135200 | tf_op jit(solution)/shard_map/ppermute | solution.py:242
  30.0 2.7 %collective-permute-done.3 = bf16[16,4224]{1,0:T(8,128)(2,1)S(1)} collective-permute-done((bf16[16,4224]{1,0:T(8,128)(2,1)S(1)}, bf16[16,4224]{1,0:T(8,128)(2,1)S(1)}, u32[]{:S(2)}, u32[]{:S(2)}) %collective-permute-start.3) | collective-permute-done | bytes 135200 | tf_op jit(solution)/shard_map/ppermute | solution.py:242
  32.8 0.0 collective-permute-done.4
  32.8 1.6 %collective-permute-start.5 = (bf16[64,2176]{1,0:T(8,128)(2,1)S(1)}, bf16[64,2176]{1,0:T(8,128)(2,1)S(1)}, u32[]{:S(2)}, u32[]{:S(2)}) collective-permute-start(bf16[64,2176]{1,0:T(8,128)(2,1)S(1)} %pad_maximum_fusion.1), channel_id=1, source_target_pairs={{0,4},{4,0},{1,5},{5,1},{2,6},{6,2},{3,7},{7,3},{8,12},{12,8},{9,1... | collective-permute-start | bytes 835592 | tf_op jit(solution)/shard_map/ppermute | solution.py:238
  34.5 1.6 %collective-permute-start.9 = (bf16[64,2048]{1,0:T(8,128)(2,1)S(1)}, bf16[64,2048]{1,0:T(8,128)(2,1)S(1)}, u32[]{:S(2)}, u32[]{:S(2)}) collective-permute-start(bf16[64,2048]{1,0:T(8,128)(2,1)S(1)} %pad_maximum_fusion.2), channel_id=1, source_target_pairs={{0,2},{2,0},{1,3},{3,1},{4,6},{6,4},{5,7},{7,5},{8,10},{10,8},{9,1... | collective-permute-start | bytes 786440 | tf_op jit(solution)/shard_map/ppermute | solution.py:234
  36.1 4.5 %collective-permute-done.5 = bf16[64,2176]{1,0:T(8,128)(2,1)S(1)} collective-permute-done((bf16[64,2176]{1,0:T(8,128)(2,1)S(1)}, bf16[64,2176]{1,0:T(8,128)(2,1)S(1)}, u32[]{:S(2)}, u32[]{:S(2)}) %collective-permute-start.5) | collective-permute-done | bytes 278560 | tf_op jit(solution)/shard_map/ppermute | solution.py:238
  40.6 1.6 %collective-permute-start.6 = (bf16[128,2176]{1,0:T(8,128)(2,1)S(1)}, bf16[128,2176]{1,0:T(8,128)(2,1)S(1)}, u32[]{:S(2)}, u32[]{:S(2)}) collective-permute-start(bf16[128,2176]{1,0:T(8,128)(2,1)S(1)} %constant_dynamic-update-slice_fusion.a0), channel_id=1, source_target_pairs={{0,2},{2,0},{1,3},{3,1},{4,6},{6,4},{5,7},{7,5},{8,10},{10,8},{9,1... | collective-permute-start | bytes 1671176 | tf_op jit(solution)/shard_map/ppermute | solution.py:234
  42.2 0.0 collective-permute-done.9
  42.2 1.5 %collective-permute-start.10 = (bf16[128,2048]{1,0:T(8,128)(2,1)S(1)}, bf16[128,2048]{1,0:T(8,128)(2,1)S(1)}, u32[]{:S(2)}, u32[]{:S(2)}) collective-permute-start(bf16[128,2048]{1,0:T(8,128)(2,1)S(1)} %constant_dynamic-update-slice_fusion.4.b0), channel_id=1, source_target_pairs={{0,4},{4,0},{1,5},{5,1},{2,6},{6,2},{3,7},{7,3},{8,12},{12,8},{9,1... | collective-permute-start | bytes 1572872 | tf_op jit(solution)/shard_map/ppermute | solution.py:238
  43.8 9.7 %collective-permute-done.6.a1 = bf16[128,2176]{1,0:T(8,128)(2,1)S(1)} collective-permute-done((bf16[128,2176]{1,0:T(8,128)(2,1)S(1)}, bf16[128,2176]{1,0:T(8,128)(2,1)S(1)}, u32[]{:S(2)}, u32[]{:S(2)}) %collective-permute-start.6) | collective-permute-done | bytes 557088 | tf_op jit(solution)/shard_map/ppermute | solution.py:234
  53.5 0.0 collective-permute-start.8
  53.5 0.5 collective-permute-start.11
  54.0 0.0 collective-permute-done.10.b1
  54.0 0.1 collective-permute-start.12
  54.1 2.2 %collective-permute-done.11.b2 = bf16[128,2048]{1,0:T(8,128)(2,1)} collective-permute-done((bf16[128,2048]{1,0:T(8,128)(2,1)S(1)}, bf16[128,2048]{1,0:T(8,128)(2,1)}, u32[]{:S(2)}, u32[]{:S(2)}) %collective-permute-start.11) | collective-permute-done | bytes 524320 | tf_op jit(solution)/shard_map/ppermute | solution.py:230
  56.3 0.0 collective-permute-done.7.a2
  56.3 0.8 collective-permute-done.12.b3
  57.1 0.0 copy-done.3
  57.1 0.8 copy-done.4
  57.9 22.8 %experts.1 = (bf16[256,2048]{1,0:T(8,128)(2,1)}, bf16[256,2048]{1,0:T(8,128)(2,1)}, bf16[256,2048]{1,0:T(8,128)(2,1)}, bf16[256,2048]{1,0:T(8,128)(2,1)}) custom-call(s32[1]{0:T(128)} %bitcast.4.place, s32[1]{0:T(128)S(6)} %select_n.16.favored, bf16[128,2176]{1,0:T(8,128)(2,1)} %copy-done, bf16[128,2176]{1,0:T(8,128)(2,1)} %copy-done.2, ...), custom_call_target="tpu_custom_call" | custom-call | flops 5284823040 | bytes 44040192 | tf_op jit(solution)/shard_map/experts/pallas_call | solution.py:512
  80.7 0.2 collective-permute-start.13
  80.9 0.4 collective-permute-start.16
  81.3 2.4 %collective-permute-done.13 = bf16[256,2048]{1,0:T(8,128)(2,1)S(1)} collective-permute-done((bf16[256,2048]{1,0:T(8,128)(2,1)}, bf16[256,2048]{1,0:T(8,128)(2,1)S(1)}, u32[]{:S(2)}, u32[]{:S(2)}) %collective-permute-start.13) | collective-permute-done | bytes 1048608 | tf_op jit(solution)/shard_map/ppermute | solution.py:230
  83.6 1.6 %add_convert_fusion.3 = (bf16[128,2048]{1,0:T(8,128)(2,1)S(1)}, bf16[128,2048]{1,0:T(8,128)(2,1)S(1)}) fusion(bf16[256,2048]{1,0:T(8,128)(2,1)S(1)} %collective-permute-done.13, bf16[256,2048]{1,0:T(8,128)(2,1)} %get-tuple-element.22), kind=kLoop, calls=%fused_computation.9 | loop fusion | flops 2097152 | bytes 3145728 | tf_op jit(solution)/shard_map/convert_element_type | solution.py:569
  85.2 1.6 %collective-permute-start.14 = (bf16[128,2048]{1,0:T(8,128)(2,1)S(1)}, bf16[128,2048]{1,0:T(8,128)(2,1)S(1)}, u32[]{:S(2)}, u32[]{:S(2)}) collective-permute-start(bf16[128,2048]{1,0:T(8,128)(2,1)S(1)} %get-tuple-element.29), channel_id=1, source_target_pairs={{0,2},{2,0},{1,3},{3,1},{4,6},{6,4},{5,7},{7,5},{8,10},{10,8},{9,1... | collective-permute-start | bytes 1572872 | tf_op jit(solution)/shard_map/ppermute | solution.py:234
  86.8 0.0 collective-permute-done.16
  86.8 1.6 %add_convert_fusion.1 = (bf16[128,2048]{1,0:T(8,128)(2,1)S(1)}, bf16[128,2048]{1,0:T(8,128)(2,1)S(1)}) fusion(bf16[256,2048]{1,0:T(8,128)(2,1)S(1)} %collective-permute-done.16, bf16[256,2048]{1,0:T(8,128)(2,1)} %get-tuple-element.24), kind=kLoop, calls=%fused_computation.7 | loop fusion | flops 2097152 | bytes 3145728 | tf_op jit(solution)/shard_map/convert_element_type | solution.py:569
  88.4 1.4 %collective-permute-start.17 = (bf16[128,2048]{1,0:T(8,128)(2,1)S(1)}, bf16[128,2048]{1,0:T(8,128)(2,1)S(1)}, u32[]{:S(2)}, u32[]{:S(2)}) collective-permute-start(bf16[128,2048]{1,0:T(8,128)(2,1)S(1)} %get-tuple-element.27), channel_id=1, source_target_pairs={{0,4},{4,0},{1,5},{5,1},{2,6},{6,2},{3,7},{7,3},{8,12},{12,8},{9,1... | collective-permute-start | bytes 1572872 | tf_op jit(solution)/shard_map/ppermute | solution.py:238
  89.8 9.5 %collective-permute-done.14 = bf16[128,2048]{1,0:T(8,128)(2,1)S(1)} collective-permute-done((bf16[128,2048]{1,0:T(8,128)(2,1)S(1)}, bf16[128,2048]{1,0:T(8,128)(2,1)S(1)}, u32[]{:S(2)}, u32[]{:S(2)}) %collective-permute-start.14) | collective-permute-done | bytes 524320 | tf_op jit(solution)/shard_map/ppermute | solution.py:234
  99.3 0.1 add_convert_fusion.6
  99.3 1.4 %collective-permute-start.15 = (bf16[64,2048]{1,0:T(8,128)(2,1)S(1)}, bf16[64,2048]{1,0:T(8,128)(2,1)S(1)}, u32[]{:S(2)}, u32[]{:S(2)}) collective-permute-start(bf16[64,2048]{1,0:T(8,128)(2,1)S(1)} %add_convert_fusion.6), channel_id=1, source_target_pairs={{0,4},{4,0},{1,5},{5,1},{2,6},{6,2},{3,7},{7,3},{8,12},{12,8},{9,1... | collective-permute-start | bytes 786440 | tf_op jit(solution)/shard_map/ppermute | solution.py:238
  100.7 2.2 %collective-permute-done.17 = bf16[128,2048]{1,0:T(8,128)(2,1)S(1)} collective-permute-done((bf16[128,2048]{1,0:T(8,128)(2,1)S(1)}, bf16[128,2048]{1,0:T(8,128)(2,1)S(1)}, u32[]{:S(2)}, u32[]{:S(2)}) %collective-permute-start.17) | collective-permute-done | bytes 524320 | tf_op jit(solution)/shard_map/ppermute | solution.py:238
  103.0 0.1 add_convert_fusion.4
  103.0 0.1 collective-permute-start.18
  103.1 4.7 %collective-permute-done.15 = bf16[64,2048]{1,0:T(8,128)(2,1)S(1)} collective-permute-done((bf16[64,2048]{1,0:T(8,128)(2,1)S(1)}, bf16[64,2048]{1,0:T(8,128)(2,1)S(1)}, u32[]{:S(2)}, u32[]{:S(2)}) %collective-permute-start.15) | collective-permute-done | bytes 262176 | tf_op jit(solution)/shard_map/ppermute | solution.py:238
  107.8 0.1 convert_add_fusion.1
  107.9 1.6 %collective-permute-done.18 = bf16[64,2048]{1,0:T(8,128)(2,1)S(1)} collective-permute-done((bf16[64,2048]{1,0:T(8,128)(2,1)S(1)}, bf16[64,2048]{1,0:T(8,128)(2,1)S(1)}, u32[]{:S(2)}, u32[]{:S(2)}) %collective-permute-start.18) | collective-permute-done | bytes 262176 | tf_op jit(solution)/shard_map/ppermute | solution.py:234
  109.5 0.1 convert_add_fusion
  109.6 0.1 fusion.1
  109.7 0.1 collective-permute-start.19
  109.8 1.9 %collective-permute-start.21 = (bf16[16,4096]{1,0:T(8,128)(2,1)S(1)}, bf16[16,4096]{1,0:T(8,128)(2,1)S(1)}, u32[]{:S(2)}, u32[]{:S(2)}) collective-permute-start(bf16[16,4096]{1,0:T(8,128)(2,1)S(1)} %get-tuple-element.32), channel_id=1, source_target_pairs={{0,24},{8,16},{16,8},{24,0},{1,25},{9,17},{17,9},{25,1},{2,26},{10... | collective-permute-start | bytes 393224 | tf_op jit(solution)/shard_map/ppermute | solution.py:242
  111.7 1.6 %collective-permute-start.20 = (bf16[16,4096]{1,0:T(8,128)(2,1)S(1)}, bf16[16,4096]{1,0:T(8,128)(2,1)S(1)}, u32[]{:S(2)}, u32[]{:S(2)}) collective-permute-start(bf16[16,4096]{1,0:T(8,128)(2,1)S(1)} %get-tuple-element.33), channel_id=1, source_target_pairs={{0,16},{8,24},{16,0},{24,8},{1,17},{9,25},{17,1},{25,9},{2,18},{10... | collective-permute-start | bytes 393224 | tf_op jit(solution)/shard_map/ppermute | solution.py:242
  113.3 1.9 %collective-permute-done.19 = bf16[16,4096]{1,0:T(8,128)(2,1)S(1)} collective-permute-done((bf16[16,4096]{1,0:T(8,128)(2,1)S(1)}, bf16[16,4096]{1,0:T(8,128)(2,1)S(1)}, u32[]{:S(2)}, u32[]{:S(2)}) %collective-permute-start.19) | collective-permute-done | bytes 131104 | tf_op jit(solution)/shard_map/ppermute | solution.py:242
  115.2 2.5 %collective-permute-done.21 = bf16[16,4096]{1,0:T(8,128)(2,1)S(1)} collective-permute-done((bf16[16,4096]{1,0:T(8,128)(2,1)S(1)}, bf16[16,4096]{1,0:T(8,128)(2,1)S(1)}, u32[]{:S(2)}, u32[]{:S(2)}) %collective-permute-start.21) | collective-permute-done | bytes 131104 | tf_op jit(solution)/shard_map/ppermute | solution.py:242
  117.6 4.9 %collective-permute-done.20 = bf16[16,4096]{1,0:T(8,128)(2,1)S(1)} collective-permute-done((bf16[16,4096]{1,0:T(8,128)(2,1)S(1)}, bf16[16,4096]{1,0:T(8,128)(2,1)S(1)}, u32[]{:S(2)}, u32[]{:S(2)}) %collective-permute-start.20) | collective-permute-done | bytes 131104 | tf_op jit(solution)/shard_map/ppermute | solution.py:242
  122.5 0.7 fusion.5
  (27 shorter events, 0.3 us)
Async XLA Ops:
  5.6 1.9 %collective-permute-start = (bf16[32,4096]{1,0:T(8,128)(2,1)}, bf16[32,4096]{1,0:T(8,128)(2,1)S(1)}, u32[]{:S(2)}, u32[]{:S(2)}) collective-permute-start(bf16[32,4096]{1,0:T(8,128)(2,1)} %get-tuple-element.15), channel_id=1, source_target_pairs={{0,1},{1,0},{2,3},{3,2},{4,5},{5,4},{6,7},{7,6},{8,9},{9,8},{10,11... | collective-permute-start | bytes 786440 | tf_op jit(solution)/shard_map/ppermute | solution.py:230
  9.9 6.8 %collective-permute-start.1 = (bf16[16,4096]{1,0:T(8,128)(2,1)S(1)}, bf16[16,4096]{1,0:T(8,128)(2,1)S(1)}, u32[]{:S(2)}, u32[]{:S(2)}) collective-permute-start(bf16[16,4096]{1,0:T(8,128)(2,1)S(1)} %add_convert_fusion.10), channel_id=1, source_target_pairs={{0,2},{2,0},{1,3},{3,1},{4,6},{6,4},{5,7},{7,5},{8,10},{10,8},{9,1... | collective-permute-start | bytes 393224 | tf_op jit(solution)/shard_map/ppermute | solution.py:234
  18.0 14.8 %collective-permute-start.4 = (bf16[16,4224]{1,0:T(8,128)(2,1)S(1)}, bf16[16,4224]{1,0:T(8,128)(2,1)S(1)}, u32[]{:S(2)}, u32[]{:S(2)}) collective-permute-start(bf16[16,4224]{1,0:T(8,128)(2,1)S(1)} %pad_maximum_fusion.3), channel_id=1, source_target_pairs={{0,24},{8,16},{16,8},{24,0},{1,25},{9,17},{17,9},{25,1},{2,26},{10... | collective-permute-start | bytes 405512 | tf_op jit(solution)/shard_map/ppermute | solution.py:242
  21.9 10.9 %collective-permute-start.3 = (bf16[16,4224]{1,0:T(8,128)(2,1)S(1)}, bf16[16,4224]{1,0:T(8,128)(2,1)S(1)}, u32[]{:S(2)}, u32[]{:S(2)}) collective-permute-start(bf16[16,4224]{1,0:T(8,128)(2,1)S(1)} %pad_maximum_fusion.3), channel_id=1, source_target_pairs={{0,16},{8,24},{16,0},{24,8},{1,17},{9,25},{17,1},{25,9},{2,18},{10... | collective-permute-start | bytes 405512 | tf_op jit(solution)/shard_map/ppermute | solution.py:242
  21.9 8.2 %collective-permute-start.2 = (bf16[16,4224]{1,0:T(8,128)(2,1)S(1)}, bf16[16,4224]{1,0:T(8,128)(2,1)S(1)}, u32[]{:S(2)}, u32[]{:S(2)}) collective-permute-start(bf16[16,4224]{1,0:T(8,128)(2,1)S(1)} %pad_maximum_fusion.3), channel_id=1, source_target_pairs={{0,8},{8,0},{16,24},{24,16},{1,9},{9,1},{17,25},{25,17},{2,10},{10... | collective-permute-start | bytes 405512 | tf_op jit(solution)/shard_map/ppermute | solution.py:242
  32.8 7.7 %collective-permute-start.5 = (bf16[64,2176]{1,0:T(8,128)(2,1)S(1)}, bf16[64,2176]{1,0:T(8,128)(2,1)S(1)}, u32[]{:S(2)}, u32[]{:S(2)}) collective-permute-start(bf16[64,2176]{1,0:T(8,128)(2,1)S(1)} %pad_maximum_fusion.1), channel_id=1, source_target_pairs={{0,4},{4,0},{1,5},{5,1},{2,6},{6,2},{3,7},{7,3},{8,12},{12,8},{9,1... | collective-permute-start | bytes 835592 | tf_op jit(solution)/shard_map/ppermute | solution.py:238
  34.5 7.7 %collective-permute-start.9 = (bf16[64,2048]{1,0:T(8,128)(2,1)S(1)}, bf16[64,2048]{1,0:T(8,128)(2,1)S(1)}, u32[]{:S(2)}, u32[]{:S(2)}) collective-permute-start(bf16[64,2048]{1,0:T(8,128)(2,1)S(1)} %pad_maximum_fusion.2), channel_id=1, source_target_pairs={{0,2},{2,0},{1,3},{3,1},{4,6},{6,4},{5,7},{7,5},{8,10},{10,8},{9,1... | collective-permute-start | bytes 786440 | tf_op jit(solution)/shard_map/ppermute | solution.py:234
  40.6 16.5 %copy-start = (bf16[128,2176]{1,0:T(8,128)(2,1)}, bf16[128,2176]{1,0:T(8,128)(2,1)S(1)}, u32[]{:S(2)}) copy-start(bf16[128,2176]{1,0:T(8,128)(2,1)S(1)} %constant_dynamic-update-slice_fusion.a0) | copy-start | bytes 1671172
  40.6 12.9 %collective-permute-start.6 = (bf16[128,2176]{1,0:T(8,128)(2,1)S(1)}, bf16[128,2176]{1,0:T(8,128)(2,1)S(1)}, u32[]{:S(2)}, u32[]{:S(2)}) collective-permute-start(bf16[128,2176]{1,0:T(8,128)(2,1)S(1)} %constant_dynamic-update-slice_fusion.a0), channel_id=1, source_target_pairs={{0,2},{2,0},{1,3},{3,1},{4,6},{6,4},{5,7},{7,5},{8,10},{10,8},{9,1... | collective-permute-start | bytes 1671176 | tf_op jit(solution)/shard_map/ppermute | solution.py:234
  42.2 14.9 %copy-start.1 = (bf16[128,2048]{1,0:T(8,128)(2,1)}, bf16[128,2048]{1,0:T(8,128)(2,1)S(1)}, u32[]{:S(2)}) copy-start(bf16[128,2048]{1,0:T(8,128)(2,1)S(1)} %constant_dynamic-update-slice_fusion.4.b0) | copy-start | bytes 1572868
  42.2 11.8 %collective-permute-start.10 = (bf16[128,2048]{1,0:T(8,128)(2,1)S(1)}, bf16[128,2048]{1,0:T(8,128)(2,1)S(1)}, u32[]{:S(2)}, u32[]{:S(2)}) collective-permute-start(bf16[128,2048]{1,0:T(8,128)(2,1)S(1)} %constant_dynamic-update-slice_fusion.4.b0), channel_id=1, source_target_pairs={{0,4},{4,0},{1,5},{5,1},{2,6},{6,2},{3,7},{7,3},{8,12},{12,8},{9,1... | collective-permute-start | bytes 1572872 | tf_op jit(solution)/shard_map/ppermute | solution.py:238
  43.8 12.6 %collective-permute-start.7 = (bf16[128,2176]{1,0:T(8,128)(2,1)S(1)}, bf16[128,2176]{1,0:T(8,128)(2,1)S(1)}, u32[]{:S(2)}, u32[]{:S(2)}) collective-permute-start(bf16[128,2176]{1,0:T(8,128)(2,1)S(1)} %constant_dynamic-update-slice_fusion.a0), channel_id=1, source_target_pairs={{0,1},{1,0},{2,3},{3,2},{4,5},{5,4},{6,7},{7,6},{8,9},{9,8},{10,11... | collective-permute-start | bytes 1671176 | tf_op jit(solution)/shard_map/ppermute | solution.py:230
  53.5 3.6 %copy-start.2 = (bf16[128,2176]{1,0:T(8,128)(2,1)}, bf16[128,2176]{1,0:T(8,128)(2,1)S(1)}, u32[]{:S(2)}) copy-start(bf16[128,2176]{1,0:T(8,128)(2,1)S(1)} %collective-permute-done.6.a1) | copy-start | bytes 1671172
  53.5 3.6 %collective-permute-start.8 = (bf16[128,2176]{1,0:T(8,128)(2,1)S(1)}, bf16[128,2176]{1,0:T(8,128)(2,1)S(1)}, u32[]{:S(2)}, u32[]{:S(2)}) collective-permute-start(bf16[128,2176]{1,0:T(8,128)(2,1)S(1)} %collective-permute-done.6.a1), channel_id=1, source_target_pairs={{0,1},{1,0},{2,3},{3,2},{4,5},{5,4},{6,7},{7,6},{8,9},{9,8},{10,11... | collective-permute-start | bytes 1671176 | tf_op jit(solution)/shard_map/ppermute | solution.py:230
  53.5 2.8 %collective-permute-start.11 = (bf16[128,2048]{1,0:T(8,128)(2,1)S(1)}, bf16[128,2048]{1,0:T(8,128)(2,1)}, u32[]{:S(2)}, u32[]{:S(2)}) collective-permute-start(bf16[128,2048]{1,0:T(8,128)(2,1)S(1)} %constant_dynamic-update-slice_fusion.4.b0), channel_id=1, source_target_pairs={{0,1},{1,0},{2,3},{3,2},{4,5},{5,4},{6,7},{7,6},{8,9},{9,8},{10,11... | collective-permute-start | bytes 1572872 | tf_op jit(solution)/shard_map/ppermute | solution.py:230
  54.0 3.1 %copy-start.5 = (bf16[128,2048]{1,0:T(8,128)(2,1)}, bf16[128,2048]{1,0:T(8,128)(2,1)S(1)}, u32[]{:S(2)}) copy-start(bf16[128,2048]{1,0:T(8,128)(2,1)S(1)} %collective-permute-done.10.b1) | copy-start | bytes 1572868
  54.0 3.1 %collective-permute-start.12 = (bf16[128,2048]{1,0:T(8,128)(2,1)S(1)}, bf16[128,2048]{1,0:T(8,128)(2,1)}, u32[]{:S(2)}, u32[]{:S(2)}) collective-permute-start(bf16[128,2048]{1,0:T(8,128)(2,1)S(1)} %collective-permute-done.10.b1), channel_id=1, source_target_pairs={{0,1},{1,0},{2,3},{3,2},{4,5},{5,4},{6,7},{7,6},{8,9},{9,8},{10,11... | collective-permute-start | bytes 1572872 | tf_op jit(solution)/shard_map/ppermute | solution.py:230
  56.3 0.8 copy-start.3
  57.1 0.8 copy-start.4
  80.7 2.9 %collective-permute-start.13 = (bf16[256,2048]{1,0:T(8,128)(2,1)}, bf16[256,2048]{1,0:T(8,128)(2,1)S(1)}, u32[]{:S(2)}, u32[]{:S(2)}) collective-permute-start(bf16[256,2048]{1,0:T(8,128)(2,1)} %get-tuple-element.21), channel_id=1, source_target_pairs={{0,1},{1,0},{2,3},{3,2},{4,5},{5,4},{6,7},{7,6},{8,9},{9,8},{10,11... | collective-permute-start | bytes 3145736 | tf_op jit(solution)/shard_map/ppermute | solution.py:230
  80.9 5.9 %collective-permute-start.16 = (bf16[256,2048]{1,0:T(8,128)(2,1)}, bf16[256,2048]{1,0:T(8,128)(2,1)S(1)}, u32[]{:S(2)}, u32[]{:S(2)}) collective-permute-start(bf16[256,2048]{1,0:T(8,128)(2,1)} %get-tuple-element.23), channel_id=1, source_target_pairs={{0,1},{1,0},{2,3},{3,2},{4,5},{5,4},{6,7},{7,6},{8,9},{9,8},{10,11... | collective-permute-start | bytes 3145736 | tf_op jit(solution)/shard_map/ppermute | solution.py:230
  85.2 14.0 %collective-permute-start.14 = (bf16[128,2048]{1,0:T(8,128)(2,1)S(1)}, bf16[128,2048]{1,0:T(8,128)(2,1)S(1)}, u32[]{:S(2)}, u32[]{:S(2)}) collective-permute-start(bf16[128,2048]{1,0:T(8,128)(2,1)S(1)} %get-tuple-element.29), channel_id=1, source_target_pairs={{0,2},{2,0},{1,3},{3,1},{4,6},{6,4},{5,7},{7,5},{8,10},{10,8},{9,1... | collective-permute-start | bytes 1572872 | tf_op jit(solution)/shard_map/ppermute | solution.py:234
  88.4 14.6 %collective-permute-start.17 = (bf16[128,2048]{1,0:T(8,128)(2,1)S(1)}, bf16[128,2048]{1,0:T(8,128)(2,1)S(1)}, u32[]{:S(2)}, u32[]{:S(2)}) collective-permute-start(bf16[128,2048]{1,0:T(8,128)(2,1)S(1)} %get-tuple-element.27), channel_id=1, source_target_pairs={{0,4},{4,0},{1,5},{5,1},{2,6},{6,2},{3,7},{7,3},{8,12},{12,8},{9,1... | collective-permute-start | bytes 1572872 | tf_op jit(solution)/shard_map/ppermute | solution.py:238
  99.3 8.5 %collective-permute-start.15 = (bf16[64,2048]{1,0:T(8,128)(2,1)S(1)}, bf16[64,2048]{1,0:T(8,128)(2,1)S(1)}, u32[]{:S(2)}, u32[]{:S(2)}) collective-permute-start(bf16[64,2048]{1,0:T(8,128)(2,1)S(1)} %add_convert_fusion.6), channel_id=1, source_target_pairs={{0,4},{4,0},{1,5},{5,1},{2,6},{6,2},{3,7},{7,3},{8,12},{12,8},{9,1... | collective-permute-start | bytes 786440 | tf_op jit(solution)/shard_map/ppermute | solution.py:238
  103.0 6.5 %collective-permute-start.18 = (bf16[64,2048]{1,0:T(8,128)(2,1)S(1)}, bf16[64,2048]{1,0:T(8,128)(2,1)S(1)}, u32[]{:S(2)}, u32[]{:S(2)}) collective-permute-start(bf16[64,2048]{1,0:T(8,128)(2,1)S(1)} %add_convert_fusion.4), channel_id=1, source_target_pairs={{0,2},{2,0},{1,3},{3,1},{4,6},{6,4},{5,7},{7,5},{8,10},{10,8},{9,1... | collective-permute-start | bytes 786440 | tf_op jit(solution)/shard_map/ppermute | solution.py:234
  109.7 5.5 %collective-permute-start.19 = (bf16[16,4096]{1,0:T(8,128)(2,1)S(1)}, bf16[16,4096]{1,0:T(8,128)(2,1)S(1)}, u32[]{:S(2)}, u32[]{:S(2)}) collective-permute-start(bf16[16,4096]{1,0:T(8,128)(2,1)S(1)} %get-tuple-element.31), channel_id=1, source_target_pairs={{0,8},{8,0},{16,24},{24,16},{1,9},{9,1},{17,25},{25,17},{2,10},{10... | collective-permute-start | bytes 393224 | tf_op jit(solution)/shard_map/ppermute | solution.py:242
  109.8 7.8 %collective-permute-start.21 = (bf16[16,4096]{1,0:T(8,128)(2,1)S(1)}, bf16[16,4096]{1,0:T(8,128)(2,1)S(1)}, u32[]{:S(2)}, u32[]{:S(2)}) collective-permute-start(bf16[16,4096]{1,0:T(8,128)(2,1)S(1)} %get-tuple-element.32), channel_id=1, source_target_pairs={{0,24},{8,16},{16,8},{24,0},{1,25},{9,17},{17,9},{25,1},{2,26},{10... | collective-permute-start | bytes 393224 | tf_op jit(solution)/shard_map/ppermute | solution.py:242
  111.7 10.8 %collective-permute-start.20 = (bf16[16,4096]{1,0:T(8,128)(2,1)S(1)}, bf16[16,4096]{1,0:T(8,128)(2,1)S(1)}, u32[]{:S(2)}, u32[]{:S(2)}) collective-permute-start(bf16[16,4096]{1,0:T(8,128)(2,1)S(1)} %get-tuple-element.33), channel_id=1, source_target_pairs={{0,16},{8,24},{16,0},{24,8},{1,17},{9,25},{17,1},{25,9},{2,18},{10... | collective-permute-start | bytes 393224 | tf_op jit(solution)/shard_map/ppermute | solution.py:242

commit v4 on v3

--- a/solution.py
+++ b/solution.py
@@ -224,6 +224,7 @@
 CAP_MOST = 3
 NEG = -1e30
 MIB = 1 << 20
+EXPERTS_MIB = 43
 
 
 def over_core(a):
@@ -250,21 +251,52 @@
     return lax.dot_general(a, b, (((1,), (0,)), ((), ())), preferred_element_type=jnp.float32)
 
 
+def note_routes(allowed, favored, chosen, shares, notes):
+    experts, count = allowed.shape[0], chosen.shape[1]
+    expert = lax.broadcasted_iota(jnp.int32, (experts, count), 0)
+    picked = [jnp.where(chosen[k : k + 1, :] == expert, 1.0, 0.0) for k in range(2)]
+    earlier = lax.broadcasted_iota(jnp.int32, (count, count), 0) < lax.broadcasted_iota(
+        jnp.int32, (count, count), 1
+    )
+    before = dot_nn(
+        (picked[0] + picked[1]).astype(jnp.bfloat16), jnp.where(earlier, 1.0, 0.0).astype(jnp.bfloat16)
+    )
+    limit = jnp.zeros((experts, count), jnp.int32)
+    for e in range(experts):
+        limit = jnp.where(expert == e, allowed[e], limit)
+    limit = jnp.where(expert == favored[0], PLACEMENT_MOST, limit).astype(jnp.float32)
+    rest = picked[0] * shares[0:1, :] + picked[1] * shares[1:2, :]
+    rest = jnp.where(before < limit, rest, 0.0)
+    parts = []
+    for _ in range(3):
+        part = rest.astype(jnp.bfloat16).astype(jnp.float32)
+        parts.append(part)
+        rest = rest - part
+    parts.append(jnp.zeros((128 - 3 * experts, count), jnp.float32))
+    parts = jnp.concatenate(parts, axis=0)
+    parts = jnp.concatenate([parts, jnp.zeros((128, 128 - count), jnp.float32)], axis=1)
+    notes[...] = parts.T[0:count, :].astype(jnp.bfloat16)
+
+
 def attend_kernel(
-    place, table, counts, q, k_new, v_new, k_hbm, v_hbm, w_hbm,
-    send, keep,
-    k_pool, v_pool, w_out, scores, times, weights, k_prompt, v_prompt, heads, ordered, sems,
+    place, table, counts, allowed, favored, chosen, shares, q_hbm, k_new_hbm, v_new_hbm, k_hbm, v_hbm, w_hbm,
+    send, keep, notes,
+    q, k_new, v_new, k_pool, v_pool, w_out, scores, times, weights, k_prompt, v_prompt, heads, ordered, sems,
 ):
     pool_rows = k_pool.shape[0]
     pages = pool_rows // 128
     slots = table.shape[0]
     group = q.shape[1] // HD
-    copies = [
-        pltpu.make_async_copy(src, dst, sems.at[i])
-        for i, (src, dst) in enumerate(((k_hbm, k_pool), (v_hbm, v_pool), (w_hbm, w_out)))
-    ]
+    pairs = [(q_hbm, q), (k_new_hbm, k_new)]
+    for source, target, parts in ((k_hbm, k_pool, 2), (v_hbm, v_pool, 2), (w_hbm, w_out, 4)):
+        rows = source.shape[0] // parts
+        for i in range(parts):
+            pairs.append((source.at[i * rows : (i + 1) * rows, :], target.at[i * rows : (i + 1) * rows, :]))
+    pairs.insert(4, (v_new_hbm, v_new))
+    copies = [pltpu.make_async_copy(src, dst, sems.at[i]) for i, (src, dst) in enumerate(pairs)]
     for copy in copies:
         copy.start()
+    note_routes(allowed, favored, chosen, shares, notes)
     root = 1.0 / math.sqrt(HD)
 
     lane = lax.broadcasted_iota(jnp.int32, (SINGLES, 128), 1)
@@ -282,7 +314,8 @@
             total = total + jnp.where(named[m] == page, seen[m], 0.0)
         times[:, page * 128 : (page + 1) * 128] = total
 
-    copies[0].wait()
+    for copy in copies[:4]:
+        copy.wait()
     q_single = jnp.concatenate([q[0:SINGLES, h * HD : (h + 1) * HD] for h in range(group)], axis=0)
     q_prompt = jnp.concatenate([q[SINGLES:, h * HD : (h + 1) * HD] for h in range(group)], axis=0)
     step = 1024
@@ -323,7 +356,8 @@
     p_new = jnp.exp(s_new - highest)
     denominator = jnp.sum(p_cache, axis=1, keepdims=True) + jnp.sum(p_new, axis=1, keepdims=True)
 
-    copies[1].wait()
+    for copy in copies[4:7]:
+        copy.wait()
     for m in range(slots):
         page = table[m, SINGLES]
         v_prompt[m * 128 : (m + 1) * 128, :] = v_pool[pl.ds(pl.multiple_of(page * 128, 128), 128), :]
@@ -343,24 +377,28 @@
     order = [(1 - y) * 2 + 1 - core, y * 2 + 1 - core, (1 - y) * 2 + core, y * 2 + core]
     for i, block in enumerate(order):
         ordered[i * 16 : (i + 1) * 16, :] = heads[pl.ds(pl.multiple_of(block * 16, 16), 16), :]
-    copies[2].wait()
+    for copy in copies[7:]:
+        copy.wait()
     for start in range(0, w_out.shape[1], 512):
         part = dot_nn(ordered[...], w_out[:, start : start + 512]).astype(jnp.bfloat16)
         send[:, start : start + 512] = part[0:32, :]
         keep[:, start : start + 512] = part[32:64, :]
 
 
-def attention_call(place, table, counts, q, k_new, v_new, k_pool, v_pool, w_out):
+def attention_call(place, table, counts, allowed, favored, chosen, shares, q, k_new, v_new, k_pool, v_pool, w_out):
     pool_rows, rows, width = k_pool.shape[0], q.shape[0], w_out.shape[1]
     vmem, smem, hbm = (pl.BlockSpec(memory_space=s) for s in (pltpu.VMEM, pltpu.SMEM, pl.ANY))
     half = jax.ShapeDtypeStruct((rows // 2, width), jnp.bfloat16)
     singles = SINGLES * (q.shape[1] // HD)
     return pl.pallas_call(
         attend_kernel,
-        out_shape=(half, half),
-        in_specs=[smem, smem, smem, vmem, vmem, vmem, hbm, hbm, hbm],
-        out_specs=(vmem, vmem),
+        out_shape=(half, half, jax.ShapeDtypeStruct((chosen.shape[1], 128), jnp.bfloat16)),
+        in_specs=[smem] * 5 + [vmem] * 2 + [hbm] * 6,
+        out_specs=(vmem,) * 3,
         scratch_shapes=[
+            pltpu.VMEM(q.shape, jnp.bfloat16),
+            pltpu.VMEM(k_new.shape, jnp.bfloat16),
+            pltpu.VMEM(v_new.shape, jnp.bfloat16),
             pltpu.VMEM((pool_rows, HD), jnp.bfloat16),
             pltpu.VMEM((pool_rows, HD), jnp.bfloat16),
             pltpu.VMEM(w_out.shape, jnp.bfloat16),
@@ -371,12 +409,12 @@
             pltpu.VMEM((table.shape[0] * 128, HD), jnp.bfloat16),
             pltpu.VMEM((rows, q.shape[1]), jnp.bfloat16),
             pltpu.VMEM((rows, q.shape[1]), jnp.bfloat16),
-            pltpu.SemaphoreType.DMA((3,)),
+            pltpu.SemaphoreType.DMA((11,)),
         ],
         compiler_params=pltpu.CompilerParams(vmem_limit_bytes=60 * MIB),
         cost_estimate=pl.CostEstimate(flops=10**9, bytes_accessed=8 * 10**6, transcendentals=6 * 10**5),
         name="attention",
-    )(place, table, counts, q, k_new, v_new, k_pool, v_pool, w_out)
+    )(place, table, counts, allowed, favored, chosen, shares, q, k_new, v_new, k_pool, v_pool, w_out)
 
 
 def slot_spans(tile):
@@ -386,10 +424,10 @@
 def experts_kernel(
     place, favored, a0, a1, a2, a3, b0, b1, b2, b3, gate, up, down,
     a_keep, a_send, b_keep, b_send,
-    tokens, ring, pick, spread, scale, taken, act, made, out_a, out_b, in_sems, w_sems, out_sems,
+    tokens, ring, pick, spread, scale, taken, act, in_sems, w_sems,
 ):
-    count = tokens.shape[0]
-    half = out_a.shape[1]
+    count, hidden = tokens.shape[0], act.shape[1]
+    half = a_keep.shape[1]
     notes_at = half
     tile = taken.shape[0] // 5
     spans = slot_spans(tile)
@@ -408,17 +446,16 @@
         load.start()
 
     def fetch(matrix, s, slot):
-        return pltpu.make_async_copy(matrix.at[expert_of[s]], ring.at[slot], w_sems.at[slot])
+        rows = ring.at[slot * hidden : (slot + 1) * hidden, :]
+        return pltpu.make_async_copy(matrix.at[expert_of[s]], rows, w_sems.at[slot])
 
     def fetch_inner(s):
         fetch(gate, s, 2 * s).start()
         fetch(up, s, 2 * s + 1).start()
 
-    fetch_inner(0)
-
     for load in loads[:4]:
         load.wait()
-    fetch_inner(1)
+    fetch_inner(0)
     notes = tokens[:, notes_at : notes_at + 128]
     width = notes.shape[1]
     source = lax.broadcasted_iota(jnp.int32, (width, width), 0)
@@ -449,8 +486,7 @@
             if row < (block + 1) * 128 and row + rows > block * 128:
                 total = total + jnp.where(ids == spot[:, s : s + 1] + row, 1.0, 0.0)
         spread[:, block * 128 : (block + 1) * 128] = total.astype(jnp.bfloat16)
-    made[5 * tile :, :] = jnp.zeros_like(made[5 * tile :, :])
-
+    fetch_inner(1)
     for load in loads[4:]:
         load.wait()
 
@@ -459,11 +495,14 @@
         taken[:, start : start + 512] = dot_nn(pick[...], tokens[:, at : at + 512]).astype(jnp.bfloat16)
 
     fetch_inner(2)
+    made = tokens
+    made[5 * tile :, :] = jnp.zeros_like(made[5 * tile :, :])
     for s, (row, rows) in enumerate(spans):
+        x = taken[row : row + rows, :]
         fetch(gate, s, 2 * s).wait()
-        g = dot_nt(taken[row : row + rows, :], ring[2 * s])
+        g = dot_nt(x, ring[2 * s * hidden : (2 * s + 1) * hidden, :])
         fetch(up, s, 2 * s + 1).wait()
-        u = dot_nt(taken[row : row + rows, :], ring[2 * s + 1])
+        u = dot_nt(x, ring[(2 * s + 1) * hidden : (2 * s + 2) * hidden, :])
         act[row : row + rows, :] = (g / (1.0 + jnp.exp(-g)) * u).astype(jnp.bfloat16)
         if s == 0:
             fetch_inner(3)
@@ -474,31 +513,20 @@
         fetch(down, s, 2 * s).wait()
         part = scale[row : row + rows, 0:1]
         for start in range(0, 2 * half, 1024):
-            o = dot_nn(act[row : row + rows, :], ring[2 * s, :, start : start + 1024])
+            o = dot_nn(act[row : row + rows, :], ring[2 * s * hidden : (2 * s + 1) * hidden, start : start + 1024])
             made[row : row + rows, start : start + 1024] = (o * part).astype(jnp.bfloat16)
 
-    stores = []
     rows = count // 2
-    for i, (out, out_keep, out_send) in enumerate(((out_a, a_keep, a_send), (out_b, b_keep, b_send))):
-        for start in range(0, half, 1024):
-            for at in range(start, start + 1024, 512):
-                y = dot_nn(spread[...], made[:, i * half + at : i * half + at + 512]).astype(jnp.bfloat16)
+    for i, outs in enumerate(((a_keep, a_send), (b_keep, b_send))):
+        for at in range(0, half, 512):
+            y = dot_nn(spread[...], made[:, i * half + at : i * half + at + 512]).astype(jnp.bfloat16)
+            for side, out in enumerate(outs):
                 if i == 0:
-                    out[:, at : at + 512] = y
+                    out[:, at : at + 512] = y[side * rows : (side + 1) * rows, :]
                 else:
-                    for j in range(8):
-                        to = (j // 4) * 4 + (j % 2) * 2 + (j // 2) % 2
-                        out[to * 64 : (to + 1) * 64, at : at + 512] = y[j * 64 : (j + 1) * 64, :]
-            for side, target_ref in enumerate((out_keep, out_send)):
-                store = pltpu.make_async_copy(
-                    out.at[side * rows : (side + 1) * rows, start : start + 1024],
-                    target_ref.at[:, start : start + 1024],
-                    out_sems.at[len(stores)],
-                )
-                store.start()
-                stores.append(store)
-    for store in stores:
-        store.wait()
+                    for j in range(4):
+                        to, row = (j % 2) * 2 + j // 2, side * rows + j * 64
+                        out[to * 64 : (to + 1) * 64, at : at + 512] = y[row : row + 64, :]
 
 
 def experts_call(place, favored, pieces_a, pieces_b, gate, up, down):
@@ -507,58 +535,30 @@
     tile = CAP_MOST * 32
     rows, padded = 5 * tile, -(-5 * tile // 128) * 128
     half = width // 2
-    smem, hbm = (pl.BlockSpec(memory_space=s) for s in (pltpu.SMEM, pl.ANY))
+    smem, vmem, hbm = (pl.BlockSpec(memory_space=s) for s in (pltpu.SMEM, pltpu.VMEM, pl.ANY))
     out = jax.ShapeDtypeStruct((count // 2, half), jnp.bfloat16)
     return pl.pallas_call(
         experts_kernel,
         out_shape=(out,) * 4,
         in_specs=[smem, smem] + [hbm] * 11,
-        out_specs=(hbm,) * 4,
+        out_specs=(vmem,) * 4,
         scratch_shapes=[
             pltpu.VMEM((count, width + 128), jnp.bfloat16),
-            pltpu.VMEM((8, hidden, width), jnp.bfloat16),
+            pltpu.VMEM((8 * hidden, width), jnp.bfloat16),
             pltpu.VMEM((rows, count), jnp.bfloat16),
             pltpu.VMEM((count, padded), jnp.bfloat16),
             pltpu.VMEM((rows, 128), jnp.float32),
             pltpu.VMEM((rows, width), jnp.bfloat16),
             pltpu.VMEM((rows, hidden), jnp.bfloat16),
-            pltpu.VMEM((padded, width), jnp.bfloat16),
-            pltpu.VMEM((count, half), jnp.bfloat16),
-            pltpu.VMEM((count, half), jnp.bfloat16),
             pltpu.SemaphoreType.DMA((12,)),
             pltpu.SemaphoreType.DMA((8,)),
-            pltpu.SemaphoreType.DMA((8,)),
         ],
-        compiler_params=pltpu.CompilerParams(vmem_limit_bytes=60 * MIB),
+        compiler_params=pltpu.CompilerParams(vmem_limit_bytes=EXPERTS_MIB * MIB),
         cost_estimate=pl.CostEstimate(
             flops=6 * rows * hidden * width, bytes_accessed=24 * hidden * width, transcendentals=rows * hidden
         ),
         name="experts",
     )(place, favored, *pieces_a, *pieces_b, gate, up, down)
-
-
-def kept_shares(chosen_specialists, selection_shares, allowed_placements, favored_specialist):
-    count, experts = chosen_specialists.shape[0], allowed_placements.shape[0]
-    index = jnp.arange(experts, dtype=jnp.int32)
-    picked = chosen_specialists[:, :, None] == index[None, None, :]
-    named = jnp.any(picked, axis=1)
-    earlier = jnp.arange(count)[:, None] > jnp.arange(count)[None, :]
-    before = jnp.dot(
-        earlier.astype(jnp.bfloat16), named.astype(jnp.bfloat16), preferred_element_type=jnp.float32
-    )
-    limit = jnp.where(index == favored_specialist[0], PLACEMENT_MOST, allowed_placements)
-    share = jnp.sum(jnp.where(picked, selection_shares[:, :, None], 0.0), axis=1)
-    return jnp.where(before < limit[None, :].astype(jnp.float32), share, 0.0)
-
-
-def notes_of(shares):
-    parts = []
-    for _ in range(3):
-        part = lax.reduce_precision(shares, 8, 7)
-        parts.append(part.astype(jnp.bfloat16))
-        shares = shares - part
-    notes = jnp.concatenate(parts, axis=1)
-    return jnp.pad(notes, ((0, 0), (0, 128 - notes.shape[1])))
 
 
 def joined(*parts):
@@ -594,10 +594,14 @@
     count = chosen_specialists.shape[0]
     x, t = lax.axis_index("expert"), lax.axis_index("tensor")
 
-    send, keep = attention_call(
+    send, keep, notes = attention_call(
         t.astype(jnp.int32)[None],
         sequence_sheet_map.T,
         stored_position_counts,
+        allowed_placements,
+        favored_specialist,
+        chosen_specialists.T,
+        selection_shares.T,
         question_vectors,
         fresh_lookup_vectors,
         fresh_content_vectors,
@@ -605,9 +609,7 @@
         stored_content_sheets.reshape(-1, HD),
         attention_merge_matrix,
     )
-    got, chosen_specialists, selection_shares, premix_scale_factor = lax.optimization_barrier(
-        (over_core(send), chosen_specialists, selection_shares, premix_scale_factor)
-    )
+    got = over_core(send)
     far = plus(got[0:count], keep[0:count])
     near = plus(got[count:], keep[count:])
     own_attn = over_y(far).astype(jnp.float32) + near.astype(jnp.float32)
@@ -618,9 +620,6 @@
         jnp.bfloat16
     )
 
-    notes = notes_of(
-        kept_shares(chosen_specialists, selection_shares, allowed_placements, favored_specialist)
-    )
     hot = favored_specialist - x * own_experts
     hot = jnp.where((hot >= 0) & (hot < own_experts), hot, -1).astype(jnp.int32)
 
@@ -645,20 +644,22 @@
     ):
         got = over_core(sent)
         rows = kept.shape[0] // 2
-        far = plus(got[rows:], kept[rows:])
-        near = plus(got[:rows], kept[:rows])
-        got = first(far)
+        from_first, got, kept = lax.optimization_barrier((first(plus(got[rows:], kept[rows:])), got, kept))
         rows = rows // 2
-        far = plus(got[rows:], near[rows:])
-        near = plus(got[:rows], near[:rows])
-        got = second(far)
+        near = plus(got[: 2 * rows], kept[: 2 * rows])
+        got = second(plus(from_first[rows:], near[rows:]))
+        near = plus(from_first[:rows], near[:rows])
         results.append(near.astype(jnp.float32) + got.astype(jnp.float32))
-    total = jnp.concatenate(results, axis=1)
-    out = total[0:count]
+    total_a, total_b = results
+    sent = jnp.concatenate([total_b[count : 2 * count], total_b[3 * count :]], axis=0).astype(jnp.bfloat16)
+    got = over_z(sent, 1).astype(jnp.float32)
+    out_a = total_a[0:count]
     for k in (1, 2, 3):
-        mine = total[k * count : (k + 1) * count].astype(jnp.bfloat16)
-        out = out + over_z(mine, k).astype(jnp.float32)
-    return (wide + out).astype(jnp.bfloat16)
+        mine = total_a[k * count : (k + 1) * count].astype(jnp.bfloat16)
+        out_a = out_a + over_z(mine, k).astype(jnp.float32)
+    far = (total_b[2 * count : 3 * count] + got[count:]).astype(jnp.bfloat16)
+    out_b = total_b[0:count] + got[0:count] + over_z(far, 2).astype(jnp.float32)
+    return (wide + jnp.concatenate([out_a, out_b], axis=1)).astype(jnp.bfloat16)
 
 
 def solution(mesh):

time: 124 us -> 117 us (0.944)
  Pallas kernels: 28.4 us -> 25.5 us
  other arithmetic: 9.38 us -> 6.66 us
  starting transfers between devices: 23.5 us -> 26 us
  waiting for transfers between devices: 60 us -> 57.6 us
    ppermute x5, waiting for transfers between devices: 23.7 us -> 27.9 us  [over_y(): return lax.ppermute(a, 'tensor', PAIRS_Y)]
    ppermute x4, waiting for transfers between devices: 11.4 us -> 7.48 us  [over_x(): return lax.ppermute(a, 'expert', PAIRS_X)]
    ppermute x6 -> x8, waiting for transfers between devices: 19.5 us -> 15.6 us  [over_z(): return lax.ppermute(a, 'dp', [(i, i ^ k) for i in range(4)])]
    pallas_call x1, Pallas kernels: 22.8 us -> 19.9 us  [experts_call(): pl.pallas_call(experts_kernel, out_shape=(out,) * 4, in_specs=[smem, smem...]
    convert_element_type x5 -> x7, other arithmetic: 4.23 us -> 1.57 us  [plus(): return (a.astype(jnp.float32) + b.astype(jnp.float32)).astype(jnp.bfloat16)]
    ppermute x5, starting transfers between devices: 7.82 us -> 9.34 us  [over_y(): return lax.ppermute(a, 'tensor', PAIRS_Y)]
    ppermute x6 -> x8, starting transfers between devices: 8.07 us -> 9.14 us  [over_z(): return lax.ppermute(a, 'dp', [(i, i ^ k) for i in range(4)])]
  transfers between devices with their start and end apart: 22 -> 24, of which waited for: 16 -> 18; matrix products, arithmetic and copies ran while one was open for 4% -> 2% of each run, Pallas kernels for 0% -> 0%
where the time goes in v4:
time: 117 us
  waiting for transfers between devices  57.6 us (49%)
  starting transfers between devices  26 us (22%)
  Pallas kernels  25.5 us (22%)
  other arithmetic  6.66 us (6%)
    ppermute x5, waiting for transfers between devices, over_y(): return lax.ppermute(a, 'tensor', PAIRS_Y)  27.9 us
    pallas_call x1, Pallas kernels, experts_call(): pl.pallas_call(experts_kernel, out_shape=(out,) * 4, in_specs=[smem, smem...  19.9 us
    ppermute x8, waiting for transfers between devices, over_z(): return lax.ppermute(a, 'dp', [(i, i ^ k) for i in range(4)])  15.6 us
    ppermute x5, starting transfers between devices, over_y(): return lax.ppermute(a, 'tensor', PAIRS_Y)  9.34 us
    ppermute x8, starting transfers between devices, over_z(): return lax.ppermute(a, 'dp', [(i, i ^ k) for i in range(4)])  9.14 us
    ppermute x4, waiting for transfers between devices, over_x(): return lax.ppermute(a, 'expert', PAIRS_X)  7.48 us
    ppermute x7, waiting for transfers between devices, over_core(): return lax.ppermute(a, 'tensor', PAIRS_CORE)  6.6 us
    ppermute x4, starting transfers between devices, over_x(): return lax.ppermute(a, 'expert', PAIRS_X)  5.95 us
  transfers between devices with their start and end apart: 24, of which 18 were waited for; matrix products, arithmetic and copies ran while one was open for 2% of the time, Pallas kernels for 0%

profile of v4, /device:TPU:0, one launch (start us, length us, event | category | flops | bytes accessed | tf_op | source)
XLA Modules:
  0.0 116.8 jit_solution(4120844688047977613)
XLA Ops:
  0.7 5.6 %attention.1 = (bf16[32,4096]{1,0:T(8,128)(2,1)}, bf16[32,4096]{1,0:T(8,128)(2,1)}, bf16[16,128]{1,0:T(8,128)(2,1)}) custom-call(s32[1]{0:T(128)} %bitcast.place, s32[8,17]{1,0:T(8,128)} %bitcast.10, s32[17]{0:T(128)} %counts.1, s32[8]{0:T(128)} %allowed.1, s32[1]{0:T(128)S(6)} %copy.26.favored, s32[2,16]{1,0:T(2,128)} %bitcast.11, f32[2,16]{1,0:T(2,128)} %bitcast.12, ...), custom_call_target="tpu_custom_call" | custom-call | flops 1000000000 | bytes 8000000 | tf_op jit(solution)/shard_map/attention/pallas_call | solution.py:393
  6.2 0.5 collective-permute-start
  6.8 1.4 %collective-permute-done = bf16[32,4096]{1,0:T(8,128)(2,1)S(1)} collective-permute-done((bf16[32,4096]{1,0:T(8,128)(2,1)}, bf16[32,4096]{1,0:T(8,128)(2,1)S(1)}, u32[]{:S(2)}, u32[]{:S(2)}) %collective-permute-start) | collective-permute-done | bytes 262176 | tf_op jit(solution)/shard_map/ppermute | solution.py:231
  8.1 0.9 add_convert_fusion.10
  9.1 3.0 %collective-permute-start.1 = (bf16[16,4096]{1,0:T(8,128)(2,1)S(1)}, bf16[16,4096]{1,0:T(8,128)(2,1)S(1)}, u32[]{:S(2)}, u32[]{:S(2)}) collective-permute-start(bf16[16,4096]{1,0:T(8,128)(2,1)S(1)} %add_convert_fusion.10), channel_id=1, source_target_pairs={{0,2},{2,0},{1,3},{3,1},{4,6},{6,4},{5,7},{7,5},{8,10},{10,8},{9,1... | collective-permute-start | bytes 393224 | tf_op jit(solution)/shard_map/ppermute | solution.py:235
  12.0 0.7 convert_element_type.159
  12.7 3.1 %collective-permute-done.1 = bf16[16,4096]{1,0:T(8,128)(2,1)S(1)} collective-permute-done((bf16[16,4096]{1,0:T(8,128)(2,1)S(1)}, bf16[16,4096]{1,0:T(8,128)(2,1)S(1)}, u32[]{:S(2)}, u32[]{:S(2)}) %collective-permute-start.1) | collective-permute-done | bytes 131104 | tf_op jit(solution)/shard_map/ppermute | solution.py:235
  15.8 1.2 %fusion = (f32[16]{0:T(128)S(1)}, bf16[16,4096]{1,0:T(8,128)(2,1)S(1)}) fusion(bf16[32,4096]{1,0:T(8,128)(2,1)} %get-tuple-element.19, bf16[32,4096]{1,0:T(8,128)(2,1)S(1)} %collective-permute-done, bf16[16,4096]{1,0:T(8,128)(2,1)S(1)} %collective-permute-done.1, bf16[16,4096]{1,0:T(8,128)(2,1)} %param.17), kind=kLoop, calls=%fused_computation.14 | loop fusion | flops 851952 | bytes 655424 | tf_op jit(solution)/shard_map/reduce_sum | solution.py:618
  17.0 0.1 fusion.2
  17.1 0.7 pad_maximum_fusion.2
  17.8 3.9 %collective-permute-start.4 = (bf16[16,4224]{1,0:T(8,128)(2,1)S(1)}, bf16[16,4224]{1,0:T(8,128)(2,1)S(1)}, u32[]{:S(2)}, u32[]{:S(2)}) collective-permute-start(bf16[16,4224]{1,0:T(8,128)(2,1)S(1)} %pad_maximum_fusion.2), channel_id=1, source_target_pairs={{0,24},{8,16},{16,8},{24,0},{1,25},{9,17},{17,9},{25,1},{2,26},{10... | collective-permute-start | bytes 405512 | tf_op jit(solution)/shard_map/ppermute | solution.py:243
  21.7 0.0 collective-permute-start.3
  21.7 0.6 collective-permute-start.2
  22.4 0.7 maximum_dynamic-update-slice_fusion
  23.1 6.8 %collective-permute-done.2 = bf16[16,4224]{1,0:T(8,128)(2,1)S(1)} collective-permute-done((bf16[16,4224]{1,0:T(8,128)(2,1)S(1)}, bf16[16,4224]{1,0:T(8,128)(2,1)S(1)}, u32[]{:S(2)}, u32[]{:S(2)}) %collective-permute-start.2) | collective-permute-done | bytes 135200 | tf_op jit(solution)/shard_map/ppermute | solution.py:243
  29.9 2.7 %collective-permute-done.3 = bf16[16,4224]{1,0:T(8,128)(2,1)S(1)} collective-permute-done((bf16[16,4224]{1,0:T(8,128)(2,1)S(1)}, bf16[16,4224]{1,0:T(8,128)(2,1)S(1)}, u32[]{:S(2)}, u32[]{:S(2)}) %collective-permute-start.3) | collective-permute-done | bytes 135200 | tf_op jit(solution)/shard_map/ppermute | solution.py:243
  32.6 0.0 collective-permute-done.4
  32.7 0.7 pad_maximum_fusion
  33.4 1.6 %collective-permute-start.5 = (bf16[64,2176]{1,0:T(8,128)(2,1)S(1)}, bf16[64,2176]{1,0:T(8,128)(2,1)S(1)}, u32[]{:S(2)}, u32[]{:S(2)}) collective-permute-start(bf16[64,2176]{1,0:T(8,128)(2,1)S(1)} %pad_maximum_fusion), channel_id=1, source_target_pairs={{0,4},{4,0},{1,5},{5,1},{2,6},{6,2},{3,7},{7,3},{8,12},{12,8},{9,1... | collective-permute-start | bytes 835592 | tf_op jit(solution)/shard_map/ppermute | solution.py:239
  35.0 1.6 %collective-permute-start.9 = (bf16[64,2048]{1,0:T(8,128)(2,1)S(1)}, bf16[64,2048]{1,0:T(8,128)(2,1)S(1)}, u32[]{:S(2)}, u32[]{:S(2)}) collective-permute-start(bf16[64,2048]{1,0:T(8,128)(2,1)S(1)} %pad_maximum_fusion.1), channel_id=1, source_target_pairs={{0,2},{2,0},{1,3},{3,1},{4,6},{6,4},{5,7},{7,5},{8,10},{10,8},{9,1... | collective-permute-start | bytes 786440 | tf_op jit(solution)/shard_map/ppermute | solution.py:235
  36.6 4.5 %collective-permute-done.5 = bf16[64,2176]{1,0:T(8,128)(2,1)S(1)} collective-permute-done((bf16[64,2176]{1,0:T(8,128)(2,1)S(1)}, bf16[64,2176]{1,0:T(8,128)(2,1)S(1)}, u32[]{:S(2)}, u32[]{:S(2)}) %collective-permute-start.5) | collective-permute-done | bytes 278560 | tf_op jit(solution)/shard_map/ppermute | solution.py:239
  41.1 1.6 %collective-permute-start.6 = (bf16[128,2176]{1,0:T(8,128)(2,1)S(1)}, bf16[128,2176]{1,0:T(8,128)(2,1)S(1)}, u32[]{:S(2)}, u32[]{:S(2)}) collective-permute-start(bf16[128,2176]{1,0:T(8,128)(2,1)S(1)} %constant_dynamic-update-slice_fusion.a0), channel_id=1, source_target_pairs={{0,2},{2,0},{1,3},{3,1},{4,6},{6,4},{5,7},{7,5},{8,10},{10,8},{9,1... | collective-permute-start | bytes 1671176 | tf_op jit(solution)/shard_map/ppermute | solution.py:235
  42.7 0.0 collective-permute-done.9
  42.7 1.6 %collective-permute-start.10 = (bf16[128,2048]{1,0:T(8,128)(2,1)S(1)}, bf16[128,2048]{1,0:T(8,128)(2,1)S(1)}, u32[]{:S(2)}, u32[]{:S(2)}) collective-permute-start(bf16[128,2048]{1,0:T(8,128)(2,1)S(1)} %constant_dynamic-update-slice_fusion.4.b0), channel_id=1, source_target_pairs={{0,4},{4,0},{1,5},{5,1},{2,6},{6,2},{3,7},{7,3},{8,12},{12,8},{9,1... | collective-permute-start | bytes 1572872 | tf_op jit(solution)/shard_map/ppermute | solution.py:239
  44.3 0.0 collective-permute-start.7
  44.3 9.7 %collective-permute-done.6.a1 = bf16[128,2176]{1,0:T(8,128)(2,1)S(1)} collective-permute-done((bf16[128,2176]{1,0:T(8,128)(2,1)S(1)}, bf16[128,2176]{1,0:T(8,128)(2,1)S(1)}, u32[]{:S(2)}, u32[]{:S(2)}) %collective-permute-start.6) | collective-permute-done | bytes 557088 | tf_op jit(solution)/shard_map/ppermute | solution.py:235
  54.1 0.0 collective-permute-start.8
  54.1 0.5 collective-permute-start.11
  54.6 0.0 collective-permute-start.12
  54.6 2.3 %collective-permute-done.11.b2 = bf16[128,2048]{1,0:T(8,128)(2,1)} collective-permute-done((bf16[128,2048]{1,0:T(8,128)(2,1)S(1)}, bf16[128,2048]{1,0:T(8,128)(2,1)}, u32[]{:S(2)}, u32[]{:S(2)}) %collective-permute-start.11) | collective-permute-done | bytes 524320 | tf_op jit(solution)/shard_map/ppermute | solution.py:231
  56.9 0.0 collective-permute-done.7.a2
  56.9 0.8 collective-permute-done.12.b3
  57.7 19.9 %experts.1 = (bf16[256,2048]{1,0:T(8,128)(2,1)S(1)}, bf16[256,2048]{1,0:T(8,128)(2,1)S(1)}, bf16[256,2048]{1,0:T(8,128)(2,1)S(1)}, bf16[256,2048]{1,0:T(8,128)(2,1)S(1)}) custom-call(s32[1]{0:T(128)} %bitcast.6.place, s32[1]{0:T(128)S(6)} %select_n.4.favored, bf16[128,2176]{1,0:T(8,128)(2,1)S(1)} %constant_dynamic-update-slice_fusion.a0, ...), custom_call_target="tpu_custom_call" | custom-call | flops 5284823040 | bytes 44040192 | tf_op jit(solution)/shard_map/experts/pallas_call | solution.py:540
  77.5 0.2 collective-permute-start.13
  77.7 0.4 collective-permute-start.19
  78.1 2.1 %collective-permute-done.13 = bf16[256,2048]{1,0:T(8,128)(2,1)S(1)} collective-permute-done((bf16[256,2048]{1,0:T(8,128)(2,1)S(1)}, bf16[256,2048]{1,0:T(8,128)(2,1)S(1)}, u32[]{:S(2)}, u32[]{:S(2)}) %collective-permute-start.13) | collective-permute-done | bytes 1048608 | tf_op jit(solution)/shard_map/ppermute | solution.py:231
  80.3 0.1 add_convert_fusion.3
  80.4 1.6 %collective-permute-start.14 = (bf16[128,2048]{1,0:T(8,128)(2,1)S(1)}, bf16[128,2048]{1,0:T(8,128)(2,1)S(1)}, u32[]{:S(2)}, u32[]{:S(2)}) collective-permute-start(bf16[128,2048]{1,0:T(8,128)(2,1)S(1)} %add_convert_fusion.3), channel_id=1, source_target_pairs={{0,2},{2,0},{1,3},{3,1},{4,6},{6,4},{5,7},{7,5},{8,10},{10,8},{9,1... | collective-permute-start | bytes 1572872 | tf_op jit(solution)/shard_map/ppermute | solution.py:235
  82.0 0.0 collective-permute-done.19
  82.0 0.1 add_convert_fusion.1
  82.1 1.4 %collective-permute-start.20 = (bf16[128,2048]{1,0:T(8,128)(2,1)S(1)}, bf16[128,2048]{1,0:T(8,128)(2,1)S(1)}, u32[]{:S(2)}, u32[]{:S(2)}) collective-permute-start(bf16[128,2048]{1,0:T(8,128)(2,1)S(1)} %add_convert_fusion.1), channel_id=1, source_target_pairs={{0,4},{4,0},{1,5},{5,1},{2,6},{6,2},{3,7},{7,3},{8,12},{12,8},{9,1... | collective-permute-start | bytes 1572872 | tf_op jit(solution)/shard_map/ppermute | solution.py:239
  83.5 10.9 %collective-permute-done.14 = bf16[128,2048]{1,0:T(8,128)(2,1)S(1)} collective-permute-done((bf16[128,2048]{1,0:T(8,128)(2,1)S(1)}, bf16[128,2048]{1,0:T(8,128)(2,1)S(1)}, u32[]{:S(2)}, u32[]{:S(2)}) %collective-permute-start.14) | collective-permute-done | bytes 524320 | tf_op jit(solution)/shard_map/ppermute | solution.py:235
  94.4 1.5 %collective-permute-done.20 = bf16[128,2048]{1,0:T(8,128)(2,1)S(1)} collective-permute-done((bf16[128,2048]{1,0:T(8,128)(2,1)S(1)}, bf16[128,2048]{1,0:T(8,128)(2,1)S(1)}, u32[]{:S(2)}, u32[]{:S(2)}) %collective-permute-start.20) | collective-permute-done | bytes 524320 | tf_op jit(solution)/shard_map/ppermute | solution.py:239
  95.9 0.1 add_convert_fusion
  96.1 0.1 add_convert_fusion.4
  96.1 1.6 %collective-permute-start.21 = (bf16[64,2048]{1,0:T(8,128)(2,1)S(1)}, bf16[64,2048]{1,0:T(8,128)(2,1)S(1)}, u32[]{:S(2)}, u32[]{:S(2)}) collective-permute-start(bf16[64,2048]{1,0:T(8,128)(2,1)S(1)} %add_convert_fusion.4), channel_id=1, source_target_pairs={{0,2},{2,0},{1,3},{3,1},{4,6},{6,4},{5,7},{7,5},{8,10},{10,8},{9,1... | collective-permute-start | bytes 786440 | tf_op jit(solution)/shard_map/ppermute | solution.py:235
  97.7 0.1 add_convert_fusion.2
  97.9 0.1 add_convert_fusion.6
  97.9 1.4 %collective-permute-start.15 = (bf16[64,2048]{1,0:T(8,128)(2,1)S(1)}, bf16[64,2048]{1,0:T(8,128)(2,1)S(1)}, u32[]{:S(2)}, u32[]{:S(2)}) collective-permute-start(bf16[64,2048]{1,0:T(8,128)(2,1)S(1)} %add_convert_fusion.6), channel_id=1, source_target_pairs={{0,4},{4,0},{1,5},{5,1},{2,6},{6,2},{3,7},{7,3},{8,12},{12,8},{9,1... | collective-permute-start | bytes 786440 | tf_op jit(solution)/shard_map/ppermute | solution.py:239
  99.3 4.2 %collective-permute-done.21 = bf16[64,2048]{1,0:T(8,128)(2,1)S(1)} collective-permute-done((bf16[64,2048]{1,0:T(8,128)(2,1)S(1)}, bf16[64,2048]{1,0:T(8,128)(2,1)S(1)}, u32[]{:S(2)}, u32[]{:S(2)}) %collective-permute-start.21) | collective-permute-done | bytes 262176 | tf_op jit(solution)/shard_map/ppermute | solution.py:235
  103.5 0.1 fusion.9
  103.7 0.1 collective-permute-start.22
  103.7 1.5 %collective-permute-done.15 = bf16[64,2048]{1,0:T(8,128)(2,1)S(1)} collective-permute-done((bf16[64,2048]{1,0:T(8,128)(2,1)S(1)}, bf16[64,2048]{1,0:T(8,128)(2,1)S(1)}, u32[]{:S(2)}, u32[]{:S(2)}) %collective-permute-start.15) | collective-permute-done | bytes 262176 | tf_op jit(solution)/shard_map/ppermute | solution.py:239
  105.2 0.1 fusion.8
  105.4 0.6 collective-permute-start.16
  105.9 1.8 %collective-permute-start.18 = (bf16[16,2048]{1,0:T(8,128)(2,1)S(1)}, bf16[16,2048]{1,0:T(8,128)(2,1)S(1)}, u32[]{:S(2)}, u32[]{:S(2)}) collective-permute-start(bf16[16,2048]{1,0:T(8,128)(2,1)S(1)} %get-tuple-element.38), channel_id=1, source_target_pairs={{0,24},{8,16},{16,8},{24,0},{1,25},{9,17},{17,9},{25,1},{2,26},{10... | collective-permute-start | bytes 196616 | tf_op jit(solution)/shard_map/ppermute | solution.py:243
  107.8 1.2 collective-permute-start.17
  108.9 0.8 collective-permute-done.22
  109.8 1.0 collective-permute-start.23
  110.8 0.1 collective-permute-done.16
  110.9 1.1 collective-permute-done.18
  112.0 3.3 %collective-permute-done.17 = bf16[16,2048]{1,0:T(8,128)(2,1)S(1)} collective-permute-done((bf16[16,2048]{1,0:T(8,128)(2,1)S(1)}, bf16[16,2048]{1,0:T(8,128)(2,1)S(1)}, u32[]{:S(2)}, u32[]{:S(2)}) %collective-permute-start.17) | collective-permute-done | bytes 65568 | tf_op jit(solution)/shard_map/ppermute | solution.py:243
  115.4 0.7 collective-permute-done.23
  116.1 0.7 fusion.3
  (20 shorter events, 0.3 us)
Async XLA Ops:
  6.2 1.9 %collective-permute-start = (bf16[32,4096]{1,0:T(8,128)(2,1)}, bf16[32,4096]{1,0:T(8,128)(2,1)S(1)}, u32[]{:S(2)}, u32[]{:S(2)}) collective-permute-start(bf16[32,4096]{1,0:T(8,128)(2,1)} %get-tuple-element.18), channel_id=1, source_target_pairs={{0,1},{1,0},{2,3},{3,2},{4,5},{5,4},{6,7},{7,6},{8,9},{9,8},{10,11... | collective-permute-start | bytes 786440 | tf_op jit(solution)/shard_map/ppermute | solution.py:231
  9.1 6.8 %collective-permute-start.1 = (bf16[16,4096]{1,0:T(8,128)(2,1)S(1)}, bf16[16,4096]{1,0:T(8,128)(2,1)S(1)}, u32[]{:S(2)}, u32[]{:S(2)}) collective-permute-start(bf16[16,4096]{1,0:T(8,128)(2,1)S(1)} %add_convert_fusion.10), channel_id=1, source_target_pairs={{0,2},{2,0},{1,3},{3,1},{4,6},{6,4},{5,7},{7,5},{8,10},{10,8},{9,1... | collective-permute-start | bytes 393224 | tf_op jit(solution)/shard_map/ppermute | solution.py:235
  17.8 14.8 %collective-permute-start.4 = (bf16[16,4224]{1,0:T(8,128)(2,1)S(1)}, bf16[16,4224]{1,0:T(8,128)(2,1)S(1)}, u32[]{:S(2)}, u32[]{:S(2)}) collective-permute-start(bf16[16,4224]{1,0:T(8,128)(2,1)S(1)} %pad_maximum_fusion.2), channel_id=1, source_target_pairs={{0,24},{8,16},{16,8},{24,0},{1,25},{9,17},{17,9},{25,1},{2,26},{10... | collective-permute-start | bytes 405512 | tf_op jit(solution)/shard_map/ppermute | solution.py:243
  21.7 10.9 %collective-permute-start.3 = (bf16[16,4224]{1,0:T(8,128)(2,1)S(1)}, bf16[16,4224]{1,0:T(8,128)(2,1)S(1)}, u32[]{:S(2)}, u32[]{:S(2)}) collective-permute-start(bf16[16,4224]{1,0:T(8,128)(2,1)S(1)} %pad_maximum_fusion.2), channel_id=1, source_target_pairs={{0,16},{8,24},{16,0},{24,8},{1,17},{9,25},{17,1},{25,9},{2,18},{10... | collective-permute-start | bytes 405512 | tf_op jit(solution)/shard_map/ppermute | solution.py:243
  21.7 8.2 %collective-permute-start.2 = (bf16[16,4224]{1,0:T(8,128)(2,1)S(1)}, bf16[16,4224]{1,0:T(8,128)(2,1)S(1)}, u32[]{:S(2)}, u32[]{:S(2)}) collective-permute-start(bf16[16,4224]{1,0:T(8,128)(2,1)S(1)} %pad_maximum_fusion.2), channel_id=1, source_target_pairs={{0,8},{8,0},{16,24},{24,16},{1,9},{9,1},{17,25},{25,17},{2,10},{10... | collective-permute-start | bytes 405512 | tf_op jit(solution)/shard_map/ppermute | solution.py:243
  33.4 7.7 %collective-permute-start.5 = (bf16[64,2176]{1,0:T(8,128)(2,1)S(1)}, bf16[64,2176]{1,0:T(8,128)(2,1)S(1)}, u32[]{:S(2)}, u32[]{:S(2)}) collective-permute-start(bf16[64,2176]{1,0:T(8,128)(2,1)S(1)} %pad_maximum_fusion), channel_id=1, source_target_pairs={{0,4},{4,0},{1,5},{5,1},{2,6},{6,2},{3,7},{7,3},{8,12},{12,8},{9,1... | collective-permute-start | bytes 835592 | tf_op jit(solution)/shard_map/ppermute | solution.py:239
  35.0 7.7 %collective-permute-start.9 = (bf16[64,2048]{1,0:T(8,128)(2,1)S(1)}, bf16[64,2048]{1,0:T(8,128)(2,1)S(1)}, u32[]{:S(2)}, u32[]{:S(2)}) collective-permute-start(bf16[64,2048]{1,0:T(8,128)(2,1)S(1)} %pad_maximum_fusion.1), channel_id=1, source_target_pairs={{0,2},{2,0},{1,3},{3,1},{4,6},{6,4},{5,7},{7,5},{8,10},{10,8},{9,1... | collective-permute-start | bytes 786440 | tf_op jit(solution)/shard_map/ppermute | solution.py:235
  41.1 13.0 %collective-permute-start.6 = (bf16[128,2176]{1,0:T(8,128)(2,1)S(1)}, bf16[128,2176]{1,0:T(8,128)(2,1)S(1)}, u32[]{:S(2)}, u32[]{:S(2)}) collective-permute-start(bf16[128,2176]{1,0:T(8,128)(2,1)S(1)} %constant_dynamic-update-slice_fusion.a0), channel_id=1, source_target_pairs={{0,2},{2,0},{1,3},{3,1},{4,6},{6,4},{5,7},{7,5},{8,10},{10,8},{9,1... | collective-permute-start | bytes 1671176 | tf_op jit(solution)/shard_map/ppermute | solution.py:235
  42.7 11.8 %collective-permute-start.10 = (bf16[128,2048]{1,0:T(8,128)(2,1)S(1)}, bf16[128,2048]{1,0:T(8,128)(2,1)S(1)}, u32[]{:S(2)}, u32[]{:S(2)}) collective-permute-start(bf16[128,2048]{1,0:T(8,128)(2,1)S(1)} %constant_dynamic-update-slice_fusion.4.b0), channel_id=1, source_target_pairs={{0,4},{4,0},{1,5},{5,1},{2,6},{6,2},{3,7},{7,3},{8,12},{12,8},{9,1... | collective-permute-start | bytes 1572872 | tf_op jit(solution)/shard_map/ppermute | solution.py:239
  44.3 12.6 %collective-permute-start.7 = (bf16[128,2176]{1,0:T(8,128)(2,1)S(1)}, bf16[128,2176]{1,0:T(8,128)(2,1)S(1)}, u32[]{:S(2)}, u32[]{:S(2)}) collective-permute-start(bf16[128,2176]{1,0:T(8,128)(2,1)S(1)} %constant_dynamic-update-slice_fusion.a0), channel_id=1, source_target_pairs={{0,1},{1,0},{2,3},{3,2},{4,5},{5,4},{6,7},{7,6},{8,9},{9,8},{10,11... | collective-permute-start | bytes 1671176 | tf_op jit(solution)/shard_map/ppermute | solution.py:231
  54.1 3.6 %collective-permute-start.8 = (bf16[128,2176]{1,0:T(8,128)(2,1)S(1)}, bf16[128,2176]{1,0:T(8,128)(2,1)S(1)}, u32[]{:S(2)}, u32[]{:S(2)}) collective-permute-start(bf16[128,2176]{1,0:T(8,128)(2,1)S(1)} %collective-permute-done.6.a1), channel_id=1, source_target_pairs={{0,1},{1,0},{2,3},{3,2},{4,5},{5,4},{6,7},{7,6},{8,9},{9,8},{10,11... | collective-permute-start | bytes 1671176 | tf_op jit(solution)/shard_map/ppermute | solution.py:231
  54.1 2.8 %collective-permute-start.11 = (bf16[128,2048]{1,0:T(8,128)(2,1)S(1)}, bf16[128,2048]{1,0:T(8,128)(2,1)}, u32[]{:S(2)}, u32[]{:S(2)}) collective-permute-start(bf16[128,2048]{1,0:T(8,128)(2,1)S(1)} %constant_dynamic-update-slice_fusion.4.b0), channel_id=1, source_target_pairs={{0,1},{1,0},{2,3},{3,2},{4,5},{5,4},{6,7},{7,6},{8,9},{9,8},{10,11... | collective-permute-start | bytes 1572872 | tf_op jit(solution)/shard_map/ppermute | solution.py:231
  54.6 3.1 %collective-permute-start.12 = (bf16[128,2048]{1,0:T(8,128)(2,1)S(1)}, bf16[128,2048]{1,0:T(8,128)(2,1)}, u32[]{:S(2)}, u32[]{:S(2)}) collective-permute-start(bf16[128,2048]{1,0:T(8,128)(2,1)S(1)} %collective-permute-done.10.b1), channel_id=1, source_target_pairs={{0,1},{1,0},{2,3},{3,2},{4,5},{5,4},{6,7},{7,6},{8,9},{9,8},{10,11... | collective-permute-start | bytes 1572872 | tf_op jit(solution)/shard_map/ppermute | solution.py:231
  77.5 2.7 %collective-permute-start.13 = (bf16[256,2048]{1,0:T(8,128)(2,1)S(1)}, bf16[256,2048]{1,0:T(8,128)(2,1)S(1)}, u32[]{:S(2)}, u32[]{:S(2)}) collective-permute-start(bf16[256,2048]{1,0:T(8,128)(2,1)S(1)} %get-tuple-element.21), channel_id=1, source_target_pairs={{0,1},{1,0},{2,3},{3,2},{4,5},{5,4},{6,7},{7,6},{8,9},{9,8},{10,11... | collective-permute-start | bytes 3145736 | tf_op jit(solution)/shard_map/ppermute | solution.py:231
  77.7 4.2 %collective-permute-start.19 = (bf16[256,2048]{1,0:T(8,128)(2,1)S(1)}, bf16[256,2048]{1,0:T(8,128)(2,1)S(1)}, u32[]{:S(2)}, u32[]{:S(2)}) collective-permute-start(bf16[256,2048]{1,0:T(8,128)(2,1)S(1)} %get-tuple-element.26), channel_id=1, source_target_pairs={{0,1},{1,0},{2,3},{3,2},{4,5},{5,4},{6,7},{7,6},{8,9},{9,8},{10,11... | collective-permute-start | bytes 3145736 | tf_op jit(solution)/shard_map/ppermute | solution.py:231
  80.4 14.0 %collective-permute-start.14 = (bf16[128,2048]{1,0:T(8,128)(2,1)S(1)}, bf16[128,2048]{1,0:T(8,128)(2,1)S(1)}, u32[]{:S(2)}, u32[]{:S(2)}) collective-permute-start(bf16[128,2048]{1,0:T(8,128)(2,1)S(1)} %add_convert_fusion.3), channel_id=1, source_target_pairs={{0,2},{2,0},{1,3},{3,1},{4,6},{6,4},{5,7},{7,5},{8,10},{10,8},{9,1... | collective-permute-start | bytes 1572872 | tf_op jit(solution)/shard_map/ppermute | solution.py:235
  82.1 13.8 %collective-permute-start.20 = (bf16[128,2048]{1,0:T(8,128)(2,1)S(1)}, bf16[128,2048]{1,0:T(8,128)(2,1)S(1)}, u32[]{:S(2)}, u32[]{:S(2)}) collective-permute-start(bf16[128,2048]{1,0:T(8,128)(2,1)S(1)} %add_convert_fusion.1), channel_id=1, source_target_pairs={{0,4},{4,0},{1,5},{5,1},{2,6},{6,2},{3,7},{7,3},{8,12},{12,8},{9,1... | collective-permute-start | bytes 1572872 | tf_op jit(solution)/shard_map/ppermute | solution.py:239
  96.1 7.4 %collective-permute-start.21 = (bf16[64,2048]{1,0:T(8,128)(2,1)S(1)}, bf16[64,2048]{1,0:T(8,128)(2,1)S(1)}, u32[]{:S(2)}, u32[]{:S(2)}) collective-permute-start(bf16[64,2048]{1,0:T(8,128)(2,1)S(1)} %add_convert_fusion.4), channel_id=1, source_target_pairs={{0,2},{2,0},{1,3},{3,1},{4,6},{6,4},{5,7},{7,5},{8,10},{10,8},{9,1... | collective-permute-start | bytes 786440 | tf_op jit(solution)/shard_map/ppermute | solution.py:235
  97.9 7.3 %collective-permute-start.15 = (bf16[64,2048]{1,0:T(8,128)(2,1)S(1)}, bf16[64,2048]{1,0:T(8,128)(2,1)S(1)}, u32[]{:S(2)}, u32[]{:S(2)}) collective-permute-start(bf16[64,2048]{1,0:T(8,128)(2,1)S(1)} %add_convert_fusion.6), channel_id=1, source_target_pairs={{0,4},{4,0},{1,5},{5,1},{2,6},{6,2},{3,7},{7,3},{8,12},{12,8},{9,1... | collective-permute-start | bytes 786440 | tf_op jit(solution)/shard_map/ppermute | solution.py:239
  103.7 6.1 %collective-permute-start.22 = (bf16[32,2048]{1,0:T(8,128)(2,1)S(1)}, bf16[32,2048]{1,0:T(8,128)(2,1)S(1)}, u32[]{:S(2)}, u32[]{:S(2)}) collective-permute-start(bf16[32,2048]{1,0:T(8,128)(2,1)S(1)} %pad_maximum_fusion.3), channel_id=1, source_target_pairs={{0,8},{8,0},{16,24},{24,16},{1,9},{9,1},{17,25},{25,17},{2,10},{10... | collective-permute-start | bytes 393224 | tf_op jit(solution)/shard_map/ppermute | solution.py:243
  105.4 5.5 %collective-permute-start.16 = (bf16[16,2048]{1,0:T(8,128)(2,1)S(1)}, bf16[16,2048]{1,0:T(8,128)(2,1)S(1)}, u32[]{:S(2)}, u32[]{:S(2)}) collective-permute-start(bf16[16,2048]{1,0:T(8,128)(2,1)S(1)} %get-tuple-element.37), channel_id=1, source_target_pairs={{0,8},{8,0},{16,24},{24,16},{1,9},{9,1},{17,25},{25,17},{2,10},{10... | collective-permute-start | bytes 196616 | tf_op jit(solution)/shard_map/ppermute | solution.py:243
  105.9 6.1 %collective-permute-start.18 = (bf16[16,2048]{1,0:T(8,128)(2,1)S(1)}, bf16[16,2048]{1,0:T(8,128)(2,1)S(1)}, u32[]{:S(2)}, u32[]{:S(2)}) collective-permute-start(bf16[16,2048]{1,0:T(8,128)(2,1)S(1)} %get-tuple-element.38), channel_id=1, source_target_pairs={{0,24},{8,16},{16,8},{24,0},{1,25},{9,17},{17,9},{25,1},{2,26},{10... | collective-permute-start | bytes 196616 | tf_op jit(solution)/shard_map/ppermute | solution.py:243
  107.8 7.6 %collective-permute-start.17 = (bf16[16,2048]{1,0:T(8,128)(2,1)S(1)}, bf16[16,2048]{1,0:T(8,128)(2,1)S(1)}, u32[]{:S(2)}, u32[]{:S(2)}) collective-permute-start(bf16[16,2048]{1,0:T(8,128)(2,1)S(1)} %get-tuple-element.39), channel_id=1, source_target_pairs={{0,16},{8,24},{16,0},{24,8},{1,17},{9,25},{17,1},{25,9},{2,18},{10... | collective-permute-start | bytes 196616 | tf_op jit(solution)/shard_map/ppermute | solution.py:243
  109.8 6.2 %collective-permute-start.23 = (bf16[16,2048]{1,0:T(8,128)(2,1)S(1)}, bf16[16,2048]{1,0:T(8,128)(2,1)S(1)}, u32[]{:S(2)}, u32[]{:S(2)}) collective-permute-start(bf16[16,2048]{1,0:T(8,128)(2,1)S(1)} %fusion.4), channel_id=1, source_target_pairs={{0,16},{8,24},{16,0},{24,8},{1,17},{9,25},{17,1},{25,9},{2,18},{10... | collective-permute-start | bytes 196616 | tf_op jit(solution)/shard_map/ppermute | solution.py:243

commit v5 on v4

--- a/solution.py
+++ b/solution.py
@@ -275,7 +275,7 @@
     parts.append(jnp.zeros((128 - 3 * experts, count), jnp.float32))
     parts = jnp.concatenate(parts, axis=0)
     parts = jnp.concatenate([parts, jnp.zeros((128, 128 - count), jnp.float32)], axis=1)
-    notes[...] = parts.T[0:count, :].astype(jnp.bfloat16)
+    notes[...] = parts.T[0:count, :]
 
 
 def attend_kernel(
@@ -392,7 +392,7 @@
     singles = SINGLES * (q.shape[1] // HD)
     return pl.pallas_call(
         attend_kernel,
-        out_shape=(half, half, jax.ShapeDtypeStruct((chosen.shape[1], 128), jnp.bfloat16)),
+        out_shape=(half, half, jax.ShapeDtypeStruct((chosen.shape[1], 128), jnp.float32)),
         in_specs=[smem] * 5 + [vmem] * 2 + [hbm] * 6,
         out_specs=(vmem,) * 3,
         scratch_shapes=[
@@ -423,11 +423,11 @@
 
 def experts_kernel(
     place, favored, a0, a1, a2, a3, b0, b1, b2, b3, gate, up, down,
-    a_keep, a_send, b_keep, b_send,
+    a_keep_near, a_keep_far, a_send_near, a_send_far, b_keep_near, b_keep_far, b_send_near, b_send_far,
     tokens, ring, pick, spread, scale, taken, act, in_sems, w_sems,
 ):
     count, hidden = tokens.shape[0], act.shape[1]
-    half = a_keep.shape[1]
+    half = a_keep_near.shape[1]
     notes_at = half
     tile = taken.shape[0] // 5
     spans = slot_spans(tile)
@@ -516,17 +516,15 @@
             o = dot_nn(act[row : row + rows, :], ring[2 * s * hidden : (2 * s + 1) * hidden, start : start + 1024])
             made[row : row + rows, start : start + 1024] = (o * part).astype(jnp.bfloat16)
 
-    rows = count // 2
-    for i, outs in enumerate(((a_keep, a_send), (b_keep, b_send))):
+    outs_a = (a_keep_near, a_keep_far, a_send_near, a_send_far)
+    outs_b = (b_keep_near, b_keep_far, b_send_near, b_send_far)
+    for i, outs in enumerate((outs_a, outs_b)):
         for at in range(0, half, 512):
             y = dot_nn(spread[...], made[:, i * half + at : i * half + at + 512]).astype(jnp.bfloat16)
-            for side, out in enumerate(outs):
-                if i == 0:
-                    out[:, at : at + 512] = y[side * rows : (side + 1) * rows, :]
-                else:
-                    for j in range(4):
-                        to, row = (j % 2) * 2 + j // 2, side * rows + j * 64
-                        out[to * 64 : (to + 1) * 64, at : at + 512] = y[row : row + 64, :]
+            for j in range(8):
+                to = j if i == 0 else j // 4 * 4 + j % 2 * 2 + j // 2 % 2
+                rows = slice(to % 2 * 64, to % 2 * 64 + 64)
+                outs[to // 2][rows, at : at + 512] = y[j * 64 : (j + 1) * 64, :]
 
 
 def experts_call(place, favored, pieces_a, pieces_b, gate, up, down):
@@ -536,12 +534,12 @@
     rows, padded = 5 * tile, -(-5 * tile // 128) * 128
     half = width // 2
     smem, vmem, hbm = (pl.BlockSpec(memory_space=s) for s in (pltpu.SMEM, pltpu.VMEM, pl.ANY))
-    out = jax.ShapeDtypeStruct((count // 2, half), jnp.bfloat16)
+    out = jax.ShapeDtypeStruct((count // 4, half), jnp.bfloat16)
     return pl.pallas_call(
         experts_kernel,
-        out_shape=(out,) * 4,
+        out_shape=(out,) * 8,
         in_specs=[smem, smem] + [hbm] * 11,
-        out_specs=(vmem,) * 4,
+        out_specs=(vmem,) * 8,
         scratch_shapes=[
             pltpu.VMEM((count, width + 128), jnp.bfloat16),
             pltpu.VMEM((8 * hidden, width), jnp.bfloat16),
@@ -610,10 +608,12 @@
         attention_merge_matrix,
     )
     got = over_core(send)
+    keep, notes = lax.optimization_barrier((keep.astype(jnp.float32), notes.astype(jnp.bfloat16)))
+    skip = lax.optimization_barrier(skip_stream_entry.astype(jnp.float32))
     far = plus(got[0:count], keep[0:count])
     near = plus(got[count:], keep[count:])
     own_attn = over_y(far).astype(jnp.float32) + near.astype(jnp.float32)
-    stream = (skip_stream_entry.astype(jnp.float32) + own_attn).astype(jnp.bfloat16)
+    stream = (skip + own_attn).astype(jnp.bfloat16)
     wide = stream.astype(jnp.float32)
     squares = jnp.mean(wide * wide, axis=1, keepdims=True)
     normed = (wide * lax.rsqrt(squares + 1e-05) * premix_scale_factor.astype(jnp.float32)).astype(
@@ -624,7 +624,8 @@
     hot = jnp.where((hot >= 0) & (hot < own_experts), hot, -1).astype(jnp.int32)
 
     part = jnp.concatenate([normed[:, :half], notes, normed[:, half:]], axis=1)
-    column = [part, over_z(part, 1), over_z(part, 2), over_z(part, 3)]
+    third, second, first = over_z(part, 3), over_z(part, 2), over_z(part, 1)
+    column = [part, first, second, third]
     gathered = []
     for lanes, first, second in (
         (slice(0, half + 128), over_x, over_y),
@@ -634,22 +635,19 @@
         part = joined(part, first(part))
         other = second(part)
         gathered.append((part, other, over_core(part), over_core(other)))
-    a_keep, a_send, b_keep, b_send = experts_call(
+    outs = experts_call(
         x.astype(jnp.int32)[None], hot, *gathered, gating_matrices, expand_matrices, contract_matrices
     )
     results = []
-    for sent, kept, first, second in (
-        (a_send, a_keep, over_y, over_x),
-        (b_send, b_keep, over_x, over_y),
+    for (keep_near, keep_far, send_near, send_far), first, second in (
+        (outs[:4], over_y, over_x),
+        (outs[4:], over_x, over_y),
     ):
-        got = over_core(sent)
-        rows = kept.shape[0] // 2
-        from_first, got, kept = lax.optimization_barrier((first(plus(got[rows:], kept[rows:])), got, kept))
-        rows = rows // 2
-        near = plus(got[: 2 * rows], kept[: 2 * rows])
-        got = second(plus(from_first[rows:], near[rows:]))
-        near = plus(from_first[:rows], near[:rows])
-        results.append(near.astype(jnp.float32) + got.astype(jnp.float32))
+        far = first(plus(over_core(send_far), keep_far))
+        near = plus(over_core(send_near), keep_near)
+        rows = near.shape[0] // 2
+        got = second(plus(far[rows:], near[rows:]))
+        results.append(plus(far[:rows], near[:rows]).astype(jnp.float32) + got.astype(jnp.float32))
     total_a, total_b = results
     sent = jnp.concatenate([total_b[count : 2 * count], total_b[3 * count :]], axis=0).astype(jnp.bfloat16)
     got = over_z(sent, 1).astype(jnp.float32)

time: 117 us -> 114 us (0.974)
  waiting for transfers between devices: 57.6 us -> 55.6 us
  other arithmetic: 6.66 us -> 5.3 us
    ppermute x5, waiting for transfers between devices: 27.9 us -> 17.1 us  [over_y(): return lax.ppermute(a, 'tensor', PAIRS_Y)]
    ppermute x4, waiting for transfers between devices: 7.48 us -> 17.4 us  [over_x(): return lax.ppermute(a, 'expert', PAIRS_X)]
    ppermute x7 -> x9, waiting for transfers between devices: 6.6 us -> 3.97 us  [over_core(): return lax.ppermute(a, 'tensor', PAIRS_CORE)]
    convert_element_type x0 -> x3, other arithmetic: none -> 2.61 us  [the longest x1 0.98 us: local_fast(): keep.astype(jnp.float32)]
    ppermute x8, waiting for transfers between devices: 15.6 us -> 17.1 us  [over_z(): return lax.ppermute(a, 'dp', [(i, i ^ k) for i in range(4)])]
  transfers between devices with their start and end apart: 24 -> 26, of which waited for: 18 -> 15; matrix products, arithmetic and copies ran while one was open for 2% -> 4% of each run, Pallas kernels for 0% -> 0%
where the time goes in v5:
time: 114 us; the launch traced here: 113 us
  waiting for transfers between devices  55.6 us (49%)
  Pallas kernels  25.7 us (23%)
  starting transfers between devices  25.7 us (23%)
  other arithmetic  5.3 us (5%)
    pallas_call x1, Pallas kernels, experts_call(): pl.pallas_call(experts_kernel, out_shape=(out,) * 8, in_specs=[smem, smem...  20.1 us
    ppermute x4, waiting for transfers between devices, over_x(): return lax.ppermute(a, 'expert', PAIRS_X)  17.4 us
    ppermute x8, waiting for transfers between devices, over_z(): return lax.ppermute(a, 'dp', [(i, i ^ k) for i in range(4)])  17.1 us
    ppermute x5, waiting for transfers between devices, over_y(): return lax.ppermute(a, 'tensor', PAIRS_Y)  17.1 us
    ppermute x8, starting transfers between devices, over_z(): return lax.ppermute(a, 'dp', [(i, i ^ k) for i in range(4)])  9.35 us
    ppermute x5, starting transfers between devices, over_y(): return lax.ppermute(a, 'tensor', PAIRS_Y)  8.27 us
    ppermute x4, starting transfers between devices, over_x(): return lax.ppermute(a, 'expert', PAIRS_X)  5.98 us
    pallas_call x1, Pallas kernels, attention_call(): pl.pallas_call(attend_kernel, out_shape=(half, half, jax.ShapeDtypeStruct...  5.58 us
  transfers between devices with their start and end apart: 26, of which 15 were waited for; matrix products, arithmetic and copies ran while one was open for 4% of the time, Pallas kernels for 0%

profile of v5, /device:TPU:0, one launch (start us, length us, event | category | flops | bytes accessed | tf_op | source)
XLA Modules:
  0.0 113.3 jit_solution(9148051499109161276)
XLA Ops:
  0.7 5.6 %attention.1 = (bf16[32,4096]{1,0:T(8,128)(2,1)}, bf16[32,4096]{1,0:T(8,128)(2,1)}, f32[16,128]{1,0:T(8,128)}) custom-call(s32[1]{0:T(128)} %bitcast.place, s32[8,17]{1,0:T(8,128)} %bitcast.10, s32[17]{0:T(128)} %counts.1, s32[8]{0:T(128)} %allowed.1, s32[1]{0:T(128)S(6)} %copy.26.favored, s32[2,16]{1,0:T(2,128)} %bitcast.11, f32[2,16]{1,0:T(2,128)} %bitcast.12, ...), custom_call_target="tpu_custom_call" | custom-call | flops 1000000000 | bytes 8000000 | tf_op jit(solution)/shard_map/attention/pallas_call | solution.py:393
  6.2 0.5 collective-permute-start
  6.8 0.7 convert_element_type.151
  7.5 1.0 convert_element_type.150
  8.5 0.0 collective-permute-done
  8.5 2.6 %collective-permute-start.1 = (bf16[16,4096]{1,0:T(8,128)(2,1)S(1)}, bf16[16,4096]{1,0:T(8,128)(2,1)S(1)}, u32[]{:S(2)}, u32[]{:S(2)}) collective-permute-start(bf16[16,4096]{1,0:T(8,128)(2,1)S(1)} %add_convert_fusion.10), channel_id=1, source_target_pairs={{0,2},{2,0},{1,3},{3,1},{4,6},{6,4},{5,7},{7,5},{8,10},{10,8},{9,1... | collective-permute-start | bytes 393224 | tf_op jit(solution)/shard_map/ppermute | solution.py:235
  11.1 0.7 convert_element_type.159
  11.8 0.9 convert_element_type.148
  12.7 2.5 %collective-permute-done.1 = bf16[16,4096]{1,0:T(8,128)(2,1)S(1)} collective-permute-done((bf16[16,4096]{1,0:T(8,128)(2,1)S(1)}, bf16[16,4096]{1,0:T(8,128)(2,1)S(1)}, u32[]{:S(2)}, u32[]{:S(2)}) %collective-permute-start.1) | collective-permute-done | bytes 131104 | tf_op jit(solution)/shard_map/ppermute | solution.py:235
  15.2 0.2 fusion
  15.4 0.1 fusion.2
  15.6 3.9 %collective-permute-start.4 = (bf16[16,4224]{1,0:T(8,128)(2,1)S(1)}, bf16[16,4224]{1,0:T(8,128)(2,1)S(1)}, u32[]{:S(2)}, u32[]{:S(2)}) collective-permute-start(bf16[16,4224]{1,0:T(8,128)(2,1)S(1)} %pad_maximum_fusion.2), channel_id=1, source_target_pairs={{0,24},{8,16},{16,8},{24,0},{1,25},{9,17},{17,9},{25,1},{2,26},{10... | collective-permute-start | bytes 405512 | tf_op jit(solution)/shard_map/ppermute | solution.py:243
  19.5 0.0 collective-permute-start.3
  19.5 0.6 collective-permute-start.2
  20.1 7.9 %collective-permute-done.2 = bf16[16,4224]{1,0:T(8,128)(2,1)S(1)} collective-permute-done((bf16[16,4224]{1,0:T(8,128)(2,1)S(1)}, bf16[16,4224]{1,0:T(8,128)(2,1)S(1)}, u32[]{:S(2)}, u32[]{:S(2)}) %collective-permute-start.2) | collective-permute-done | bytes 135200 | tf_op jit(solution)/shard_map/ppermute | solution.py:243
  28.0 2.7 %collective-permute-done.3 = bf16[16,4224]{1,0:T(8,128)(2,1)S(1)} collective-permute-done((bf16[16,4224]{1,0:T(8,128)(2,1)S(1)}, bf16[16,4224]{1,0:T(8,128)(2,1)S(1)}, u32[]{:S(2)}, u32[]{:S(2)}) %collective-permute-start.3) | collective-permute-done | bytes 135200 | tf_op jit(solution)/shard_map/ppermute | solution.py:243
  30.8 1.6 %collective-permute-start.5 = (bf16[64,2176]{1,0:T(8,128)(2,1)S(1)}, bf16[64,2176]{1,0:T(8,128)(2,1)S(1)}, u32[]{:S(2)}, u32[]{:S(2)}) collective-permute-start(bf16[64,2176]{1,0:T(8,128)(2,1)S(1)} %pad_maximum_fusion), channel_id=1, source_target_pairs={{0,4},{4,0},{1,5},{5,1},{2,6},{6,2},{3,7},{7,3},{8,12},{12,8},{9,1... | collective-permute-start | bytes 835592 | tf_op jit(solution)/shard_map/ppermute | solution.py:239
  32.5 1.6 %collective-permute-start.9 = (bf16[64,2048]{1,0:T(8,128)(2,1)S(1)}, bf16[64,2048]{1,0:T(8,128)(2,1)S(1)}, u32[]{:S(2)}, u32[]{:S(2)}) collective-permute-start(bf16[64,2048]{1,0:T(8,128)(2,1)S(1)} %pad_maximum_fusion.1), channel_id=1, source_target_pairs={{0,2},{2,0},{1,3},{3,1},{4,6},{6,4},{5,7},{7,5},{8,10},{10,8},{9,1... | collective-permute-start | bytes 786440 | tf_op jit(solution)/shard_map/ppermute | solution.py:235
  34.0 4.5 %collective-permute-done.5 = bf16[64,2176]{1,0:T(8,128)(2,1)S(1)} collective-permute-done((bf16[64,2176]{1,0:T(8,128)(2,1)S(1)}, bf16[64,2176]{1,0:T(8,128)(2,1)S(1)}, u32[]{:S(2)}, u32[]{:S(2)}) %collective-permute-start.5) | collective-permute-done | bytes 278560 | tf_op jit(solution)/shard_map/ppermute | solution.py:239
  38.6 1.6 %collective-permute-start.6 = (bf16[128,2176]{1,0:T(8,128)(2,1)S(1)}, bf16[128,2176]{1,0:T(8,128)(2,1)S(1)}, u32[]{:S(2)}, u32[]{:S(2)}) collective-permute-start(bf16[128,2176]{1,0:T(8,128)(2,1)S(1)} %constant_dynamic-update-slice_fusion.a0), channel_id=1, source_target_pairs={{0,2},{2,0},{1,3},{3,1},{4,6},{6,4},{5,7},{7,5},{8,10},{10,8},{9,1... | collective-permute-start | bytes 1671176 | tf_op jit(solution)/shard_map/ppermute | solution.py:235
  40.2 0.0 collective-permute-done.9
  40.2 1.5 %collective-permute-start.10 = (bf16[128,2048]{1,0:T(8,128)(2,1)S(1)}, bf16[128,2048]{1,0:T(8,128)(2,1)S(1)}, u32[]{:S(2)}, u32[]{:S(2)}) collective-permute-start(bf16[128,2048]{1,0:T(8,128)(2,1)S(1)} %constant_dynamic-update-slice_fusion.4.b0), channel_id=1, source_target_pairs={{0,4},{4,0},{1,5},{5,1},{2,6},{6,2},{3,7},{7,3},{8,12},{12,8},{9,1... | collective-permute-start | bytes 1572872 | tf_op jit(solution)/shard_map/ppermute | solution.py:239
  41.8 9.8 %collective-permute-done.6.a1 = bf16[128,2176]{1,0:T(8,128)(2,1)S(1)} collective-permute-done((bf16[128,2176]{1,0:T(8,128)(2,1)S(1)}, bf16[128,2176]{1,0:T(8,128)(2,1)S(1)}, u32[]{:S(2)}, u32[]{:S(2)}) %collective-permute-start.6) | collective-permute-done | bytes 557088 | tf_op jit(solution)/shard_map/ppermute | solution.py:235
  51.5 0.0 collective-permute-start.8
  51.5 0.5 collective-permute-start.11
  52.0 0.0 collective-permute-done.10.b1
  52.0 0.0 collective-permute-start.12
  52.0 2.3 %collective-permute-done.11.b2 = bf16[128,2048]{1,0:T(8,128)(2,1)} collective-permute-done((bf16[128,2048]{1,0:T(8,128)(2,1)S(1)}, bf16[128,2048]{1,0:T(8,128)(2,1)}, u32[]{:S(2)}, u32[]{:S(2)}) %collective-permute-start.11) | collective-permute-done | bytes 524320 | tf_op jit(solution)/shard_map/ppermute | solution.py:231
  54.4 0.0 collective-permute-done.7.a2
  54.4 0.8 collective-permute-done.12.b3
  55.1 20.1 %experts.1 = (bf16[128,2048]{1,0:T(8,128)(2,1)S(1)}, bf16[128,2048]{1,0:T(8,128)(2,1)S(1)}, bf16[128,2048]{1,0:T(8,128)(2,1)S(1)}, bf16[128,2048]{1,0:T(8,128)(2...) custom-call(s32[1]{0:T(128)} %bitcast.6.place, ...), custom_call_target="tpu_custom_call" | custom-call | flops 5284823040 | bytes 44040192 | tf_op jit(solution)/shard_map/experts/pallas_call | solution.py:538
  75.2 0.2 collective-permute-start.13
  75.4 0.4 collective-permute-start.20
  75.8 0.1 collective-permute-start.15
  75.9 0.4 collective-permute-start.22
  76.3 0.9 collective-permute-done.13
  77.2 0.1 add_convert_fusion.3
  77.3 1.6 %collective-permute-start.14 = (bf16[128,2048]{1,0:T(8,128)(2,1)S(1)}, bf16[128,2048]{1,0:T(8,128)(2,1)S(1)}, u32[]{:S(2)}, u32[]{:S(2)}) collective-permute-start(bf16[128,2048]{1,0:T(8,128)(2,1)S(1)} %add_convert_fusion.3), channel_id=1, source_target_pairs={{0,2},{2,0},{1,3},{3,1},{4,6},{6,4},{5,7},{7,5},{8,10},{10,8},{9,1... | collective-permute-start | bytes 1572872 | tf_op jit(solution)/shard_map/ppermute | solution.py:235
  78.9 0.0 collective-permute-done.20
  78.9 0.1 add_convert_fusion.1
  79.1 1.4 %collective-permute-start.21 = (bf16[128,2048]{1,0:T(8,128)(2,1)S(1)}, bf16[128,2048]{1,0:T(8,128)(2,1)S(1)}, u32[]{:S(2)}, u32[]{:S(2)}) collective-permute-start(bf16[128,2048]{1,0:T(8,128)(2,1)S(1)} %add_convert_fusion.1), channel_id=1, source_target_pairs={{0,4},{4,0},{1,5},{5,1},{2,6},{6,2},{3,7},{7,3},{8,12},{12,8},{9,1... | collective-permute-start | bytes 1572872 | tf_op jit(solution)/shard_map/ppermute | solution.py:239
  80.5 0.0 collective-permute-done.15
  80.5 0.1 add_convert_fusion.2
  80.6 0.1 add_convert_fusion
  80.8 12.0 %collective-permute-done.21 = bf16[128,2048]{1,0:T(8,128)(2,1)S(1)} collective-permute-done((bf16[128,2048]{1,0:T(8,128)(2,1)S(1)}, bf16[128,2048]{1,0:T(8,128)(2,1)S(1)}, u32[]{:S(2)}, u32[]{:S(2)}) %collective-permute-start.21) | collective-permute-done | bytes 524320 | tf_op jit(solution)/shard_map/ppermute | solution.py:239
  92.8 0.1 add_convert_fusion.4
  92.9 0.9 collective-permute-start.23
  93.8 0.1 add_convert_fusion.6
  93.8 1.4 %collective-permute-start.16 = (bf16[64,2048]{1,0:T(8,128)(2,1)S(1)}, bf16[64,2048]{1,0:T(8,128)(2,1)S(1)}, u32[]{:S(2)}, u32[]{:S(2)}) collective-permute-start(bf16[64,2048]{1,0:T(8,128)(2,1)S(1)} %add_convert_fusion.6), channel_id=1, source_target_pairs={{0,4},{4,0},{1,5},{5,1},{2,6},{6,2},{3,7},{7,3},{8,12},{12,8},{9,1... | collective-permute-start | bytes 786440 | tf_op jit(solution)/shard_map/ppermute | solution.py:239
  95.3 4.9 %collective-permute-done.23 = bf16[64,2048]{1,0:T(8,128)(2,1)S(1)} collective-permute-done((bf16[64,2048]{1,0:T(8,128)(2,1)S(1)}, bf16[64,2048]{1,0:T(8,128)(2,1)S(1)}, u32[]{:S(2)}, u32[]{:S(2)}) %collective-permute-start.23) | collective-permute-done | bytes 262176 | tf_op jit(solution)/shard_map/ppermute | solution.py:235
  100.1 0.1 fusion.9
  100.3 0.1 collective-permute-start.24
  100.4 0.8 collective-permute-done.16
  101.1 0.1 fusion.8
  101.3 1.3 %collective-permute-start.17 = (bf16[16,2048]{1,0:T(8,128)(2,1)S(1)}, bf16[16,2048]{1,0:T(8,128)(2,1)S(1)}, u32[]{:S(2)}, u32[]{:S(2)}) collective-permute-start(bf16[16,2048]{1,0:T(8,128)(2,1)S(1)} %get-tuple-element.37), channel_id=1, source_target_pairs={{0,8},{8,0},{16,24},{24,16},{1,9},{9,1},{17,25},{25,17},{2,10},{10... | collective-permute-start | bytes 196616 | tf_op jit(solution)/shard_map/ppermute | solution.py:243
  102.6 2.1 %collective-permute-start.19 = (bf16[16,2048]{1,0:T(8,128)(2,1)S(1)}, bf16[16,2048]{1,0:T(8,128)(2,1)S(1)}, u32[]{:S(2)}, u32[]{:S(2)}) collective-permute-start(bf16[16,2048]{1,0:T(8,128)(2,1)S(1)} %get-tuple-element.38), channel_id=1, source_target_pairs={{0,24},{8,16},{16,8},{24,0},{1,25},{9,17},{17,9},{25,1},{2,26},{10... | collective-permute-start | bytes 196616 | tf_op jit(solution)/shard_map/ppermute | solution.py:243
  104.7 0.1 collective-permute-start.18
  104.8 1.7 %collective-permute-done.24 = bf16[32,2048]{1,0:T(8,128)(2,1)S(1)} collective-permute-done((bf16[32,2048]{1,0:T(8,128)(2,1)S(1)}, bf16[32,2048]{1,0:T(8,128)(2,1)S(1)}, u32[]{:S(2)}, u32[]{:S(2)}) %collective-permute-start.24) | collective-permute-done | bytes 131104 | tf_op jit(solution)/shard_map/ppermute | solution.py:243
  106.6 1.2 %collective-permute-start.25 = (bf16[16,2048]{1,0:T(8,128)(2,1)S(1)}, bf16[16,2048]{1,0:T(8,128)(2,1)S(1)}, u32[]{:S(2)}, u32[]{:S(2)}) collective-permute-start(bf16[16,2048]{1,0:T(8,128)(2,1)S(1)} %fusion.4), channel_id=1, source_target_pairs={{0,16},{8,24},{16,0},{24,8},{1,17},{9,25},{17,1},{25,9},{2,18},{10... | collective-permute-start | bytes 196616 | tf_op jit(solution)/shard_map/ppermute | solution.py:243
  107.8 0.0 collective-permute-done.17
  107.8 1.3 %collective-permute-done.19 = bf16[16,2048]{1,0:T(8,128)(2,1)S(1)} collective-permute-done((bf16[16,2048]{1,0:T(8,128)(2,1)S(1)}, bf16[16,2048]{1,0:T(8,128)(2,1)S(1)}, u32[]{:S(2)}, u32[]{:S(2)}) %collective-permute-start.19) | collective-permute-done | bytes 65568 | tf_op jit(solution)/shard_map/ppermute | solution.py:243
  109.1 2.9 %collective-permute-done.18 = bf16[16,2048]{1,0:T(8,128)(2,1)S(1)} collective-permute-done((bf16[16,2048]{1,0:T(8,128)(2,1)S(1)}, bf16[16,2048]{1,0:T(8,128)(2,1)S(1)}, u32[]{:S(2)}, u32[]{:S(2)}) %collective-permute-start.18) | collective-permute-done | bytes 65568 | tf_op jit(solution)/shard_map/ppermute | solution.py:243
  112.0 0.7 collective-permute-done.25
  112.7 0.7 fusion.3
  (27 shorter events, 0.4 us)
Async XLA Ops:
  6.2 2.2 %collective-permute-start = (bf16[32,4096]{1,0:T(8,128)(2,1)}, bf16[32,4096]{1,0:T(8,128)(2,1)S(1)}, u32[]{:S(2)}, u32[]{:S(2)}) collective-permute-start(bf16[32,4096]{1,0:T(8,128)(2,1)} %get-tuple-element.18), channel_id=1, source_target_pairs={{0,1},{1,0},{2,3},{3,2},{4,5},{5,4},{6,7},{7,6},{8,9},{9,8},{10,11... | collective-permute-start | bytes 786440 | tf_op jit(solution)/shard_map/ppermute | solution.py:231
  8.5 6.8 %collective-permute-start.1 = (bf16[16,4096]{1,0:T(8,128)(2,1)S(1)}, bf16[16,4096]{1,0:T(8,128)(2,1)S(1)}, u32[]{:S(2)}, u32[]{:S(2)}) collective-permute-start(bf16[16,4096]{1,0:T(8,128)(2,1)S(1)} %add_convert_fusion.10), channel_id=1, source_target_pairs={{0,2},{2,0},{1,3},{3,1},{4,6},{6,4},{5,7},{7,5},{8,10},{10,8},{9,1... | collective-permute-start | bytes 393224 | tf_op jit(solution)/shard_map/ppermute | solution.py:235
  15.6 15.2 %collective-permute-start.4 = (bf16[16,4224]{1,0:T(8,128)(2,1)S(1)}, bf16[16,4224]{1,0:T(8,128)(2,1)S(1)}, u32[]{:S(2)}, u32[]{:S(2)}) collective-permute-start(bf16[16,4224]{1,0:T(8,128)(2,1)S(1)} %pad_maximum_fusion.2), channel_id=1, source_target_pairs={{0,24},{8,16},{16,8},{24,0},{1,25},{9,17},{17,9},{25,1},{2,26},{10... | collective-permute-start | bytes 405512 | tf_op jit(solution)/shard_map/ppermute | solution.py:243
  19.5 11.3 %collective-permute-start.3 = (bf16[16,4224]{1,0:T(8,128)(2,1)S(1)}, bf16[16,4224]{1,0:T(8,128)(2,1)S(1)}, u32[]{:S(2)}, u32[]{:S(2)}) collective-permute-start(bf16[16,4224]{1,0:T(8,128)(2,1)S(1)} %pad_maximum_fusion.2), channel_id=1, source_target_pairs={{0,16},{8,24},{16,0},{24,8},{1,17},{9,25},{17,1},{25,9},{2,18},{10... | collective-permute-start | bytes 405512 | tf_op jit(solution)/shard_map/ppermute | solution.py:243
  19.5 8.5 %collective-permute-start.2 = (bf16[16,4224]{1,0:T(8,128)(2,1)S(1)}, bf16[16,4224]{1,0:T(8,128)(2,1)S(1)}, u32[]{:S(2)}, u32[]{:S(2)}) collective-permute-start(bf16[16,4224]{1,0:T(8,128)(2,1)S(1)} %pad_maximum_fusion.2), channel_id=1, source_target_pairs={{0,8},{8,0},{16,24},{24,16},{1,9},{9,1},{17,25},{25,17},{2,10},{10... | collective-permute-start | bytes 405512 | tf_op jit(solution)/shard_map/ppermute | solution.py:243
  30.8 7.8 %collective-permute-start.5 = (bf16[64,2176]{1,0:T(8,128)(2,1)S(1)}, bf16[64,2176]{1,0:T(8,128)(2,1)S(1)}, u32[]{:S(2)}, u32[]{:S(2)}) collective-permute-start(bf16[64,2176]{1,0:T(8,128)(2,1)S(1)} %pad_maximum_fusion), channel_id=1, source_target_pairs={{0,4},{4,0},{1,5},{5,1},{2,6},{6,2},{3,7},{7,3},{8,12},{12,8},{9,1... | collective-permute-start | bytes 835592 | tf_op jit(solution)/shard_map/ppermute | solution.py:239
  32.5 7.7 %collective-permute-start.9 = (bf16[64,2048]{1,0:T(8,128)(2,1)S(1)}, bf16[64,2048]{1,0:T(8,128)(2,1)S(1)}, u32[]{:S(2)}, u32[]{:S(2)}) collective-permute-start(bf16[64,2048]{1,0:T(8,128)(2,1)S(1)} %pad_maximum_fusion.1), channel_id=1, source_target_pairs={{0,2},{2,0},{1,3},{3,1},{4,6},{6,4},{5,7},{7,5},{8,10},{10,8},{9,1... | collective-permute-start | bytes 786440 | tf_op jit(solution)/shard_map/ppermute | solution.py:235
  38.6 12.9 %collective-permute-start.6 = (bf16[128,2176]{1,0:T(8,128)(2,1)S(1)}, bf16[128,2176]{1,0:T(8,128)(2,1)S(1)}, u32[]{:S(2)}, u32[]{:S(2)}) collective-permute-start(bf16[128,2176]{1,0:T(8,128)(2,1)S(1)} %constant_dynamic-update-slice_fusion.a0), channel_id=1, source_target_pairs={{0,2},{2,0},{1,3},{3,1},{4,6},{6,4},{5,7},{7,5},{8,10},{10,8},{9,1... | collective-permute-start | bytes 1671176 | tf_op jit(solution)/shard_map/ppermute | solution.py:235
  40.2 11.8 %collective-permute-start.10 = (bf16[128,2048]{1,0:T(8,128)(2,1)S(1)}, bf16[128,2048]{1,0:T(8,128)(2,1)S(1)}, u32[]{:S(2)}, u32[]{:S(2)}) collective-permute-start(bf16[128,2048]{1,0:T(8,128)(2,1)S(1)} %constant_dynamic-update-slice_fusion.4.b0), channel_id=1, source_target_pairs={{0,4},{4,0},{1,5},{5,1},{2,6},{6,2},{3,7},{7,3},{8,12},{12,8},{9,1... | collective-permute-start | bytes 1572872 | tf_op jit(solution)/shard_map/ppermute | solution.py:239
  41.8 12.6 %collective-permute-start.7 = (bf16[128,2176]{1,0:T(8,128)(2,1)S(1)}, bf16[128,2176]{1,0:T(8,128)(2,1)S(1)}, u32[]{:S(2)}, u32[]{:S(2)}) collective-permute-start(bf16[128,2176]{1,0:T(8,128)(2,1)S(1)} %constant_dynamic-update-slice_fusion.a0), channel_id=1, source_target_pairs={{0,1},{1,0},{2,3},{3,2},{4,5},{5,4},{6,7},{7,6},{8,9},{9,8},{10,11... | collective-permute-start | bytes 1671176 | tf_op jit(solution)/shard_map/ppermute | solution.py:231
  51.5 3.6 %collective-permute-start.8 = (bf16[128,2176]{1,0:T(8,128)(2,1)S(1)}, bf16[128,2176]{1,0:T(8,128)(2,1)S(1)}, u32[]{:S(2)}, u32[]{:S(2)}) collective-permute-start(bf16[128,2176]{1,0:T(8,128)(2,1)S(1)} %collective-permute-done.6.a1), channel_id=1, source_target_pairs={{0,1},{1,0},{2,3},{3,2},{4,5},{5,4},{6,7},{7,6},{8,9},{9,8},{10,11... | collective-permute-start | bytes 1671176 | tf_op jit(solution)/shard_map/ppermute | solution.py:231
  51.5 2.8 %collective-permute-start.11 = (bf16[128,2048]{1,0:T(8,128)(2,1)S(1)}, bf16[128,2048]{1,0:T(8,128)(2,1)}, u32[]{:S(2)}, u32[]{:S(2)}) collective-permute-start(bf16[128,2048]{1,0:T(8,128)(2,1)S(1)} %constant_dynamic-update-slice_fusion.4.b0), channel_id=1, source_target_pairs={{0,1},{1,0},{2,3},{3,2},{4,5},{5,4},{6,7},{7,6},{8,9},{9,8},{10,11... | collective-permute-start | bytes 1572872 | tf_op jit(solution)/shard_map/ppermute | solution.py:231
  52.0 3.1 %collective-permute-start.12 = (bf16[128,2048]{1,0:T(8,128)(2,1)S(1)}, bf16[128,2048]{1,0:T(8,128)(2,1)}, u32[]{:S(2)}, u32[]{:S(2)}) collective-permute-start(bf16[128,2048]{1,0:T(8,128)(2,1)S(1)} %collective-permute-done.10.b1), channel_id=1, source_target_pairs={{0,1},{1,0},{2,3},{3,2},{4,5},{5,4},{6,7},{7,6},{8,9},{9,8},{10,11... | collective-permute-start | bytes 1572872 | tf_op jit(solution)/shard_map/ppermute | solution.py:231
  75.2 2.0 %collective-permute-start.13 = (bf16[128,2048]{1,0:T(8,128)(2,1)S(1)}, bf16[128,2048]{1,0:T(8,128)(2,1)S(1)}, u32[]{:S(2)}, u32[]{:S(2)}) collective-permute-start(bf16[128,2048]{1,0:T(8,128)(2,1)S(1)} %get-tuple-element.23), channel_id=1, source_target_pairs={{0,1},{1,0},{2,3},{3,2},{4,5},{5,4},{6,7},{7,6},{8,9},{9,8},{10,11... | collective-permute-start | bytes 1572872 | tf_op jit(solution)/shard_map/ppermute | solution.py:231
  75.4 3.5 %collective-permute-start.20 = (bf16[128,2048]{1,0:T(8,128)(2,1)S(1)}, bf16[128,2048]{1,0:T(8,128)(2,1)S(1)}, u32[]{:S(2)}, u32[]{:S(2)}) collective-permute-start(bf16[128,2048]{1,0:T(8,128)(2,1)S(1)} %get-tuple-element.27), channel_id=1, source_target_pairs={{0,1},{1,0},{2,3},{3,2},{4,5},{5,4},{6,7},{7,6},{8,9},{9,8},{10,11... | collective-permute-start | bytes 1572872 | tf_op jit(solution)/shard_map/ppermute | solution.py:231
  75.8 4.7 %collective-permute-start.15 = (bf16[128,2048]{1,0:T(8,128)(2,1)S(1)}, bf16[128,2048]{1,0:T(8,128)(2,1)S(1)}, u32[]{:S(2)}, u32[]{:S(2)}) collective-permute-start(bf16[128,2048]{1,0:T(8,128)(2,1)S(1)} %get-tuple-element.25), channel_id=1, source_target_pairs={{0,1},{1,0},{2,3},{3,2},{4,5},{5,4},{6,7},{7,6},{8,9},{9,8},{10,11... | collective-permute-start | bytes 1572872 | tf_op jit(solution)/shard_map/ppermute | solution.py:231
  75.9 4.7 %collective-permute-start.22 = (bf16[128,2048]{1,0:T(8,128)(2,1)S(1)}, bf16[128,2048]{1,0:T(8,128)(2,1)S(1)}, u32[]{:S(2)}, u32[]{:S(2)}) collective-permute-start(bf16[128,2048]{1,0:T(8,128)(2,1)S(1)} %get-tuple-element.29), channel_id=1, source_target_pairs={{0,1},{1,0},{2,3},{3,2},{4,5},{5,4},{6,7},{7,6},{8,9},{9,8},{10,11... | collective-permute-start | bytes 1572872 | tf_op jit(solution)/shard_map/ppermute | solution.py:231
  77.3 16.4 %collective-permute-start.14 = (bf16[128,2048]{1,0:T(8,128)(2,1)S(1)}, bf16[128,2048]{1,0:T(8,128)(2,1)S(1)}, u32[]{:S(2)}, u32[]{:S(2)}) collective-permute-start(bf16[128,2048]{1,0:T(8,128)(2,1)S(1)} %add_convert_fusion.3), channel_id=1, source_target_pairs={{0,2},{2,0},{1,3},{3,1},{4,6},{6,4},{5,7},{7,5},{8,10},{10,8},{9,1... | collective-permute-start | bytes 1572872 | tf_op jit(solution)/shard_map/ppermute | solution.py:235
  79.1 13.8 %collective-permute-start.21 = (bf16[128,2048]{1,0:T(8,128)(2,1)S(1)}, bf16[128,2048]{1,0:T(8,128)(2,1)S(1)}, u32[]{:S(2)}, u32[]{:S(2)}) collective-permute-start(bf16[128,2048]{1,0:T(8,128)(2,1)S(1)} %add_convert_fusion.1), channel_id=1, source_target_pairs={{0,4},{4,0},{1,5},{5,1},{2,6},{6,2},{3,7},{7,3},{8,12},{12,8},{9,1... | collective-permute-start | bytes 1572872 | tf_op jit(solution)/shard_map/ppermute | solution.py:239
  92.9 7.3 %collective-permute-start.23 = (bf16[64,2048]{1,0:T(8,128)(2,1)S(1)}, bf16[64,2048]{1,0:T(8,128)(2,1)S(1)}, u32[]{:S(2)}, u32[]{:S(2)}) collective-permute-start(bf16[64,2048]{1,0:T(8,128)(2,1)S(1)} %add_convert_fusion.4), channel_id=1, source_target_pairs={{0,2},{2,0},{1,3},{3,1},{4,6},{6,4},{5,7},{7,5},{8,10},{10,8},{9,1... | collective-permute-start | bytes 786440 | tf_op jit(solution)/shard_map/ppermute | solution.py:235
  93.8 7.3 %collective-permute-start.16 = (bf16[64,2048]{1,0:T(8,128)(2,1)S(1)}, bf16[64,2048]{1,0:T(8,128)(2,1)S(1)}, u32[]{:S(2)}, u32[]{:S(2)}) collective-permute-start(bf16[64,2048]{1,0:T(8,128)(2,1)S(1)} %add_convert_fusion.6), channel_id=1, source_target_pairs={{0,4},{4,0},{1,5},{5,1},{2,6},{6,2},{3,7},{7,3},{8,12},{12,8},{9,1... | collective-permute-start | bytes 786440 | tf_op jit(solution)/shard_map/ppermute | solution.py:239
  100.3 6.2 %collective-permute-start.24 = (bf16[32,2048]{1,0:T(8,128)(2,1)S(1)}, bf16[32,2048]{1,0:T(8,128)(2,1)S(1)}, u32[]{:S(2)}, u32[]{:S(2)}) collective-permute-start(bf16[32,2048]{1,0:T(8,128)(2,1)S(1)} %pad_maximum_fusion.3), channel_id=1, source_target_pairs={{0,8},{8,0},{16,24},{24,16},{1,9},{9,1},{17,25},{25,17},{2,10},{10... | collective-permute-start | bytes 393224 | tf_op jit(solution)/shard_map/ppermute | solution.py:243
  101.3 6.5 %collective-permute-start.17 = (bf16[16,2048]{1,0:T(8,128)(2,1)S(1)}, bf16[16,2048]{1,0:T(8,128)(2,1)S(1)}, u32[]{:S(2)}, u32[]{:S(2)}) collective-permute-start(bf16[16,2048]{1,0:T(8,128)(2,1)S(1)} %get-tuple-element.37), channel_id=1, source_target_pairs={{0,8},{8,0},{16,24},{24,16},{1,9},{9,1},{17,25},{25,17},{2,10},{10... | collective-permute-start | bytes 196616 | tf_op jit(solution)/shard_map/ppermute | solution.py:243
  102.6 6.5 %collective-permute-start.19 = (bf16[16,2048]{1,0:T(8,128)(2,1)S(1)}, bf16[16,2048]{1,0:T(8,128)(2,1)S(1)}, u32[]{:S(2)}, u32[]{:S(2)}) collective-permute-start(bf16[16,2048]{1,0:T(8,128)(2,1)S(1)} %get-tuple-element.38), channel_id=1, source_target_pairs={{0,24},{8,16},{16,8},{24,0},{1,25},{9,17},{17,9},{25,1},{2,26},{10... | collective-permute-start | bytes 196616 | tf_op jit(solution)/shard_map/ppermute | solution.py:243
  104.7 7.2 %collective-permute-start.18 = (bf16[16,2048]{1,0:T(8,128)(2,1)S(1)}, bf16[16,2048]{1,0:T(8,128)(2,1)S(1)}, u32[]{:S(2)}, u32[]{:S(2)}) collective-permute-start(bf16[16,2048]{1,0:T(8,128)(2,1)S(1)} %get-tuple-element.39), channel_id=1, source_target_pairs={{0,16},{8,24},{16,0},{24,8},{1,17},{9,25},{17,1},{25,9},{2,18},{10... | collective-permute-start | bytes 196616 | tf_op jit(solution)/shard_map/ppermute | solution.py:243
  106.6 6.1 %collective-permute-start.25 = (bf16[16,2048]{1,0:T(8,128)(2,1)S(1)}, bf16[16,2048]{1,0:T(8,128)(2,1)S(1)}, u32[]{:S(2)}, u32[]{:S(2)}) collective-permute-start(bf16[16,2048]{1,0:T(8,128)(2,1)S(1)} %fusion.4), channel_id=1, source_target_pairs={{0,16},{8,24},{16,0},{24,8},{1,17},{9,25},{17,1},{25,9},{2,18},{10... | collective-permute-start | bytes 196616 | tf_op jit(solution)/shard_map/ppermute | solution.py:243

commit v6 on v5

--- a/solution.py
+++ b/solution.py
@@ -383,6 +383,10 @@
         part = dot_nn(ordered[...], w_out[:, start : start + 512]).astype(jnp.bfloat16)
         send[:, start : start + 512] = part[0:32, :]
         keep[:, start : start + 512] = part[32:64, :]
+
+
+def in_hbm(array):
+    return pltpu.with_memory_space_constraint(array, pltpu.HBM)
 
 
 def attention_call(place, table, counts, allowed, favored, chosen, shares, q, k_new, v_new, k_pool, v_pool, w_out):
@@ -434,28 +438,28 @@
     first = jnp.maximum(favored[0], 0)
     expert_of = [first] + [jnp.where(s - 1 < first, s - 1, s) for s in (1, 2, 3)]
 
+    def fetch(matrix, s, slot):
+        rows = ring.at[slot * hidden : (slot + 1) * hidden, :]
+        return pltpu.make_async_copy(matrix.at[expert_of[s]], rows, w_sems.at[slot])
+
+    def fetch_inner(s):
+        fetch(gate, s, 2 * s).start()
+        fetch(up, s, 2 * s + 1).start()
+
     loads = []
-    for i, ref in enumerate((a0, a1, a2, a3)):
-        loads.append((ref, tokens.at[i * 128 : (i + 1) * 128, 0 : half + 128]))
     for i, ref in enumerate((b0, b1, b2, b3)):
         for j in range(2):
             row = (i // 2) * 256 + j * 128 + (i % 2) * 64
-            loads.append((ref.at[j * 64 : (j + 1) * 64, :], tokens.at[row : row + 64, half + 128 :]))
-    loads = [pltpu.make_async_copy(src, dst, in_sems.at[i]) for i, (src, dst) in enumerate(loads)]
-    for load in loads:
-        load.start()
-
-    def fetch(matrix, s, slot):
-        rows = ring.at[slot * hidden : (slot + 1) * hidden, :]
-        return pltpu.make_async_copy(matrix.at[expert_of[s]], rows, w_sems.at[slot])
-
-    def fetch_inner(s):
-        fetch(gate, s, 2 * s).start()
-        fetch(up, s, 2 * s + 1).start()
-
-    for load in loads[:4]:
-        load.wait()
+            rows = tokens.at[row : row + 64, half + 128 :]
+            loads.append(
+                pltpu.make_async_copy(ref.at[j * 64 : (j + 1) * 64, :], rows, in_sems.at[len(loads)])
+            )
+            loads[-1].start()
     fetch_inner(0)
+    fetch_inner(1)
+    for i, ref in enumerate((a0, a1, a2, a3)):
+        tokens[i * 128 : (i + 1) * 128, 0 : half + 128] = ref[...]
+
     notes = tokens[:, notes_at : notes_at + 128]
     width = notes.shape[1]
     source = lax.broadcasted_iota(jnp.int32, (width, width), 0)
@@ -464,39 +468,56 @@
     wanted = (source < 24) & (target < 4) & (lax.rem(source, 8) == place[0] * 4 + expert)
     share = dot_nn(notes, jnp.where(wanted, 1.0, 0.0).astype(jnp.bfloat16))
     kept = jnp.where(share > 0.0, 1.0, 0.0)
-    below = lax.broadcasted_iota(jnp.int32, (count, count), 1) < lax.broadcasted_iota(
-        jnp.int32, (count, count), 0
-    )
-    rank = dot_nn(jnp.where(below, 1.0, 0.0).astype(jnp.bfloat16), kept.astype(jnp.bfloat16))
-    spot = jnp.where(kept > 0.0, rank, -1000.0)
-    spot_t = spot.T
+    side = count // 2
+    side_rows = 5 * tile // 2
+    below = lax.broadcasted_iota(jnp.int32, (side, side), 1) < lax.broadcasted_iota(
+        jnp.int32, (side, side), 0
+    )
+    below = jnp.where(below, 1.0, 0.0).astype(jnp.bfloat16)
     lane = lax.broadcasted_iota(jnp.int32, (1, width), 1)
-    for s, (row, rows) in enumerate(spans):
-        ids = lax.broadcasted_iota(jnp.int32, (rows, count), 0).astype(jnp.float32)
-        picked = jnp.where(ids == spot_t[s : s + 1, :], 1.0, 0.0).astype(jnp.bfloat16)
-        pick[row : row + rows, :] = picked
-        found = dot_nn(picked, notes)
-        mine = (lane < 24) & (lax.rem(lane, 8) == place[0] * 4 + expert_of[s])
-        part = jnp.sum(jnp.where(mine, found, 0.0), axis=1, keepdims=True)
-        scale[row : row + rows, :] = jnp.broadcast_to(part, (rows, width))
-    for block in range(spread.shape[1] // 128):
-        ids = (lax.broadcasted_iota(jnp.int32, (count, 128), 1) + block * 128).astype(jnp.float32)
-        total = jnp.zeros((count, 128), jnp.float32)
+    for h in range(2):
+        here = slice(h * side, (h + 1) * side)
+        rank = dot_nn(below, kept[here].astype(jnp.bfloat16))
+        spot = jnp.where(kept[here] > 0.0, rank, -1000.0)
+        spot_t = spot.T
         for s, (row, rows) in enumerate(spans):
-            if row < (block + 1) * 128 and row + rows > block * 128:
-                total = total + jnp.where(ids == spot[:, s : s + 1] + row, 1.0, 0.0)
-        spread[:, block * 128 : (block + 1) * 128] = total.astype(jnp.bfloat16)
-    fetch_inner(1)
-    for load in loads[4:]:
+            size, at = rows // 2, h * side_rows + row // 2
+            ids = lax.broadcasted_iota(jnp.int32, (size, side), 0).astype(jnp.float32)
+            picked = jnp.where(ids == spot_t[s : s + 1, :], 1.0, 0.0).astype(jnp.bfloat16)
+            pick[at : at + size, :] = picked
+            found = dot_nn(picked, notes[here])
+            mine = (lane < 24) & (lax.rem(lane, 8) == place[0] * 4 + expert_of[s])
+            part = jnp.sum(jnp.where(mine, found, 0.0), axis=1, keepdims=True)
+            scale[row + h * size : row + (h + 1) * size, :] = jnp.broadcast_to(part, (size, width))
+        for block in range(spread.shape[1] // 128):
+            ids = (lax.broadcasted_iota(jnp.int32, (side, 128), 1) + block * 128).astype(jnp.float32)
+            total = jnp.zeros((side, 128), jnp.float32)
+            for s, (row, rows) in enumerate(spans):
+                if row // 2 < (block + 1) * 128 and (row + rows) // 2 > block * 128:
+                    total = total + jnp.where(ids == spot[:, s : s + 1] + row // 2, 1.0, 0.0)
+            spread[here, block * 128 : (block + 1) * 128] = total.astype(jnp.bfloat16)
+
+    fetch_inner(2)
+    for load in loads:
         load.wait()
 
     for start in range(0, 2 * half, 512):
         at = start if start < half else start + 128
-        taken[:, start : start + 512] = dot_nn(pick[...], tokens[:, at : at + 512]).astype(jnp.bfloat16)
-
-    fetch_inner(2)
+        for h in range(2):
+            found = dot_nn(
+                pick[h * side_rows : (h + 1) * side_rows, :], tokens[h * side : (h + 1) * side, at : at + 512]
+            ).astype(jnp.bfloat16)
+            for row, rows in spans:
+                size = rows // 2
+                taken[row + h * size : row + (h + 1) * size, start : start + 512] = found[
+                    row // 2 : row // 2 + size, :
+                ]
+
+    fetch_inner(3)
     made = tokens
-    made[5 * tile :, :] = jnp.zeros_like(made[5 * tile :, :])
+    for h in range(2):
+        rest = slice(h * side + side_rows, (h + 1) * side)
+        made[rest, :] = jnp.zeros_like(made[rest, :])
     for s, (row, rows) in enumerate(spans):
         x = taken[row : row + rows, :]
         fetch(gate, s, 2 * s).wait()
@@ -504,51 +525,56 @@
         fetch(up, s, 2 * s + 1).wait()
         u = dot_nt(x, ring[(2 * s + 1) * hidden : (2 * s + 2) * hidden, :])
         act[row : row + rows, :] = (g / (1.0 + jnp.exp(-g)) * u).astype(jnp.bfloat16)
-        if s == 0:
-            fetch_inner(3)
-        for later in ((), (0,), (1, 2), (3,))[s]:
-            fetch(down, later, 2 * later).start()
+        for later in (2 * s, 2 * s + 1):
+            if later < 4:
+                fetch(down, later, later).start()
 
     for s, (row, rows) in enumerate(spans):
-        fetch(down, s, 2 * s).wait()
+        fetch(down, s, s).wait()
         part = scale[row : row + rows, 0:1]
         for start in range(0, 2 * half, 1024):
-            o = dot_nn(act[row : row + rows, :], ring[2 * s * hidden : (2 * s + 1) * hidden, start : start + 1024])
-            made[row : row + rows, start : start + 1024] = (o * part).astype(jnp.bfloat16)
+            o = dot_nn(act[row : row + rows, :], ring[s * hidden : (s + 1) * hidden, start : start + 1024])
+            o = (o * part).astype(jnp.bfloat16)
+            size = rows // 2
+            for h in range(2):
+                at = h * side + row // 2
+                made[at : at + size, start : start + 1024] = o[h * size : (h + 1) * size, :]
 
     outs_a = (a_keep_near, a_keep_far, a_send_near, a_send_far)
     outs_b = (b_keep_near, b_keep_far, b_send_near, b_send_far)
     for i, outs in enumerate((outs_a, outs_b)):
         for at in range(0, half, 512):
-            y = dot_nn(spread[...], made[:, i * half + at : i * half + at + 512]).astype(jnp.bfloat16)
-            for j in range(8):
-                to = j if i == 0 else j // 4 * 4 + j % 2 * 2 + j // 2 % 2
-                rows = slice(to % 2 * 64, to % 2 * 64 + 64)
-                outs[to // 2][rows, at : at + 512] = y[j * 64 : (j + 1) * 64, :]
+            for h in range(2):
+                here = slice(h * side, (h + 1) * side)
+                y = dot_nn(spread[here, :], made[here, i * half + at : i * half + at + 512]).astype(jnp.bfloat16)
+                for j in range(4):
+                    to = j if i == 0 else j % 2 * 2 + j // 2
+                    rows = slice(to % 2 * 64, to % 2 * 64 + 64)
+                    outs[h * 2 + to // 2][rows, at : at + 512] = y[j * 64 : (j + 1) * 64, :]
 
 
 def experts_call(place, favored, pieces_a, pieces_b, gate, up, down):
     _, hidden, width = gate.shape
     count = sum(piece.shape[0] for piece in pieces_a)
     tile = CAP_MOST * 32
-    rows, padded = 5 * tile, -(-5 * tile // 128) * 128
+    rows, padded = 5 * tile, -(-5 * tile // 256) * 128
     half = width // 2
     smem, vmem, hbm = (pl.BlockSpec(memory_space=s) for s in (pltpu.SMEM, pltpu.VMEM, pl.ANY))
     out = jax.ShapeDtypeStruct((count // 4, half), jnp.bfloat16)
     return pl.pallas_call(
         experts_kernel,
         out_shape=(out,) * 8,
-        in_specs=[smem, smem] + [hbm] * 11,
+        in_specs=[smem, smem] + [vmem] * 4 + [hbm] * 7,
         out_specs=(vmem,) * 8,
         scratch_shapes=[
             pltpu.VMEM((count, width + 128), jnp.bfloat16),
             pltpu.VMEM((8 * hidden, width), jnp.bfloat16),
-            pltpu.VMEM((rows, count), jnp.bfloat16),
+            pltpu.VMEM((rows, count // 2), jnp.bfloat16),
             pltpu.VMEM((count, padded), jnp.bfloat16),
             pltpu.VMEM((rows, 128), jnp.float32),
             pltpu.VMEM((rows, width), jnp.bfloat16),
             pltpu.VMEM((rows, hidden), jnp.bfloat16),
-            pltpu.SemaphoreType.DMA((12,)),
+            pltpu.SemaphoreType.DMA((8,)),
             pltpu.SemaphoreType.DMA((8,)),
         ],
         compiler_params=pltpu.CompilerParams(vmem_limit_bytes=EXPERTS_MIB * MIB),
@@ -556,7 +582,7 @@
             flops=6 * rows * hidden * width, bytes_accessed=24 * hidden * width, transcendentals=rows * hidden
         ),
         name="experts",
-    )(place, favored, *pieces_a, *pieces_b, gate, up, down)
+    )(place, favored, *pieces_a, *pieces_b, *map(in_hbm, (gate, up, down)))
 
 
 def joined(*parts):
@@ -623,15 +649,14 @@
     hot = favored_specialist - x * own_experts
     hot = jnp.where((hot >= 0) & (hot < own_experts), hot, -1).astype(jnp.int32)
 
-    part = jnp.concatenate([normed[:, :half], notes, normed[:, half:]], axis=1)
-    third, second, first = over_z(part, 3), over_z(part, 2), over_z(part, 1)
-    column = [part, first, second, third]
+    part_a, part_b = jnp.concatenate([normed[:, :half], notes], axis=1), normed[:, half:]
+    second = over_z(part_b, 2)
+    third, middle, first = over_z(part_a, 3), over_z(part_a, 2), over_z(part_a, 1)
+    pairs = over_z(joined(part_b, second), 1)
+    part_a = joined(part_a, first, middle, third)
+    part_b = joined(part_b, pairs[:count], second, pairs[count:])
     gathered = []
-    for lanes, first, second in (
-        (slice(0, half + 128), over_x, over_y),
-        (slice(half + 128, None), over_y, over_x),
-    ):
-        part = joined(*[rows[:, lanes] for rows in column])
+    for part, first, second in ((part_a, over_x, over_y), (part_b, over_y, over_x)):
         part = joined(part, first(part))
         other = second(part)
         gathered.append((part, other, over_core(part), over_core(other)))

time: 114 us -> 110 us (0.965)
  waiting for transfers between devices: 55.6 us -> 44.5 us
  starting transfers between devices: 25.7 us -> 36.1 us
  Pallas kernels: 25.7 us -> 23.2 us
    ppermute x8 -> x10, waiting for transfers between devices: 17.1 us -> 6.67 us  [over_z(): return lax.ppermute(a, 'dp', [(i, i ^ k) for i in range(4)])]
    ppermute x8 -> x10, starting transfers between devices: 9.35 us -> 19.5 us  [over_z(): return lax.ppermute(a, 'dp', [(i, i ^ k) for i in range(4)])]
    pallas_call x1, Pallas kernels: 20.1 us -> 17.6 us  [experts_call(): pl.pallas_call(experts_kernel, out_shape=(out,) * 8, in_specs=[smem, smem...]
    ppermute x4, waiting for transfers between devices: 17.4 us -> 15.6 us  [over_x(): return lax.ppermute(a, 'expert', PAIRS_X)]
    ppermute x5, waiting for transfers between devices: 17.1 us -> 18.3 us  [over_y(): return lax.ppermute(a, 'tensor', PAIRS_Y)]
  transfers between devices with their start and end apart: 26 -> 28, of which waited for: 15 -> 15; matrix products, arithmetic and copies ran while one was open for 4% -> 4% of each run, Pallas kernels for 0% -> 0%
where the time goes in v6:
time: 110 us
  waiting for transfers between devices  44.5 us (40%)
  starting transfers between devices  36.1 us (33%)
  Pallas kernels  23.2 us (21%)
  other arithmetic  5.3 us (5%)
    ppermute x10, starting transfers between devices, over_z(): return lax.ppermute(a, 'dp', [(i, i ^ k) for i in range(4)])  19.5 us
    ppermute x5, waiting for transfers between devices, over_y(): return lax.ppermute(a, 'tensor', PAIRS_Y)  18.3 us
    pallas_call x1, Pallas kernels, experts_call(): pl.pallas_call(experts_kernel, out_shape=(out,) * 8, in_specs=[smem, smem...  17.6 us
    ppermute x4, waiting for transfers between devices, over_x(): return lax.ppermute(a, 'expert', PAIRS_X)  15.6 us
    ppermute x5, starting transfers between devices, over_y(): return lax.ppermute(a, 'tensor', PAIRS_Y)  8.27 us
    ppermute x10, waiting for transfers between devices, over_z(): return lax.ppermute(a, 'dp', [(i, i ^ k) for i in range(4)])  6.67 us
    ppermute x4, starting transfers between devices, over_x(): return lax.ppermute(a, 'expert', PAIRS_X)  6.21 us
    pallas_call x1, Pallas kernels, attention_call(): pl.pallas_call(attend_kernel, out_shape=(half, half, jax.ShapeDtypeStruct...  5.58 us
  transfers between devices with their start and end apart: 28, of which 15 were waited for; matrix products, arithmetic and copies ran while one was open for 4% of the time, Pallas kernels for 0%

profile of v6, /device:TPU:0, one launch (start us, length us, event | category | flops | bytes accessed | tf_op | source)
XLA Modules:
  0.0 110.2 jit_solution(5376993427977854151)
XLA Ops:
  0.7 5.6 %attention.1 = (bf16[32,4096]{1,0:T(8,128)(2,1)}, bf16[32,4096]{1,0:T(8,128)(2,1)}, f32[16,128]{1,0:T(8,128)}) custom-call(s32[1]{0:T(128)} %bitcast.place, s32[8,17]{1,0:T(8,128)} %bitcast.10, s32[17]{0:T(128)} %counts.1, s32[8]{0:T(128)} %allowed.1, s32[1]{0:T(128)S(6)} %copy.26.favored, s32[2,16]{1,0:T(2,128)} %bitcast.11, f32[2,16]{1,0:T(2,128)} %bitcast.12, ...), custom_call_target="tpu_custom_call" | custom-call | flops 1000000000 | bytes 8000000 | tf_op jit(solution)/shard_map/attention/pallas_call | solution.py:397
  6.2 0.5 collective-permute-start
  6.8 0.7 convert_element_type.151
  7.5 1.0 convert_element_type.150
  8.5 2.6 %collective-permute-start.1 = (bf16[16,4096]{1,0:T(8,128)(2,1)S(1)}, bf16[16,4096]{1,0:T(8,128)(2,1)S(1)}, u32[]{:S(2)}, u32[]{:S(2)}) collective-permute-start(bf16[16,4096]{1,0:T(8,128)(2,1)S(1)} %add_convert_fusion.10), channel_id=1, source_target_pairs={{0,2},{2,0},{1,3},{3,1},{4,6},{6,4},{5,7},{7,5},{8,10},{10,8},{9,1... | collective-permute-start | bytes 393224 | tf_op jit(solution)/shard_map/ppermute | solution.py:235
  11.1 0.7 convert_element_type.159
  11.8 0.9 convert_element_type.148
  12.7 2.5 %collective-permute-done.1 = bf16[16,4096]{1,0:T(8,128)(2,1)S(1)} collective-permute-done((bf16[16,4096]{1,0:T(8,128)(2,1)S(1)}, bf16[16,4096]{1,0:T(8,128)(2,1)S(1)}, u32[]{:S(2)}, u32[]{:S(2)}) %collective-permute-start.1) | collective-permute-done | bytes 131104 | tf_op jit(solution)/shard_map/ppermute | solution.py:235
  15.2 0.2 fusion
  15.4 0.1 fusion.2
  15.6 2.9 %collective-permute-start.9 = (bf16[16,2048]{1,0:T(8,128)(2,1)S(1)}, bf16[16,2048]{1,0:T(8,128)(2,1)S(1)}, u32[]{:S(2)}, u32[]{:S(2)}) collective-permute-start(bf16[16,2048]{1,0:T(8,128)(2,1)S(1)} %get-tuple-element.45), channel_id=1, source_target_pairs={{0,16},{8,24},{16,0},{24,8},{1,17},{9,25},{17,1},{25,9},{2,18},{10... | collective-permute-start | bytes 196616 | tf_op jit(solution)/shard_map/ppermute | solution.py:243
  18.4 0.2 collective-permute-start.3
  18.6 1.8 %collective-permute-start.2 = (bf16[16,2176]{1,0:T(8,128)(2,1)S(1)}, bf16[16,2176]{1,0:T(8,128)(2,1)S(1)}, u32[]{:S(2)}, u32[]{:S(2)}) collective-permute-start(bf16[16,2176]{1,0:T(8,128)(2,1)S(1)} %get-tuple-element.48), channel_id=1, source_target_pairs={{0,8},{8,0},{16,24},{24,16},{1,9},{9,1},{17,25},{25,17},{2,10},{10... | collective-permute-start | bytes 208904 | tf_op jit(solution)/shard_map/ppermute | solution.py:243
  20.4 2.5 %collective-permute-start.4 = (bf16[16,2176]{1,0:T(8,128)(2,1)S(1)}, bf16[16,2176]{1,0:T(8,128)(2,1)S(1)}, u32[]{:S(2)}, u32[]{:S(2)}) collective-permute-start(bf16[16,2176]{1,0:T(8,128)(2,1)S(1)} %get-tuple-element.48), channel_id=1, source_target_pairs={{0,24},{8,16},{16,8},{24,0},{1,25},{9,17},{17,9},{25,1},{2,26},{10... | collective-permute-start | bytes 208904 | tf_op jit(solution)/shard_map/ppermute | solution.py:243
  22.9 1.6 %collective-permute-start.10 = (bf16[32,2048]{1,0:T(8,128)(2,1)S(1)}, bf16[32,2048]{1,0:T(8,128)(2,1)S(1)}, u32[]{:S(2)}, u32[]{:S(2)}) collective-permute-start(bf16[32,2048]{1,0:T(8,128)(2,1)S(1)} %pad_maximum_fusion.2), channel_id=1, source_target_pairs={{0,8},{8,0},{16,24},{24,16},{1,9},{9,1},{17,25},{25,17},{2,10},{10... | collective-permute-start | bytes 393224 | tf_op jit(solution)/shard_map/ppermute | solution.py:243
  24.5 1.6 %collective-permute-done.3 = bf16[16,2176]{1,0:T(8,128)(2,1)S(1)} collective-permute-done((bf16[16,2176]{1,0:T(8,128)(2,1)S(1)}, bf16[16,2176]{1,0:T(8,128)(2,1)S(1)}, u32[]{:S(2)}, u32[]{:S(2)}) %collective-permute-start.3) | collective-permute-done | bytes 69664 | tf_op jit(solution)/shard_map/ppermute | solution.py:243
  26.1 1.0 collective-permute-done.4
  27.1 1.6 %collective-permute-start.5 = (bf16[64,2176]{1,0:T(8,128)(2,1)S(1)}, bf16[64,2176]{1,0:T(8,128)(2,1)S(1)}, u32[]{:S(2)}, u32[]{:S(2)}) collective-permute-start(bf16[64,2176]{1,0:T(8,128)(2,1)S(1)} %pad_maximum_fusion), channel_id=1, source_target_pairs={{0,4},{4,0},{1,5},{5,1},{2,6},{6,2},{3,7},{7,3},{8,12},{12,8},{9,1... | collective-permute-start | bytes 835592 | tf_op jit(solution)/shard_map/ppermute | solution.py:239
  28.7 0.4 collective-permute-done.10
  29.1 1.6 %collective-permute-start.11 = (bf16[64,2048]{1,0:T(8,128)(2,1)S(1)}, bf16[64,2048]{1,0:T(8,128)(2,1)S(1)}, u32[]{:S(2)}, u32[]{:S(2)}) collective-permute-start(bf16[64,2048]{1,0:T(8,128)(2,1)S(1)} %pad_maximum_fusion.1), channel_id=1, source_target_pairs={{0,2},{2,0},{1,3},{3,1},{4,6},{6,4},{5,7},{7,5},{8,10},{10,8},{9,1... | collective-permute-start | bytes 786440 | tf_op jit(solution)/shard_map/ppermute | solution.py:235
  30.7 3.6 %collective-permute-done.5 = bf16[64,2176]{1,0:T(8,128)(2,1)S(1)} collective-permute-done((bf16[64,2176]{1,0:T(8,128)(2,1)S(1)}, bf16[64,2176]{1,0:T(8,128)(2,1)S(1)}, u32[]{:S(2)}, u32[]{:S(2)}) %collective-permute-start.5) | collective-permute-done | bytes 278560 | tf_op jit(solution)/shard_map/ppermute | solution.py:239
  34.4 1.6 %collective-permute-start.6 = (bf16[128,2176]{1,0:T(8,128)(2,1)S(1)}, bf16[128,2176]{1,0:T(8,128)(2,1)S(1)}, u32[]{:S(2)}, u32[]{:S(2)}) collective-permute-start(bf16[128,2176]{1,0:T(8,128)(2,1)S(1)} %constant_dynamic-update-slice_fusion.a0), channel_id=1, source_target_pairs={{0,2},{2,0},{1,3},{3,1},{4,6},{6,4},{5,7},{7,5},{8,10},{10,8},{9,1... | collective-permute-start | bytes 1671176 | tf_op jit(solution)/shard_map/ppermute | solution.py:235
  36.0 2.5 %collective-permute-done.11 = bf16[64,2048]{1,0:T(8,128)(2,1)S(1)} collective-permute-done((bf16[64,2048]{1,0:T(8,128)(2,1)S(1)}, bf16[64,2048]{1,0:T(8,128)(2,1)S(1)}, u32[]{:S(2)}, u32[]{:S(2)}) %collective-permute-start.11) | collective-permute-done | bytes 262176 | tf_op jit(solution)/shard_map/ppermute | solution.py:235
  38.5 1.6 %collective-permute-start.12 = (bf16[128,2048]{1,0:T(8,128)(2,1)S(1)}, bf16[128,2048]{1,0:T(8,128)(2,1)S(1)}, u32[]{:S(2)}, u32[]{:S(2)}) collective-permute-start(bf16[128,2048]{1,0:T(8,128)(2,1)S(1)} %constant_dynamic-update-slice_fusion.5.b0), channel_id=1, source_target_pairs={{0,4},{4,0},{1,5},{5,1},{2,6},{6,2},{3,7},{7,3},{8,12},{12,8},{9,1... | collective-permute-start | bytes 1572872 | tf_op jit(solution)/shard_map/ppermute | solution.py:239
  40.0 0.0 collective-permute-start.7
  40.0 8.6 %collective-permute-done.6.a1 = bf16[128,2176]{1,0:T(8,128)(2,1)S(1)} collective-permute-done((bf16[128,2176]{1,0:T(8,128)(2,1)S(1)}, bf16[128,2176]{1,0:T(8,128)(2,1)S(1)}, u32[]{:S(2)}, u32[]{:S(2)}) %collective-permute-start.6) | collective-permute-done | bytes 557088 | tf_op jit(solution)/shard_map/ppermute | solution.py:235
  48.6 0.5 collective-permute-start.13
  49.1 0.0 collective-permute-done.12.b1
  49.1 0.0 collective-permute-start.14
  49.1 2.3 %collective-permute-done.13.b2 = bf16[128,2048]{1,0:T(8,128)(2,1)} collective-permute-done((bf16[128,2048]{1,0:T(8,128)(2,1)S(1)}, bf16[128,2048]{1,0:T(8,128)(2,1)}, u32[]{:S(2)}, u32[]{:S(2)}) %collective-permute-start.13) | collective-permute-done | bytes 524320 | tf_op jit(solution)/shard_map/ppermute | solution.py:231
  51.4 0.8 collective-permute-done.14.b3
  52.2 17.6 %experts.1 = (bf16[128,2048]{1,0:T(8,128)(2,1)S(1)}, bf16[128,2048]{1,0:T(8,128)(2,1)S(1)}, bf16[128,2048]{1,0:T(8,128)(2,1)S(1)}, bf16[128,2048]{1,0:T(8,128)(2...) custom-call(s32[1]{0:T(128)} %bitcast.6.place, ...), custom_call_target="tpu_custom_call" | custom-call | flops 5284823040 | bytes 44040192 | tf_op jit(solution)/shard_map/experts/pallas_call | solution.py:564
  69.8 0.2 collective-permute-start.15
  70.0 0.4 collective-permute-start.22
  70.4 0.1 collective-permute-start.17
  70.5 0.4 collective-permute-start.24
  70.9 0.9 collective-permute-done.15
  71.8 0.1 add_convert_fusion.3
  71.9 1.6 %collective-permute-start.16 = (bf16[128,2048]{1,0:T(8,128)(2,1)S(1)}, bf16[128,2048]{1,0:T(8,128)(2,1)S(1)}, u32[]{:S(2)}, u32[]{:S(2)}) collective-permute-start(bf16[128,2048]{1,0:T(8,128)(2,1)S(1)} %add_convert_fusion.3), channel_id=1, source_target_pairs={{0,2},{2,0},{1,3},{3,1},{4,6},{6,4},{5,7},{7,5},{8,10},{10,8},{9,1... | collective-permute-start | bytes 1572872 | tf_op jit(solution)/shard_map/ppermute | solution.py:235
  73.5 0.0 collective-permute-done.22
  73.5 0.1 add_convert_fusion.1
  73.6 1.5 %collective-permute-start.23 = (bf16[128,2048]{1,0:T(8,128)(2,1)S(1)}, bf16[128,2048]{1,0:T(8,128)(2,1)S(1)}, u32[]{:S(2)}, u32[]{:S(2)}) collective-permute-start(bf16[128,2048]{1,0:T(8,128)(2,1)S(1)} %add_convert_fusion.1), channel_id=1, source_target_pairs={{0,4},{4,0},{1,5},{5,1},{2,6},{6,2},{3,7},{7,3},{8,12},{12,8},{9,1... | collective-permute-start | bytes 1572872 | tf_op jit(solution)/shard_map/ppermute | solution.py:239
  75.2 0.0 collective-permute-done.17
  75.2 0.1 add_convert_fusion.2
  75.3 0.0 collective-permute-done.24
  75.3 0.1 add_convert_fusion
  75.5 11.9 %collective-permute-done.23 = bf16[128,2048]{1,0:T(8,128)(2,1)S(1)} collective-permute-done((bf16[128,2048]{1,0:T(8,128)(2,1)S(1)}, bf16[128,2048]{1,0:T(8,128)(2,1)S(1)}, u32[]{:S(2)}, u32[]{:S(2)}) %collective-permute-start.23) | collective-permute-done | bytes 524320 | tf_op jit(solution)/shard_map/ppermute | solution.py:239
  87.4 0.1 add_convert_fusion.4
  87.5 0.9 collective-permute-start.25
  88.4 0.0 collective-permute-done.16
  88.4 0.1 add_convert_fusion.6
  88.4 1.5 %collective-permute-start.18 = (bf16[64,2048]{1,0:T(8,128)(2,1)S(1)}, bf16[64,2048]{1,0:T(8,128)(2,1)S(1)}, u32[]{:S(2)}, u32[]{:S(2)}) collective-permute-start(bf16[64,2048]{1,0:T(8,128)(2,1)S(1)} %add_convert_fusion.6), channel_id=1, source_target_pairs={{0,4},{4,0},{1,5},{5,1},{2,6},{6,2},{3,7},{7,3},{8,12},{12,8},{9,1... | collective-permute-start | bytes 786440 | tf_op jit(solution)/shard_map/ppermute | solution.py:239
  90.0 4.8 %collective-permute-done.25 = bf16[64,2048]{1,0:T(8,128)(2,1)S(1)} collective-permute-done((bf16[64,2048]{1,0:T(8,128)(2,1)S(1)}, bf16[64,2048]{1,0:T(8,128)(2,1)S(1)}, u32[]{:S(2)}, u32[]{:S(2)}) %collective-permute-start.25) | collective-permute-done | bytes 262176 | tf_op jit(solution)/shard_map/ppermute | solution.py:235
  94.7 0.1 fusion.9
  94.9 2.3 %collective-permute-start.26 = (bf16[32,2048]{1,0:T(8,128)(2,1)S(1)}, bf16[32,2048]{1,0:T(8,128)(2,1)S(1)}, u32[]{:S(2)}, u32[]{:S(2)}) collective-permute-start(bf16[32,2048]{1,0:T(8,128)(2,1)S(1)} %pad_maximum_fusion.3), channel_id=1, source_target_pairs={{0,8},{8,0},{16,24},{24,16},{1,9},{9,1},{17,25},{25,17},{2,10},{10... | collective-permute-start | bytes 393224 | tf_op jit(solution)/shard_map/ppermute | solution.py:243
  97.1 0.0 collective-permute-done.18
  97.1 0.1 fusion.8
  97.3 0.9 collective-permute-start.19
  98.1 3.6 %collective-permute-start.21 = (bf16[16,2048]{1,0:T(8,128)(2,1)S(1)}, bf16[16,2048]{1,0:T(8,128)(2,1)S(1)}, u32[]{:S(2)}, u32[]{:S(2)}) collective-permute-start(bf16[16,2048]{1,0:T(8,128)(2,1)S(1)} %get-tuple-element.38), channel_id=1, source_target_pairs={{0,24},{8,16},{16,8},{24,0},{1,25},{9,17},{17,9},{25,1},{2,26},{10... | collective-permute-start | bytes 196616 | tf_op jit(solution)/shard_map/ppermute | solution.py:243
  101.7 3.9 %collective-permute-start.27 = (bf16[16,2048]{1,0:T(8,128)(2,1)S(1)}, bf16[16,2048]{1,0:T(8,128)(2,1)S(1)}, u32[]{:S(2)}, u32[]{:S(2)}) collective-permute-start(bf16[16,2048]{1,0:T(8,128)(2,1)S(1)} %fusion.4), channel_id=1, source_target_pairs={{0,16},{8,24},{16,0},{24,8},{1,17},{9,25},{17,1},{25,9},{2,18},{10... | collective-permute-start | bytes 196616 | tf_op jit(solution)/shard_map/ppermute | solution.py:243
  105.7 0.8 collective-permute-done.21
  106.5 2.2 %collective-permute-done.20 = bf16[16,2048]{1,0:T(8,128)(2,1)S(1)} collective-permute-done((bf16[16,2048]{1,0:T(8,128)(2,1)S(1)}, bf16[16,2048]{1,0:T(8,128)(2,1)S(1)}, u32[]{:S(2)}, u32[]{:S(2)}) %collective-permute-start.20) | collective-permute-done | bytes 65568 | tf_op jit(solution)/shard_map/ppermute | solution.py:243
  108.8 0.7 collective-permute-done.27
  109.5 0.7 fusion.3
  (31 shorter events, 0.4 us)
Async XLA Ops:
  6.2 2.2 %collective-permute-start = (bf16[32,4096]{1,0:T(8,128)(2,1)}, bf16[32,4096]{1,0:T(8,128)(2,1)S(1)}, u32[]{:S(2)}, u32[]{:S(2)}) collective-permute-start(bf16[32,4096]{1,0:T(8,128)(2,1)} %get-tuple-element.18), channel_id=1, source_target_pairs={{0,1},{1,0},{2,3},{3,2},{4,5},{5,4},{6,7},{7,6},{8,9},{9,8},{10,11... | collective-permute-start | bytes 786440 | tf_op jit(solution)/shard_map/ppermute | solution.py:231
  8.5 6.8 %collective-permute-start.1 = (bf16[16,4096]{1,0:T(8,128)(2,1)S(1)}, bf16[16,4096]{1,0:T(8,128)(2,1)S(1)}, u32[]{:S(2)}, u32[]{:S(2)}) collective-permute-start(bf16[16,4096]{1,0:T(8,128)(2,1)S(1)} %add_convert_fusion.10), channel_id=1, source_target_pairs={{0,2},{2,0},{1,3},{3,1},{4,6},{6,4},{5,7},{7,5},{8,10},{10,8},{9,1... | collective-permute-start | bytes 393224 | tf_op jit(solution)/shard_map/ppermute | solution.py:235
  15.6 7.3 %collective-permute-start.9 = (bf16[16,2048]{1,0:T(8,128)(2,1)S(1)}, bf16[16,2048]{1,0:T(8,128)(2,1)S(1)}, u32[]{:S(2)}, u32[]{:S(2)}) collective-permute-start(bf16[16,2048]{1,0:T(8,128)(2,1)S(1)} %get-tuple-element.45), channel_id=1, source_target_pairs={{0,16},{8,24},{16,0},{24,8},{1,17},{9,25},{17,1},{25,9},{2,18},{10... | collective-permute-start | bytes 196616 | tf_op jit(solution)/shard_map/ppermute | solution.py:243
  18.4 7.7 %collective-permute-start.3 = (bf16[16,2176]{1,0:T(8,128)(2,1)S(1)}, bf16[16,2176]{1,0:T(8,128)(2,1)S(1)}, u32[]{:S(2)}, u32[]{:S(2)}) collective-permute-start(bf16[16,2176]{1,0:T(8,128)(2,1)S(1)} %get-tuple-element.48), channel_id=1, source_target_pairs={{0,16},{8,24},{16,0},{24,8},{1,17},{9,25},{17,1},{25,9},{2,18},{10... | collective-permute-start | bytes 208904 | tf_op jit(solution)/shard_map/ppermute | solution.py:243
  18.6 7.5 %collective-permute-start.2 = (bf16[16,2176]{1,0:T(8,128)(2,1)S(1)}, bf16[16,2176]{1,0:T(8,128)(2,1)S(1)}, u32[]{:S(2)}, u32[]{:S(2)}) collective-permute-start(bf16[16,2176]{1,0:T(8,128)(2,1)S(1)} %get-tuple-element.48), channel_id=1, source_target_pairs={{0,8},{8,0},{16,24},{24,16},{1,9},{9,1},{17,25},{25,17},{2,10},{10... | collective-permute-start | bytes 208904 | tf_op jit(solution)/shard_map/ppermute | solution.py:243
  20.4 6.7 %collective-permute-start.4 = (bf16[16,2176]{1,0:T(8,128)(2,1)S(1)}, bf16[16,2176]{1,0:T(8,128)(2,1)S(1)}, u32[]{:S(2)}, u32[]{:S(2)}) collective-permute-start(bf16[16,2176]{1,0:T(8,128)(2,1)S(1)} %get-tuple-element.48), channel_id=1, source_target_pairs={{0,24},{8,16},{16,8},{24,0},{1,25},{9,17},{17,9},{25,1},{2,26},{10... | collective-permute-start | bytes 208904 | tf_op jit(solution)/shard_map/ppermute | solution.py:243
  22.9 6.2 %collective-permute-start.10 = (bf16[32,2048]{1,0:T(8,128)(2,1)S(1)}, bf16[32,2048]{1,0:T(8,128)(2,1)S(1)}, u32[]{:S(2)}, u32[]{:S(2)}) collective-permute-start(bf16[32,2048]{1,0:T(8,128)(2,1)S(1)} %pad_maximum_fusion.2), channel_id=1, source_target_pairs={{0,8},{8,0},{16,24},{24,16},{1,9},{9,1},{17,25},{25,17},{2,10},{10... | collective-permute-start | bytes 393224 | tf_op jit(solution)/shard_map/ppermute | solution.py:243
  27.1 7.2 %collective-permute-start.5 = (bf16[64,2176]{1,0:T(8,128)(2,1)S(1)}, bf16[64,2176]{1,0:T(8,128)(2,1)S(1)}, u32[]{:S(2)}, u32[]{:S(2)}) collective-permute-start(bf16[64,2176]{1,0:T(8,128)(2,1)S(1)} %pad_maximum_fusion), channel_id=1, source_target_pairs={{0,4},{4,0},{1,5},{5,1},{2,6},{6,2},{3,7},{7,3},{8,12},{12,8},{9,1... | collective-permute-start | bytes 835592 | tf_op jit(solution)/shard_map/ppermute | solution.py:239
  29.1 9.3 %collective-permute-start.11 = (bf16[64,2048]{1,0:T(8,128)(2,1)S(1)}, bf16[64,2048]{1,0:T(8,128)(2,1)S(1)}, u32[]{:S(2)}, u32[]{:S(2)}) collective-permute-start(bf16[64,2048]{1,0:T(8,128)(2,1)S(1)} %pad_maximum_fusion.1), channel_id=1, source_target_pairs={{0,2},{2,0},{1,3},{3,1},{4,6},{6,4},{5,7},{7,5},{8,10},{10,8},{9,1... | collective-permute-start | bytes 786440 | tf_op jit(solution)/shard_map/ppermute | solution.py:235
  34.4 14.2 %collective-permute-start.6 = (bf16[128,2176]{1,0:T(8,128)(2,1)S(1)}, bf16[128,2176]{1,0:T(8,128)(2,1)S(1)}, u32[]{:S(2)}, u32[]{:S(2)}) collective-permute-start(bf16[128,2176]{1,0:T(8,128)(2,1)S(1)} %constant_dynamic-update-slice_fusion.a0), channel_id=1, source_target_pairs={{0,2},{2,0},{1,3},{3,1},{4,6},{6,4},{5,7},{7,5},{8,10},{10,8},{9,1... | collective-permute-start | bytes 1671176 | tf_op jit(solution)/shard_map/ppermute | solution.py:235
  38.5 10.7 %collective-permute-start.12 = (bf16[128,2048]{1,0:T(8,128)(2,1)S(1)}, bf16[128,2048]{1,0:T(8,128)(2,1)S(1)}, u32[]{:S(2)}, u32[]{:S(2)}) collective-permute-start(bf16[128,2048]{1,0:T(8,128)(2,1)S(1)} %constant_dynamic-update-slice_fusion.5.b0), channel_id=1, source_target_pairs={{0,4},{4,0},{1,5},{5,1},{2,6},{6,2},{3,7},{7,3},{8,12},{12,8},{9,1... | collective-permute-start | bytes 1572872 | tf_op jit(solution)/shard_map/ppermute | solution.py:239
  40.0 9.1 %collective-permute-start.7 = (bf16[128,2176]{1,0:T(8,128)(2,1)S(1)}, bf16[128,2176]{1,0:T(8,128)(2,1)S(1)}, u32[]{:S(2)}, u32[]{:S(2)}) collective-permute-start(bf16[128,2176]{1,0:T(8,128)(2,1)S(1)} %constant_dynamic-update-slice_fusion.a0), channel_id=1, source_target_pairs={{0,1},{1,0},{2,3},{3,2},{4,5},{5,4},{6,7},{7,6},{8,9},{9,8},{10,11... | collective-permute-start | bytes 1671176 | tf_op jit(solution)/shard_map/ppermute | solution.py:231
  48.6 2.8 %collective-permute-start.8 = (bf16[128,2176]{1,0:T(8,128)(2,1)S(1)}, bf16[128,2176]{1,0:T(8,128)(2,1)S(1)}, u32[]{:S(2)}, u32[]{:S(2)}) collective-permute-start(bf16[128,2176]{1,0:T(8,128)(2,1)S(1)} %collective-permute-done.6.a1), channel_id=1, source_target_pairs={{0,1},{1,0},{2,3},{3,2},{4,5},{5,4},{6,7},{7,6},{8,9},{9,8},{10,11... | collective-permute-start | bytes 1671176 | tf_op jit(solution)/shard_map/ppermute | solution.py:231
  48.6 2.8 %collective-permute-start.13 = (bf16[128,2048]{1,0:T(8,128)(2,1)S(1)}, bf16[128,2048]{1,0:T(8,128)(2,1)}, u32[]{:S(2)}, u32[]{:S(2)}) collective-permute-start(bf16[128,2048]{1,0:T(8,128)(2,1)S(1)} %constant_dynamic-update-slice_fusion.5.b0), channel_id=1, source_target_pairs={{0,1},{1,0},{2,3},{3,2},{4,5},{5,4},{6,7},{7,6},{8,9},{9,8},{10,11... | collective-permute-start | bytes 1572872 | tf_op jit(solution)/shard_map/ppermute | solution.py:231
  49.1 3.1 %collective-permute-start.14 = (bf16[128,2048]{1,0:T(8,128)(2,1)S(1)}, bf16[128,2048]{1,0:T(8,128)(2,1)}, u32[]{:S(2)}, u32[]{:S(2)}) collective-permute-start(bf16[128,2048]{1,0:T(8,128)(2,1)S(1)} %collective-permute-done.12.b1), channel_id=1, source_target_pairs={{0,1},{1,0},{2,3},{3,2},{4,5},{5,4},{6,7},{7,6},{8,9},{9,8},{10,11... | collective-permute-start | bytes 1572872 | tf_op jit(solution)/shard_map/ppermute | solution.py:231
  69.8 2.0 %collective-permute-start.15 = (bf16[128,2048]{1,0:T(8,128)(2,1)S(1)}, bf16[128,2048]{1,0:T(8,128)(2,1)S(1)}, u32[]{:S(2)}, u32[]{:S(2)}) collective-permute-start(bf16[128,2048]{1,0:T(8,128)(2,1)S(1)} %get-tuple-element.23), channel_id=1, source_target_pairs={{0,1},{1,0},{2,3},{3,2},{4,5},{5,4},{6,7},{7,6},{8,9},{9,8},{10,11... | collective-permute-start | bytes 1572872 | tf_op jit(solution)/shard_map/ppermute | solution.py:231
  70.0 3.5 %collective-permute-start.22 = (bf16[128,2048]{1,0:T(8,128)(2,1)S(1)}, bf16[128,2048]{1,0:T(8,128)(2,1)S(1)}, u32[]{:S(2)}, u32[]{:S(2)}) collective-permute-start(bf16[128,2048]{1,0:T(8,128)(2,1)S(1)} %get-tuple-element.27), channel_id=1, source_target_pairs={{0,1},{1,0},{2,3},{3,2},{4,5},{5,4},{6,7},{7,6},{8,9},{9,8},{10,11... | collective-permute-start | bytes 1572872 | tf_op jit(solution)/shard_map/ppermute | solution.py:231
  70.4 4.8 %collective-permute-start.17 = (bf16[128,2048]{1,0:T(8,128)(2,1)S(1)}, bf16[128,2048]{1,0:T(8,128)(2,1)S(1)}, u32[]{:S(2)}, u32[]{:S(2)}) collective-permute-start(bf16[128,2048]{1,0:T(8,128)(2,1)S(1)} %get-tuple-element.25), channel_id=1, source_target_pairs={{0,1},{1,0},{2,3},{3,2},{4,5},{5,4},{6,7},{7,6},{8,9},{9,8},{10,11... | collective-permute-start | bytes 1572872 | tf_op jit(solution)/shard_map/ppermute | solution.py:231
  70.5 4.8 %collective-permute-start.24 = (bf16[128,2048]{1,0:T(8,128)(2,1)S(1)}, bf16[128,2048]{1,0:T(8,128)(2,1)S(1)}, u32[]{:S(2)}, u32[]{:S(2)}) collective-permute-start(bf16[128,2048]{1,0:T(8,128)(2,1)S(1)} %get-tuple-element.29), channel_id=1, source_target_pairs={{0,1},{1,0},{2,3},{3,2},{4,5},{5,4},{6,7},{7,6},{8,9},{9,8},{10,11... | collective-permute-start | bytes 1572872 | tf_op jit(solution)/shard_map/ppermute | solution.py:231
  71.9 16.4 %collective-permute-start.16 = (bf16[128,2048]{1,0:T(8,128)(2,1)S(1)}, bf16[128,2048]{1,0:T(8,128)(2,1)S(1)}, u32[]{:S(2)}, u32[]{:S(2)}) collective-permute-start(bf16[128,2048]{1,0:T(8,128)(2,1)S(1)} %add_convert_fusion.3), channel_id=1, source_target_pairs={{0,2},{2,0},{1,3},{3,1},{4,6},{6,4},{5,7},{7,5},{8,10},{10,8},{9,1... | collective-permute-start | bytes 1572872 | tf_op jit(solution)/shard_map/ppermute | solution.py:235
  73.6 13.8 %collective-permute-start.23 = (bf16[128,2048]{1,0:T(8,128)(2,1)S(1)}, bf16[128,2048]{1,0:T(8,128)(2,1)S(1)}, u32[]{:S(2)}, u32[]{:S(2)}) collective-permute-start(bf16[128,2048]{1,0:T(8,128)(2,1)S(1)} %add_convert_fusion.1), channel_id=1, source_target_pairs={{0,4},{4,0},{1,5},{5,1},{2,6},{6,2},{3,7},{7,3},{8,12},{12,8},{9,1... | collective-permute-start | bytes 1572872 | tf_op jit(solution)/shard_map/ppermute | solution.py:239
  87.5 7.3 %collective-permute-start.25 = (bf16[64,2048]{1,0:T(8,128)(2,1)S(1)}, bf16[64,2048]{1,0:T(8,128)(2,1)S(1)}, u32[]{:S(2)}, u32[]{:S(2)}) collective-permute-start(bf16[64,2048]{1,0:T(8,128)(2,1)S(1)} %add_convert_fusion.4), channel_id=1, source_target_pairs={{0,2},{2,0},{1,3},{3,1},{4,6},{6,4},{5,7},{7,5},{8,10},{10,8},{9,1... | collective-permute-start | bytes 786440 | tf_op jit(solution)/shard_map/ppermute | solution.py:235
  88.4 8.7 %collective-permute-start.18 = (bf16[64,2048]{1,0:T(8,128)(2,1)S(1)}, bf16[64,2048]{1,0:T(8,128)(2,1)S(1)}, u32[]{:S(2)}, u32[]{:S(2)}) collective-permute-start(bf16[64,2048]{1,0:T(8,128)(2,1)S(1)} %add_convert_fusion.6), channel_id=1, source_target_pairs={{0,4},{4,0},{1,5},{5,1},{2,6},{6,2},{3,7},{7,3},{8,12},{12,8},{9,1... | collective-permute-start | bytes 786440 | tf_op jit(solution)/shard_map/ppermute | solution.py:239
  94.9 6.8 %collective-permute-start.26 = (bf16[32,2048]{1,0:T(8,128)(2,1)S(1)}, bf16[32,2048]{1,0:T(8,128)(2,1)S(1)}, u32[]{:S(2)}, u32[]{:S(2)}) collective-permute-start(bf16[32,2048]{1,0:T(8,128)(2,1)S(1)} %pad_maximum_fusion.3), channel_id=1, source_target_pairs={{0,8},{8,0},{16,24},{24,16},{1,9},{9,1},{17,25},{25,17},{2,10},{10... | collective-permute-start | bytes 393224 | tf_op jit(solution)/shard_map/ppermute | solution.py:243
  97.3 8.4 %collective-permute-start.19 = (bf16[16,2048]{1,0:T(8,128)(2,1)S(1)}, bf16[16,2048]{1,0:T(8,128)(2,1)S(1)}, u32[]{:S(2)}, u32[]{:S(2)}) collective-permute-start(bf16[16,2048]{1,0:T(8,128)(2,1)S(1)} %get-tuple-element.37), channel_id=1, source_target_pairs={{0,8},{8,0},{16,24},{24,16},{1,9},{9,1},{17,25},{25,17},{2,10},{10... | collective-permute-start | bytes 196616 | tf_op jit(solution)/shard_map/ppermute | solution.py:243
  98.1 8.4 %collective-permute-start.21 = (bf16[16,2048]{1,0:T(8,128)(2,1)S(1)}, bf16[16,2048]{1,0:T(8,128)(2,1)S(1)}, u32[]{:S(2)}, u32[]{:S(2)}) collective-permute-start(bf16[16,2048]{1,0:T(8,128)(2,1)S(1)} %get-tuple-element.38), channel_id=1, source_target_pairs={{0,24},{8,16},{16,8},{24,0},{1,25},{9,17},{17,9},{25,1},{2,26},{10... | collective-permute-start | bytes 196616 | tf_op jit(solution)/shard_map/ppermute | solution.py:243
  101.7 7.1 %collective-permute-start.20 = (bf16[16,2048]{1,0:T(8,128)(2,1)S(1)}, bf16[16,2048]{1,0:T(8,128)(2,1)S(1)}, u32[]{:S(2)}, u32[]{:S(2)}) collective-permute-start(bf16[16,2048]{1,0:T(8,128)(2,1)S(1)} %get-tuple-element.39), channel_id=1, source_target_pairs={{0,16},{8,24},{16,0},{24,8},{1,17},{9,25},{17,1},{25,9},{2,18},{10... | collective-permute-start | bytes 196616 | tf_op jit(solution)/shard_map/ppermute | solution.py:243
  101.7 7.7 %collective-permute-start.27 = (bf16[16,2048]{1,0:T(8,128)(2,1)S(1)}, bf16[16,2048]{1,0:T(8,128)(2,1)S(1)}, u32[]{:S(2)}, u32[]{:S(2)}) collective-permute-start(bf16[16,2048]{1,0:T(8,128)(2,1)S(1)} %fusion.4), channel_id=1, source_target_pairs={{0,16},{8,24},{16,0},{24,8},{1,17},{9,25},{17,1},{25,9},{2,18},{10... | collective-permute-start | bytes 196616 | tf_op jit(solution)/shard_map/ppermute | solution.py:243

commit v7 on v6

--- a/solution.py
+++ b/solution.py
@@ -673,7 +673,7 @@
         rows = near.shape[0] // 2
         got = second(plus(far[rows:], near[rows:]))
         results.append(plus(far[:rows], near[:rows]).astype(jnp.float32) + got.astype(jnp.float32))
-    total_a, total_b = results
+    total_b, total_a = results
     sent = jnp.concatenate([total_b[count : 2 * count], total_b[3 * count :]], axis=0).astype(jnp.bfloat16)
     got = over_z(sent, 1).astype(jnp.float32)
     out_a = total_a[0:count]
@@ -682,7 +682,7 @@
         out_a = out_a + over_z(mine, k).astype(jnp.float32)
     far = (total_b[2 * count : 3 * count] + got[count:]).astype(jnp.bfloat16)
     out_b = total_b[0:count] + got[0:count] + over_z(far, 2).astype(jnp.float32)
-    return (wide + jnp.concatenate([out_a, out_b], axis=1)).astype(jnp.bfloat16)
+    return (wide + jnp.concatenate([out_b, out_a], axis=1)).astype(jnp.bfloat16)
 
 
 def solution(mesh):

time: 110 us -> 110 us (level)
  waiting for transfers between devices: 44.5 us -> 43 us
    ppermute x4, waiting for transfers between devices: 15.6 us -> 8.03 us  [over_x(): return lax.ppermute(a, 'expert', PAIRS_X)]
    ppermute x5, waiting for transfers between devices: 18.3 us -> 24 us  [over_y(): return lax.ppermute(a, 'tensor', PAIRS_Y)]
where the time goes in v7:
time: 110 us; the launch traced here: 109 us
  waiting for transfers between devices  43 us (39%)
  starting transfers between devices  37 us (34%)
  Pallas kernels  23.2 us (21%)
  other arithmetic  5.3 us (5%)
    ppermute x5, waiting for transfers between devices, over_y(): return lax.ppermute(a, 'tensor', PAIRS_Y)  24 us
    ppermute x10, starting transfers between devices, over_z(): return lax.ppermute(a, 'dp', [(i, i ^ k) for i in range(4)])  19.7 us
    pallas_call x1, Pallas kernels, experts_call(): pl.pallas_call(experts_kernel, out_shape=(out,) * 8, in_specs=[smem, smem...  17.6 us
    ppermute x5, starting transfers between devices, over_y(): return lax.ppermute(a, 'tensor', PAIRS_Y)  8.96 us
    ppermute x4, waiting for transfers between devices, over_x(): return lax.ppermute(a, 'expert', PAIRS_X)  8.03 us
    ppermute x10, waiting for transfers between devices, over_z(): return lax.ppermute(a, 'dp', [(i, i ^ k) for i in range(4)])  6.95 us
    ppermute x4, starting transfers between devices, over_x(): return lax.ppermute(a, 'expert', PAIRS_X)  6.21 us
    pallas_call x1, Pallas kernels, attention_call(): pl.pallas_call(attend_kernel, out_shape=(half, half, jax.ShapeDtypeStruct...  5.58 us
  transfers between devices with their start and end apart: 28, of which 15 were waited for; matrix products, arithmetic and copies ran while one was open for 4% of the time, Pallas kernels for 0%

profile of v7, /device:TPU:0, one launch (start us, length us, event | category | flops | bytes accessed | tf_op | source)
XLA Modules:
  0.0 109.4 jit_solution(4315409403838115482)
XLA Ops:
  0.7 5.6 %attention.1 = (bf16[32,4096]{1,0:T(8,128)(2,1)}, bf16[32,4096]{1,0:T(8,128)(2,1)}, f32[16,128]{1,0:T(8,128)}) custom-call(s32[1]{0:T(128)} %bitcast.place, s32[8,17]{1,0:T(8,128)} %bitcast.10, s32[17]{0:T(128)} %counts.1, s32[8]{0:T(128)} %allowed.1, s32[1]{0:T(128)S(6)} %copy.26.favored, s32[2,16]{1,0:T(2,128)} %bitcast.11, f32[2,16]{1,0:T(2,128)} %bitcast.12, ...), custom_call_target="tpu_custom_call" | custom-call | flops 1000000000 | bytes 8000000 | tf_op jit(solution)/shard_map/attention/pallas_call | solution.py:397
  6.2 0.5 collective-permute-start
  6.8 0.7 convert_element_type.151
  7.5 1.0 convert_element_type.150
  8.4 0.0 collective-permute-done
  8.5 2.6 %collective-permute-start.1 = (bf16[16,4096]{1,0:T(8,128)(2,1)S(1)}, bf16[16,4096]{1,0:T(8,128)(2,1)S(1)}, u32[]{:S(2)}, u32[]{:S(2)}) collective-permute-start(bf16[16,4096]{1,0:T(8,128)(2,1)S(1)} %add_convert_fusion.10), channel_id=1, source_target_pairs={{0,2},{2,0},{1,3},{3,1},{4,6},{6,4},{5,7},{7,5},{8,10},{10,8},{9,1... | collective-permute-start | bytes 393224 | tf_op jit(solution)/shard_map/ppermute | solution.py:235
  11.1 0.7 convert_element_type.159
  11.8 0.9 convert_element_type.148
  12.7 2.5 %collective-permute-done.1 = bf16[16,4096]{1,0:T(8,128)(2,1)S(1)} collective-permute-done((bf16[16,4096]{1,0:T(8,128)(2,1)S(1)}, bf16[16,4096]{1,0:T(8,128)(2,1)S(1)}, u32[]{:S(2)}, u32[]{:S(2)}) %collective-permute-start.1) | collective-permute-done | bytes 131104 | tf_op jit(solution)/shard_map/ppermute | solution.py:235
  15.2 0.2 fusion
  15.4 0.1 fusion.2
  15.6 2.9 %collective-permute-start.9 = (bf16[16,2048]{1,0:T(8,128)(2,1)S(1)}, bf16[16,2048]{1,0:T(8,128)(2,1)S(1)}, u32[]{:S(2)}, u32[]{:S(2)}) collective-permute-start(bf16[16,2048]{1,0:T(8,128)(2,1)S(1)} %get-tuple-element.45), channel_id=1, source_target_pairs={{0,16},{8,24},{16,0},{24,8},{1,17},{9,25},{17,1},{25,9},{2,18},{10... | collective-permute-start | bytes 196616 | tf_op jit(solution)/shard_map/ppermute | solution.py:243
  18.4 0.2 collective-permute-start.3
  18.6 1.8 %collective-permute-start.2 = (bf16[16,2176]{1,0:T(8,128)(2,1)S(1)}, bf16[16,2176]{1,0:T(8,128)(2,1)S(1)}, u32[]{:S(2)}, u32[]{:S(2)}) collective-permute-start(bf16[16,2176]{1,0:T(8,128)(2,1)S(1)} %get-tuple-element.48), channel_id=1, source_target_pairs={{0,8},{8,0},{16,24},{24,16},{1,9},{9,1},{17,25},{25,17},{2,10},{10... | collective-permute-start | bytes 208904 | tf_op jit(solution)/shard_map/ppermute | solution.py:243
  20.4 2.5 %collective-permute-start.4 = (bf16[16,2176]{1,0:T(8,128)(2,1)S(1)}, bf16[16,2176]{1,0:T(8,128)(2,1)S(1)}, u32[]{:S(2)}, u32[]{:S(2)}) collective-permute-start(bf16[16,2176]{1,0:T(8,128)(2,1)S(1)} %get-tuple-element.48), channel_id=1, source_target_pairs={{0,24},{8,16},{16,8},{24,0},{1,25},{9,17},{17,9},{25,1},{2,26},{10... | collective-permute-start | bytes 208904 | tf_op jit(solution)/shard_map/ppermute | solution.py:243
  22.9 1.6 %collective-permute-start.10 = (bf16[32,2048]{1,0:T(8,128)(2,1)S(1)}, bf16[32,2048]{1,0:T(8,128)(2,1)S(1)}, u32[]{:S(2)}, u32[]{:S(2)}) collective-permute-start(bf16[32,2048]{1,0:T(8,128)(2,1)S(1)} %pad_maximum_fusion.2), channel_id=1, source_target_pairs={{0,8},{8,0},{16,24},{24,16},{1,9},{9,1},{17,25},{25,17},{2,10},{10... | collective-permute-start | bytes 393224 | tf_op jit(solution)/shard_map/ppermute | solution.py:243
  24.5 1.6 %collective-permute-done.3 = bf16[16,2176]{1,0:T(8,128)(2,1)S(1)} collective-permute-done((bf16[16,2176]{1,0:T(8,128)(2,1)S(1)}, bf16[16,2176]{1,0:T(8,128)(2,1)S(1)}, u32[]{:S(2)}, u32[]{:S(2)}) %collective-permute-start.3) | collective-permute-done | bytes 69664 | tf_op jit(solution)/shard_map/ppermute | solution.py:243
  26.1 0.0 collective-permute-done.2
  26.1 1.0 collective-permute-done.4
  27.1 1.6 %collective-permute-start.5 = (bf16[64,2176]{1,0:T(8,128)(2,1)S(1)}, bf16[64,2176]{1,0:T(8,128)(2,1)S(1)}, u32[]{:S(2)}, u32[]{:S(2)}) collective-permute-start(bf16[64,2176]{1,0:T(8,128)(2,1)S(1)} %pad_maximum_fusion), channel_id=1, source_target_pairs={{0,4},{4,0},{1,5},{5,1},{2,6},{6,2},{3,7},{7,3},{8,12},{12,8},{9,1... | collective-permute-start | bytes 835592 | tf_op jit(solution)/shard_map/ppermute | solution.py:239
  28.7 0.4 collective-permute-done.10
  29.1 1.6 %collective-permute-start.11 = (bf16[64,2048]{1,0:T(8,128)(2,1)S(1)}, bf16[64,2048]{1,0:T(8,128)(2,1)S(1)}, u32[]{:S(2)}, u32[]{:S(2)}) collective-permute-start(bf16[64,2048]{1,0:T(8,128)(2,1)S(1)} %pad_maximum_fusion.1), channel_id=1, source_target_pairs={{0,2},{2,0},{1,3},{3,1},{4,6},{6,4},{5,7},{7,5},{8,10},{10,8},{9,1... | collective-permute-start | bytes 786440 | tf_op jit(solution)/shard_map/ppermute | solution.py:235
  30.7 3.6 %collective-permute-done.5 = bf16[64,2176]{1,0:T(8,128)(2,1)S(1)} collective-permute-done((bf16[64,2176]{1,0:T(8,128)(2,1)S(1)}, bf16[64,2176]{1,0:T(8,128)(2,1)S(1)}, u32[]{:S(2)}, u32[]{:S(2)}) %collective-permute-start.5) | collective-permute-done | bytes 278560 | tf_op jit(solution)/shard_map/ppermute | solution.py:239
  34.4 1.6 %collective-permute-start.6 = (bf16[128,2176]{1,0:T(8,128)(2,1)S(1)}, bf16[128,2176]{1,0:T(8,128)(2,1)S(1)}, u32[]{:S(2)}, u32[]{:S(2)}) collective-permute-start(bf16[128,2176]{1,0:T(8,128)(2,1)S(1)} %constant_dynamic-update-slice_fusion.a0), channel_id=1, source_target_pairs={{0,2},{2,0},{1,3},{3,1},{4,6},{6,4},{5,7},{7,5},{8,10},{10,8},{9,1... | collective-permute-start | bytes 1671176 | tf_op jit(solution)/shard_map/ppermute | solution.py:235
  36.0 2.5 %collective-permute-done.11 = bf16[64,2048]{1,0:T(8,128)(2,1)S(1)} collective-permute-done((bf16[64,2048]{1,0:T(8,128)(2,1)S(1)}, bf16[64,2048]{1,0:T(8,128)(2,1)S(1)}, u32[]{:S(2)}, u32[]{:S(2)}) %collective-permute-start.11) | collective-permute-done | bytes 262176 | tf_op jit(solution)/shard_map/ppermute | solution.py:235
  38.5 1.6 %collective-permute-start.12 = (bf16[128,2048]{1,0:T(8,128)(2,1)S(1)}, bf16[128,2048]{1,0:T(8,128)(2,1)S(1)}, u32[]{:S(2)}, u32[]{:S(2)}) collective-permute-start(bf16[128,2048]{1,0:T(8,128)(2,1)S(1)} %constant_dynamic-update-slice_fusion.5.b0), channel_id=1, source_target_pairs={{0,4},{4,0},{1,5},{5,1},{2,6},{6,2},{3,7},{7,3},{8,12},{12,8},{9,1... | collective-permute-start | bytes 1572872 | tf_op jit(solution)/shard_map/ppermute | solution.py:239
  40.0 8.6 %collective-permute-done.6.a1 = bf16[128,2176]{1,0:T(8,128)(2,1)S(1)} collective-permute-done((bf16[128,2176]{1,0:T(8,128)(2,1)S(1)}, bf16[128,2176]{1,0:T(8,128)(2,1)S(1)}, u32[]{:S(2)}, u32[]{:S(2)}) %collective-permute-start.6) | collective-permute-done | bytes 557088 | tf_op jit(solution)/shard_map/ppermute | solution.py:235
  48.6 0.5 collective-permute-start.13
  49.1 0.0 collective-permute-done.12.b1
  49.1 0.0 collective-permute-start.14
  49.1 2.3 %collective-permute-done.13.b2 = bf16[128,2048]{1,0:T(8,128)(2,1)} collective-permute-done((bf16[128,2048]{1,0:T(8,128)(2,1)S(1)}, bf16[128,2048]{1,0:T(8,128)(2,1)}, u32[]{:S(2)}, u32[]{:S(2)}) %collective-permute-start.13) | collective-permute-done | bytes 524320 | tf_op jit(solution)/shard_map/ppermute | solution.py:231
  51.4 0.8 collective-permute-done.14.b3
  52.2 17.6 %experts.1 = (bf16[128,2048]{1,0:T(8,128)(2,1)S(1)}, bf16[128,2048]{1,0:T(8,128)(2,1)S(1)}, bf16[128,2048]{1,0:T(8,128)(2,1)S(1)}, bf16[128,2048]{1,0:T(8,128)(2...) custom-call(s32[1]{0:T(128)} %bitcast.6.place, ...), custom_call_target="tpu_custom_call" | custom-call | flops 5284823040 | bytes 44040192 | tf_op jit(solution)/shard_map/experts/pallas_call | solution.py:564
  69.8 0.2 collective-permute-start.15
  70.0 0.4 collective-permute-start.21
  70.4 0.1 collective-permute-start.17
  70.5 0.4 collective-permute-start.23
  70.9 0.9 collective-permute-done.15
  71.8 0.1 add_convert_fusion.3
  71.9 1.6 %collective-permute-start.16 = (bf16[128,2048]{1,0:T(8,128)(2,1)S(1)}, bf16[128,2048]{1,0:T(8,128)(2,1)S(1)}, u32[]{:S(2)}, u32[]{:S(2)}) collective-permute-start(bf16[128,2048]{1,0:T(8,128)(2,1)S(1)} %add_convert_fusion.3), channel_id=1, source_target_pairs={{0,2},{2,0},{1,3},{3,1},{4,6},{6,4},{5,7},{7,5},{8,10},{10,8},{9,1... | collective-permute-start | bytes 1572872 | tf_op jit(solution)/shard_map/ppermute | solution.py:235
  73.5 0.1 add_convert_fusion.1
  73.6 1.5 %collective-permute-start.22 = (bf16[128,2048]{1,0:T(8,128)(2,1)S(1)}, bf16[128,2048]{1,0:T(8,128)(2,1)S(1)}, u32[]{:S(2)}, u32[]{:S(2)}) collective-permute-start(bf16[128,2048]{1,0:T(8,128)(2,1)S(1)} %add_convert_fusion.1), channel_id=1, source_target_pairs={{0,4},{4,0},{1,5},{5,1},{2,6},{6,2},{3,7},{7,3},{8,12},{12,8},{9,1... | collective-permute-start | bytes 1572872 | tf_op jit(solution)/shard_map/ppermute | solution.py:239
  75.2 0.1 add_convert_fusion.2
  75.3 0.0 collective-permute-done.23
  75.3 0.1 add_convert_fusion
  75.5 10.5 %collective-permute-done.16 = bf16[128,2048]{1,0:T(8,128)(2,1)S(1)} collective-permute-done((bf16[128,2048]{1,0:T(8,128)(2,1)S(1)}, bf16[128,2048]{1,0:T(8,128)(2,1)S(1)}, u32[]{:S(2)}, u32[]{:S(2)}) %collective-permute-start.16) | collective-permute-done | bytes 524320 | tf_op jit(solution)/shard_map/ppermute | solution.py:235
  85.9 0.1 add_convert_fusion.6
  86.0 1.5 %collective-permute-start.18 = (bf16[64,2048]{1,0:T(8,128)(2,1)S(1)}, bf16[64,2048]{1,0:T(8,128)(2,1)S(1)}, u32[]{:S(2)}, u32[]{:S(2)}) collective-permute-start(bf16[64,2048]{1,0:T(8,128)(2,1)S(1)} %add_convert_fusion.6), channel_id=1, source_target_pairs={{0,4},{4,0},{1,5},{5,1},{2,6},{6,2},{3,7},{7,3},{8,12},{12,8},{9,1... | collective-permute-start | bytes 786440 | tf_op jit(solution)/shard_map/ppermute | solution.py:239
  87.6 0.1 add_convert_fusion.4
  87.6 1.6 %collective-permute-start.24 = (bf16[64,2048]{1,0:T(8,128)(2,1)S(1)}, bf16[64,2048]{1,0:T(8,128)(2,1)S(1)}, u32[]{:S(2)}, u32[]{:S(2)}) collective-permute-start(bf16[64,2048]{1,0:T(8,128)(2,1)S(1)} %add_convert_fusion.4), channel_id=1, source_target_pairs={{0,2},{2,0},{1,3},{3,1},{4,6},{6,4},{5,7},{7,5},{8,10},{10,8},{9,1... | collective-permute-start | bytes 786440 | tf_op jit(solution)/shard_map/ppermute | solution.py:235
  89.2 4.4 %collective-permute-done.18 = bf16[64,2048]{1,0:T(8,128)(2,1)S(1)} collective-permute-done((bf16[64,2048]{1,0:T(8,128)(2,1)S(1)}, bf16[64,2048]{1,0:T(8,128)(2,1)S(1)}, u32[]{:S(2)}, u32[]{:S(2)}) %collective-permute-start.18) | collective-permute-done | bytes 262176 | tf_op jit(solution)/shard_map/ppermute | solution.py:239
  93.6 0.1 fusion.8
  93.7 2.3 %collective-permute-start.19 = (bf16[32,2048]{1,0:T(8,128)(2,1)S(1)}, bf16[32,2048]{1,0:T(8,128)(2,1)S(1)}, u32[]{:S(2)}, u32[]{:S(2)}) collective-permute-start(bf16[32,2048]{1,0:T(8,128)(2,1)S(1)} %pad_maximum_fusion.3), channel_id=1, source_target_pairs={{0,8},{8,0},{16,24},{24,16},{1,9},{9,1},{17,25},{25,17},{2,10},{10... | collective-permute-start | bytes 393224 | tf_op jit(solution)/shard_map/ppermute | solution.py:243
  96.0 0.1 fusion.9
  96.1 1.2 %collective-permute-start.25 = (bf16[16,2048]{1,0:T(8,128)(2,1)S(1)}, bf16[16,2048]{1,0:T(8,128)(2,1)S(1)}, u32[]{:S(2)}, u32[]{:S(2)}) collective-permute-start(bf16[16,2048]{1,0:T(8,128)(2,1)S(1)} %get-tuple-element.39), channel_id=1, source_target_pairs={{0,8},{8,0},{16,24},{24,16},{1,9},{9,1},{17,25},{25,17},{2,10},{10... | collective-permute-start | bytes 196616 | tf_op jit(solution)/shard_map/ppermute | solution.py:243
  97.3 3.6 %collective-permute-start.27 = (bf16[16,2048]{1,0:T(8,128)(2,1)S(1)}, bf16[16,2048]{1,0:T(8,128)(2,1)S(1)}, u32[]{:S(2)}, u32[]{:S(2)}) collective-permute-start(bf16[16,2048]{1,0:T(8,128)(2,1)S(1)} %get-tuple-element.40), channel_id=1, source_target_pairs={{0,24},{8,16},{16,8},{24,0},{1,25},{9,17},{17,9},{25,1},{2,26},{10... | collective-permute-start | bytes 196616 | tf_op jit(solution)/shard_map/ppermute | solution.py:243
  100.9 0.0 collective-permute-start.26
  100.9 0.0 collective-permute-done.19
  101.0 3.7 %collective-permute-start.20 = (bf16[16,2048]{1,0:T(8,128)(2,1)S(1)}, bf16[16,2048]{1,0:T(8,128)(2,1)S(1)}, u32[]{:S(2)}, u32[]{:S(2)}) collective-permute-start(bf16[16,2048]{1,0:T(8,128)(2,1)S(1)} %fusion.6), channel_id=1, source_target_pairs={{0,16},{8,24},{16,0},{24,8},{1,17},{9,25},{17,1},{25,9},{2,18},{10... | collective-permute-start | bytes 196616 | tf_op jit(solution)/shard_map/ppermute | solution.py:243
  104.6 0.0 collective-permute-done.25
  104.7 1.0 collective-permute-done.27
  105.6 2.4 %collective-permute-done.26 = bf16[16,2048]{1,0:T(8,128)(2,1)S(1)} collective-permute-done((bf16[16,2048]{1,0:T(8,128)(2,1)S(1)}, bf16[16,2048]{1,0:T(8,128)(2,1)S(1)}, u32[]{:S(2)}, u32[]{:S(2)}) %collective-permute-start.26) | collective-permute-done | bytes 65568 | tf_op jit(solution)/shard_map/ppermute | solution.py:243
  108.0 0.7 collective-permute-done.20
  108.7 0.7 fusion.3
  (31 shorter events, 0.4 us)
Async XLA Ops:
  6.2 2.2 %collective-permute-start = (bf16[32,4096]{1,0:T(8,128)(2,1)}, bf16[32,4096]{1,0:T(8,128)(2,1)S(1)}, u32[]{:S(2)}, u32[]{:S(2)}) collective-permute-start(bf16[32,4096]{1,0:T(8,128)(2,1)} %get-tuple-element.18), channel_id=1, source_target_pairs={{0,1},{1,0},{2,3},{3,2},{4,5},{5,4},{6,7},{7,6},{8,9},{9,8},{10,11... | collective-permute-start | bytes 786440 | tf_op jit(solution)/shard_map/ppermute | solution.py:231
  8.5 6.8 %collective-permute-start.1 = (bf16[16,4096]{1,0:T(8,128)(2,1)S(1)}, bf16[16,4096]{1,0:T(8,128)(2,1)S(1)}, u32[]{:S(2)}, u32[]{:S(2)}) collective-permute-start(bf16[16,4096]{1,0:T(8,128)(2,1)S(1)} %add_convert_fusion.10), channel_id=1, source_target_pairs={{0,2},{2,0},{1,3},{3,1},{4,6},{6,4},{5,7},{7,5},{8,10},{10,8},{9,1... | collective-permute-start | bytes 393224 | tf_op jit(solution)/shard_map/ppermute | solution.py:235
  15.6 7.3 %collective-permute-start.9 = (bf16[16,2048]{1,0:T(8,128)(2,1)S(1)}, bf16[16,2048]{1,0:T(8,128)(2,1)S(1)}, u32[]{:S(2)}, u32[]{:S(2)}) collective-permute-start(bf16[16,2048]{1,0:T(8,128)(2,1)S(1)} %get-tuple-element.45), channel_id=1, source_target_pairs={{0,16},{8,24},{16,0},{24,8},{1,17},{9,25},{17,1},{25,9},{2,18},{10... | collective-permute-start | bytes 196616 | tf_op jit(solution)/shard_map/ppermute | solution.py:243
  18.4 7.7 %collective-permute-start.3 = (bf16[16,2176]{1,0:T(8,128)(2,1)S(1)}, bf16[16,2176]{1,0:T(8,128)(2,1)S(1)}, u32[]{:S(2)}, u32[]{:S(2)}) collective-permute-start(bf16[16,2176]{1,0:T(8,128)(2,1)S(1)} %get-tuple-element.48), channel_id=1, source_target_pairs={{0,16},{8,24},{16,0},{24,8},{1,17},{9,25},{17,1},{25,9},{2,18},{10... | collective-permute-start | bytes 208904 | tf_op jit(solution)/shard_map/ppermute | solution.py:243
  18.6 7.5 %collective-permute-start.2 = (bf16[16,2176]{1,0:T(8,128)(2,1)S(1)}, bf16[16,2176]{1,0:T(8,128)(2,1)S(1)}, u32[]{:S(2)}, u32[]{:S(2)}) collective-permute-start(bf16[16,2176]{1,0:T(8,128)(2,1)S(1)} %get-tuple-element.48), channel_id=1, source_target_pairs={{0,8},{8,0},{16,24},{24,16},{1,9},{9,1},{17,25},{25,17},{2,10},{10... | collective-permute-start | bytes 208904 | tf_op jit(solution)/shard_map/ppermute | solution.py:243
  20.4 6.7 %collective-permute-start.4 = (bf16[16,2176]{1,0:T(8,128)(2,1)S(1)}, bf16[16,2176]{1,0:T(8,128)(2,1)S(1)}, u32[]{:S(2)}, u32[]{:S(2)}) collective-permute-start(bf16[16,2176]{1,0:T(8,128)(2,1)S(1)} %get-tuple-element.48), channel_id=1, source_target_pairs={{0,24},{8,16},{16,8},{24,0},{1,25},{9,17},{17,9},{25,1},{2,26},{10... | collective-permute-start | bytes 208904 | tf_op jit(solution)/shard_map/ppermute | solution.py:243
  22.9 6.2 %collective-permute-start.10 = (bf16[32,2048]{1,0:T(8,128)(2,1)S(1)}, bf16[32,2048]{1,0:T(8,128)(2,1)S(1)}, u32[]{:S(2)}, u32[]{:S(2)}) collective-permute-start(bf16[32,2048]{1,0:T(8,128)(2,1)S(1)} %pad_maximum_fusion.2), channel_id=1, source_target_pairs={{0,8},{8,0},{16,24},{24,16},{1,9},{9,1},{17,25},{25,17},{2,10},{10... | collective-permute-start | bytes 393224 | tf_op jit(solution)/shard_map/ppermute | solution.py:243
  27.1 7.2 %collective-permute-start.5 = (bf16[64,2176]{1,0:T(8,128)(2,1)S(1)}, bf16[64,2176]{1,0:T(8,128)(2,1)S(1)}, u32[]{:S(2)}, u32[]{:S(2)}) collective-permute-start(bf16[64,2176]{1,0:T(8,128)(2,1)S(1)} %pad_maximum_fusion), channel_id=1, source_target_pairs={{0,4},{4,0},{1,5},{5,1},{2,6},{6,2},{3,7},{7,3},{8,12},{12,8},{9,1... | collective-permute-start | bytes 835592 | tf_op jit(solution)/shard_map/ppermute | solution.py:239
  29.1 9.3 %collective-permute-start.11 = (bf16[64,2048]{1,0:T(8,128)(2,1)S(1)}, bf16[64,2048]{1,0:T(8,128)(2,1)S(1)}, u32[]{:S(2)}, u32[]{:S(2)}) collective-permute-start(bf16[64,2048]{1,0:T(8,128)(2,1)S(1)} %pad_maximum_fusion.1), channel_id=1, source_target_pairs={{0,2},{2,0},{1,3},{3,1},{4,6},{6,4},{5,7},{7,5},{8,10},{10,8},{9,1... | collective-permute-start | bytes 786440 | tf_op jit(solution)/shard_map/ppermute | solution.py:235
  34.4 14.2 %collective-permute-start.6 = (bf16[128,2176]{1,0:T(8,128)(2,1)S(1)}, bf16[128,2176]{1,0:T(8,128)(2,1)S(1)}, u32[]{:S(2)}, u32[]{:S(2)}) collective-permute-start(bf16[128,2176]{1,0:T(8,128)(2,1)S(1)} %constant_dynamic-update-slice_fusion.a0), channel_id=1, source_target_pairs={{0,2},{2,0},{1,3},{3,1},{4,6},{6,4},{5,7},{7,5},{8,10},{10,8},{9,1... | collective-permute-start | bytes 1671176 | tf_op jit(solution)/shard_map/ppermute | solution.py:235
  38.5 10.7 %collective-permute-start.12 = (bf16[128,2048]{1,0:T(8,128)(2,1)S(1)}, bf16[128,2048]{1,0:T(8,128)(2,1)S(1)}, u32[]{:S(2)}, u32[]{:S(2)}) collective-permute-start(bf16[128,2048]{1,0:T(8,128)(2,1)S(1)} %constant_dynamic-update-slice_fusion.5.b0), channel_id=1, source_target_pairs={{0,4},{4,0},{1,5},{5,1},{2,6},{6,2},{3,7},{7,3},{8,12},{12,8},{9,1... | collective-permute-start | bytes 1572872 | tf_op jit(solution)/shard_map/ppermute | solution.py:239
  40.0 9.1 %collective-permute-start.7 = (bf16[128,2176]{1,0:T(8,128)(2,1)S(1)}, bf16[128,2176]{1,0:T(8,128)(2,1)S(1)}, u32[]{:S(2)}, u32[]{:S(2)}) collective-permute-start(bf16[128,2176]{1,0:T(8,128)(2,1)S(1)} %constant_dynamic-update-slice_fusion.a0), channel_id=1, source_target_pairs={{0,1},{1,0},{2,3},{3,2},{4,5},{5,4},{6,7},{7,6},{8,9},{9,8},{10,11... | collective-permute-start | bytes 1671176 | tf_op jit(solution)/shard_map/ppermute | solution.py:231
  48.6 2.8 %collective-permute-start.8 = (bf16[128,2176]{1,0:T(8,128)(2,1)S(1)}, bf16[128,2176]{1,0:T(8,128)(2,1)S(1)}, u32[]{:S(2)}, u32[]{:S(2)}) collective-permute-start(bf16[128,2176]{1,0:T(8,128)(2,1)S(1)} %collective-permute-done.6.a1), channel_id=1, source_target_pairs={{0,1},{1,0},{2,3},{3,2},{4,5},{5,4},{6,7},{7,6},{8,9},{9,8},{10,11... | collective-permute-start | bytes 1671176 | tf_op jit(solution)/shard_map/ppermute | solution.py:231
  48.6 2.8 %collective-permute-start.13 = (bf16[128,2048]{1,0:T(8,128)(2,1)S(1)}, bf16[128,2048]{1,0:T(8,128)(2,1)}, u32[]{:S(2)}, u32[]{:S(2)}) collective-permute-start(bf16[128,2048]{1,0:T(8,128)(2,1)S(1)} %constant_dynamic-update-slice_fusion.5.b0), channel_id=1, source_target_pairs={{0,1},{1,0},{2,3},{3,2},{4,5},{5,4},{6,7},{7,6},{8,9},{9,8},{10,11... | collective-permute-start | bytes 1572872 | tf_op jit(solution)/shard_map/ppermute | solution.py:231
  49.1 3.1 %collective-permute-start.14 = (bf16[128,2048]{1,0:T(8,128)(2,1)S(1)}, bf16[128,2048]{1,0:T(8,128)(2,1)}, u32[]{:S(2)}, u32[]{:S(2)}) collective-permute-start(bf16[128,2048]{1,0:T(8,128)(2,1)S(1)} %collective-permute-done.12.b1), channel_id=1, source_target_pairs={{0,1},{1,0},{2,3},{3,2},{4,5},{5,4},{6,7},{7,6},{8,9},{9,8},{10,11... | collective-permute-start | bytes 1572872 | tf_op jit(solution)/shard_map/ppermute | solution.py:231
  69.8 2.0 %collective-permute-start.15 = (bf16[128,2048]{1,0:T(8,128)(2,1)S(1)}, bf16[128,2048]{1,0:T(8,128)(2,1)S(1)}, u32[]{:S(2)}, u32[]{:S(2)}) collective-permute-start(bf16[128,2048]{1,0:T(8,128)(2,1)S(1)} %get-tuple-element.23), channel_id=1, source_target_pairs={{0,1},{1,0},{2,3},{3,2},{4,5},{5,4},{6,7},{7,6},{8,9},{9,8},{10,11... | collective-permute-start | bytes 1572872 | tf_op jit(solution)/shard_map/ppermute | solution.py:231
  70.0 3.5 %collective-permute-start.21 = (bf16[128,2048]{1,0:T(8,128)(2,1)S(1)}, bf16[128,2048]{1,0:T(8,128)(2,1)S(1)}, u32[]{:S(2)}, u32[]{:S(2)}) collective-permute-start(bf16[128,2048]{1,0:T(8,128)(2,1)S(1)} %get-tuple-element.27), channel_id=1, source_target_pairs={{0,1},{1,0},{2,3},{3,2},{4,5},{5,4},{6,7},{7,6},{8,9},{9,8},{10,11... | collective-permute-start | bytes 1572872 | tf_op jit(solution)/shard_map/ppermute | solution.py:231
  70.4 4.8 %collective-permute-start.17 = (bf16[128,2048]{1,0:T(8,128)(2,1)S(1)}, bf16[128,2048]{1,0:T(8,128)(2,1)S(1)}, u32[]{:S(2)}, u32[]{:S(2)}) collective-permute-start(bf16[128,2048]{1,0:T(8,128)(2,1)S(1)} %get-tuple-element.25), channel_id=1, source_target_pairs={{0,1},{1,0},{2,3},{3,2},{4,5},{5,4},{6,7},{7,6},{8,9},{9,8},{10,11... | collective-permute-start | bytes 1572872 | tf_op jit(solution)/shard_map/ppermute | solution.py:231
  70.5 4.8 %collective-permute-start.23 = (bf16[128,2048]{1,0:T(8,128)(2,1)S(1)}, bf16[128,2048]{1,0:T(8,128)(2,1)S(1)}, u32[]{:S(2)}, u32[]{:S(2)}) collective-permute-start(bf16[128,2048]{1,0:T(8,128)(2,1)S(1)} %get-tuple-element.29), channel_id=1, source_target_pairs={{0,1},{1,0},{2,3},{3,2},{4,5},{5,4},{6,7},{7,6},{8,9},{9,8},{10,11... | collective-permute-start | bytes 1572872 | tf_op jit(solution)/shard_map/ppermute | solution.py:231
  71.9 14.0 %collective-permute-start.16 = (bf16[128,2048]{1,0:T(8,128)(2,1)S(1)}, bf16[128,2048]{1,0:T(8,128)(2,1)S(1)}, u32[]{:S(2)}, u32[]{:S(2)}) collective-permute-start(bf16[128,2048]{1,0:T(8,128)(2,1)S(1)} %add_convert_fusion.3), channel_id=1, source_target_pairs={{0,2},{2,0},{1,3},{3,1},{4,6},{6,4},{5,7},{7,5},{8,10},{10,8},{9,1... | collective-permute-start | bytes 1572872 | tf_op jit(solution)/shard_map/ppermute | solution.py:235
  73.6 13.9 %collective-permute-start.22 = (bf16[128,2048]{1,0:T(8,128)(2,1)S(1)}, bf16[128,2048]{1,0:T(8,128)(2,1)S(1)}, u32[]{:S(2)}, u32[]{:S(2)}) collective-permute-start(bf16[128,2048]{1,0:T(8,128)(2,1)S(1)} %add_convert_fusion.1), channel_id=1, source_target_pairs={{0,4},{4,0},{1,5},{5,1},{2,6},{6,2},{3,7},{7,3},{8,12},{12,8},{9,1... | collective-permute-start | bytes 1572872 | tf_op jit(solution)/shard_map/ppermute | solution.py:239
  86.0 7.6 %collective-permute-start.18 = (bf16[64,2048]{1,0:T(8,128)(2,1)S(1)}, bf16[64,2048]{1,0:T(8,128)(2,1)S(1)}, u32[]{:S(2)}, u32[]{:S(2)}) collective-permute-start(bf16[64,2048]{1,0:T(8,128)(2,1)S(1)} %add_convert_fusion.6), channel_id=1, source_target_pairs={{0,4},{4,0},{1,5},{5,1},{2,6},{6,2},{3,7},{7,3},{8,12},{12,8},{9,1... | collective-permute-start | bytes 786440 | tf_op jit(solution)/shard_map/ppermute | solution.py:239
  87.6 8.4 %collective-permute-start.24 = (bf16[64,2048]{1,0:T(8,128)(2,1)S(1)}, bf16[64,2048]{1,0:T(8,128)(2,1)S(1)}, u32[]{:S(2)}, u32[]{:S(2)}) collective-permute-start(bf16[64,2048]{1,0:T(8,128)(2,1)S(1)} %add_convert_fusion.4), channel_id=1, source_target_pairs={{0,2},{2,0},{1,3},{3,1},{4,6},{6,4},{5,7},{7,5},{8,10},{10,8},{9,1... | collective-permute-start | bytes 786440 | tf_op jit(solution)/shard_map/ppermute | solution.py:235
  93.7 7.2 %collective-permute-start.19 = (bf16[32,2048]{1,0:T(8,128)(2,1)S(1)}, bf16[32,2048]{1,0:T(8,128)(2,1)S(1)}, u32[]{:S(2)}, u32[]{:S(2)}) collective-permute-start(bf16[32,2048]{1,0:T(8,128)(2,1)S(1)} %pad_maximum_fusion.3), channel_id=1, source_target_pairs={{0,8},{8,0},{16,24},{24,16},{1,9},{9,1},{17,25},{25,17},{2,10},{10... | collective-permute-start | bytes 393224 | tf_op jit(solution)/shard_map/ppermute | solution.py:243
  96.1 8.5 %collective-permute-start.25 = (bf16[16,2048]{1,0:T(8,128)(2,1)S(1)}, bf16[16,2048]{1,0:T(8,128)(2,1)S(1)}, u32[]{:S(2)}, u32[]{:S(2)}) collective-permute-start(bf16[16,2048]{1,0:T(8,128)(2,1)S(1)} %get-tuple-element.39), channel_id=1, source_target_pairs={{0,8},{8,0},{16,24},{24,16},{1,9},{9,1},{17,25},{25,17},{2,10},{10... | collective-permute-start | bytes 196616 | tf_op jit(solution)/shard_map/ppermute | solution.py:243
  97.3 8.3 %collective-permute-start.27 = (bf16[16,2048]{1,0:T(8,128)(2,1)S(1)}, bf16[16,2048]{1,0:T(8,128)(2,1)S(1)}, u32[]{:S(2)}, u32[]{:S(2)}) collective-permute-start(bf16[16,2048]{1,0:T(8,128)(2,1)S(1)} %get-tuple-element.40), channel_id=1, source_target_pairs={{0,24},{8,16},{16,8},{24,0},{1,25},{9,17},{17,9},{25,1},{2,26},{10... | collective-permute-start | bytes 196616 | tf_op jit(solution)/shard_map/ppermute | solution.py:243
  100.9 7.1 %collective-permute-start.26 = (bf16[16,2048]{1,0:T(8,128)(2,1)S(1)}, bf16[16,2048]{1,0:T(8,128)(2,1)S(1)}, u32[]{:S(2)}, u32[]{:S(2)}) collective-permute-start(bf16[16,2048]{1,0:T(8,128)(2,1)S(1)} %get-tuple-element.41), channel_id=1, source_target_pairs={{0,16},{8,24},{16,0},{24,8},{1,17},{9,25},{17,1},{25,9},{2,18},{10... | collective-permute-start | bytes 196616 | tf_op jit(solution)/shard_map/ppermute | solution.py:243
  101.0 7.7 %collective-permute-start.20 = (bf16[16,2048]{1,0:T(8,128)(2,1)S(1)}, bf16[16,2048]{1,0:T(8,128)(2,1)S(1)}, u32[]{:S(2)}, u32[]{:S(2)}) collective-permute-start(bf16[16,2048]{1,0:T(8,128)(2,1)S(1)} %fusion.6), channel_id=1, source_target_pairs={{0,16},{8,24},{16,0},{24,8},{1,17},{9,25},{17,1},{25,9},{2,18},{10... | collective-permute-start | bytes 196616 | tf_op jit(solution)/shard_map/ppermute | solution.py:243
